TPU v7x, 256 devices: a whole 4x4x8 slice. The times are simulated.
256 devices in a mesh: seq: 64 (over z, y, core), book: 4 (over x).
Axes of the slice: x: 4, y: 4, z: 8, core: 2. Of those that a mesh axis runs over, the one named last changes fastest.
Arguments:
- frames: bfloat16 [65536, 1024], P('seq'), may hold values from -6 to 6
- norm_gain: float32 [1024], replicated, may hold values from 0.5 to 1.5
- x_weight: bfloat16 [1024, 2048], P(None, 'book'), may hold values from -0.1875 to 0.1875
- z_weight: bfloat16 [1024, 2048], P(None, 'book'), may hold values from -0.1875 to 0.1875
- bc_weight: bfloat16 [1024, 256], replicated, may hold values from -0.1875 to 0.1875
- dt_weight: bfloat16 [1024, 16], P(None, 'book'), may hold values from -0.1875 to 0.1875
- dt_bias: float32 [16], P('book'), may hold values from -1.5 to 0.5
- decay_rate: float32 [16], P('book'), may hold values from 7.6293945e-07 to 0.1
- out_gain: float32 [2048], P('book'), may hold values from 0.5 to 1.5
- out_weight: bfloat16 [2048, 1024], P('book'), may hold values from -0.125 to 0.125
- codebook: float32 [3, 65536, 1024], P(None, 'seq', 'book'), may hold values from -4 to 4
- code_ids: int32 [3, 16384], P(None, 'seq'), may hold values from 0 to 65535, as said below
Outputs:
- residual: float32 [16384, 1024], P('seq', 'book')
- code_grad: float32 [3, 65536, 1024], P(None, 'seq', 'book')
Inputs may be any that keep to these rules, and one draw needn't show every extreme that they name: `code_ids`: the owner of a code is its index // 1024. In each level, of the 256 rows of one seq index at most 12 name codes of one owner; one owner, drawn for each level and different in different levels, gets exactly 12 rows from every seq index; every other owner gets at most 4. The owner that gets 12 rows in level 0 gets exactly 4 rows from every seq index in every other level, so that over all levels the rows of one seq index name codes of one owner at most 20 times, and exactly so for that owner.
All inputs are finite; a program needn't handle non-finite values.
Results may differ from a plain program's by a relative error of at most 0.005.
Values sent between devices are 32-bit elements; how exact they have to be, the bound alone decides.
No kernel may reach another device: no remote copies, remote signals or barrier semaphores. Data moves between devices by JAX's collectives and lax.ppermute only.
A program may use at most 128 MiB of HBM per device.

v0:
```python
import jax
import jax.numpy as jnp
from jax import lax
from jax.sharding import Mesh
from jax.sharding import PartitionSpec as P

BLOCK = 256
POOL = 4
SEQ = ("seq_0", "seq_1", "seq_2")


def neutral_like(array, identity):
    return jax.tree.map(
        lambda part, zero: jnp.zeros_like(part) + jnp.asarray(zero, part.dtype), array, identity
    )


def carried_in(array, axes, combine, identity):
    before = start = neutral_like(array, identity)
    total = array
    for axis in reversed(axes):
        devices, place = (lax.axis_size(axis), lax.axis_index(axis))
        pieces = jax.tree.map(lambda part: lax.all_gather(part, axis), total)
        inside, total = (start, start)
        for k in range(devices):
            passed = k < place
            total = combine(total, jax.tree.map(lambda part: part[k], pieces))
            inside = jax.tree.map(lambda new, old: jnp.where(passed, new, old), total, inside)
        before = combine(inside, before)
    return before


def cut_along(array, dim, devices):
    before, after = (array.shape[:dim], array.shape[dim + 1 :])
    return jnp.moveaxis(array.reshape(*before, devices, -1, *after), dim, 0)


def sum_at_owner(array, axis, dim):
    devices = lax.axis_size(axis)
    pieces = lax.all_to_all(cut_along(array, dim, devices), axis, 0, 0, tiled=True)
    return jnp.sum(pieces, axis=0)


def rms_scaled(values, scales):
    mean_square = jnp.mean(values * values, axis=-1, keepdims=True)
    return values * lax.rsqrt(mean_square + 1e-05) * scales


def block_pass(carried, inputs):
    x_part, b_part, c_part, dt_part, log_part = inputs
    cumulative = jnp.cumsum(log_part, axis=0)
    length = log_part.shape[0]
    causal = jnp.arange(length)[:, None] >= jnp.arange(length)[None, :]
    log_gaps = cumulative[:, None, :] - cumulative[None, :, :]
    weights = jnp.where(
        causal[:, :, None], jnp.exp(jnp.where(causal[:, :, None], log_gaps, 0.0)), 0.0
    )
    scores = jnp.dot(c_part, b_part.T, precision=lax.Precision.HIGHEST)
    inflow = x_part * dt_part[:, :, None]
    outputs = jnp.einsum(
        "tjh,jhp->thp", weights * scores[:, :, None], inflow, precision=lax.Precision.HIGHEST
    )
    outputs = outputs + jnp.exp(cumulative)[:, :, None] * jnp.einsum(
        "tn,hpn->thp", c_part, carried, precision=lax.Precision.HIGHEST
    )
    tail_decay = jnp.exp(cumulative[-1:] - cumulative)
    updated = jnp.exp(cumulative[-1])[:, None, None] * carried + jnp.einsum(
        "jh,jhp,jn->hpn", tail_decay, inflow, b_part, precision=lax.Precision.HIGHEST
    )
    return (updated, outputs)


def block_state(carried, inputs):
    x_part, b_part, c_part, dt_part, log_part = inputs
    cumulative = jnp.cumsum(log_part, axis=0)
    inflow = x_part * dt_part[:, :, None]
    tail_decay = jnp.exp(cumulative[-1:] - cumulative)
    updated = jnp.exp(cumulative[-1])[:, None, None] * carried + jnp.einsum(
        "jh,jhp,jn->hpn", tail_decay, inflow, b_part, precision=lax.Precision.HIGHEST
    )
    return (updated, None)


def combine_states(earlier, later):
    return (earlier[0] + later[0], jnp.exp(later[0])[:, None, None] * earlier[1] + later[1])


def carry_in(total_log, local_state):
    identity = (jnp.zeros_like(total_log), jnp.zeros_like(local_state))
    prefix = carried_in((total_log, local_state), SEQ, combine_states, identity)
    return prefix[1]


def body(
    frames,
    norm_gain,
    x_weight,
    z_weight,
    bc_weight,
    dt_weight,
    dt_bias,
    decay_rate,
    out_gain,
    out_weight,
    codebook,
    code_ids,
):
    frame_rows = frames.shape[0]
    heads_here = dt_bias.shape[0]
    head_width = x_weight.shape[1] // heads_here
    state_width = bc_weight.shape[1] // 2
    frames_wide = frames.astype(jnp.float32)
    normed = rms_scaled(frames_wide, norm_gain).astype(jnp.bfloat16)
    x_proj = jnp.dot(normed, x_weight, preferred_element_type=jnp.float32).astype(jnp.bfloat16)
    z_proj = jnp.dot(normed, z_weight, preferred_element_type=jnp.float32).astype(jnp.bfloat16)
    bc_proj = jnp.dot(normed, bc_weight, preferred_element_type=jnp.float32).astype(jnp.bfloat16)
    dt_full = jax.nn.softplus(
        jnp.dot(normed, dt_weight, preferred_element_type=jnp.float32) + dt_bias
    )
    x_act = jax.nn.silu(x_proj.astype(jnp.float32)).reshape(frame_rows, heads_here, head_width)
    bc_act = jax.nn.silu(bc_proj.astype(jnp.float32))
    b_full = bc_act[:, :state_width]
    c_full = bc_act[:, state_width:]
    log_decay = -dt_full * decay_rate
    blocks = frame_rows // BLOCK
    stacked = (
        x_act.reshape(blocks, BLOCK, heads_here, head_width),
        b_full.reshape(blocks, BLOCK, state_width),
        c_full.reshape(blocks, BLOCK, state_width),
        dt_full.reshape(blocks, BLOCK, heads_here),
        log_decay.reshape(blocks, BLOCK, heads_here),
    )
    total_log = jnp.sum(log_decay, axis=0)
    initial = jnp.zeros((heads_here, head_width, state_width), jnp.float32)
    local_state = lax.scan(block_state, initial, stacked)[0]
    incoming = carry_in(total_log, local_state)
    ssd_out = lax.scan(block_pass, incoming, stacked)[1]
    ssd_out = ssd_out.reshape(frame_rows, heads_here, head_width)
    gated_rows = ssd_out * jax.nn.silu(z_proj.astype(jnp.float32)).reshape(
        frame_rows, heads_here, head_width
    )
    gated_rows = (
        rms_scaled(gated_rows, out_gain.reshape(heads_here, head_width))
        .reshape(frame_rows, heads_here * head_width)
        .astype(jnp.bfloat16)
    )
    partial_out = jnp.dot(gated_rows, out_weight, preferred_element_type=jnp.float32)
    column_width = out_weight.shape[1] // lax.axis_size("book")
    col_start = lax.axis_index("book") * column_width
    own_frames = lax.dynamic_slice_in_dim(frames_wide, col_start, column_width, 1)
    quant_rows = frame_rows // POOL
    encoded = own_frames + sum_at_owner(partial_out, "book", 1)
    pooled = jnp.mean(encoded.reshape(quant_rows, POOL, column_width), axis=1)
    levels = code_ids.shape[0]
    owners = lax.axis_size(SEQ)
    codes_here = codebook.shape[1]
    ordinary = (quant_rows + owners - 1) // owners
    capacity = 3 * ordinary
    owner_of = code_ids // codes_here
    row_of = code_ids % codes_here
    member = (owner_of[:, :, None] == jnp.arange(owners, dtype=jnp.int32)[None, None, :]).astype(
        jnp.bfloat16
    )
    earlier_rows = (jnp.arange(quant_rows)[None, :] < jnp.arange(quant_rows)[:, None]).astype(
        jnp.bfloat16
    )
    before_count = jnp.einsum(
        "fg,lgo->lfo", earlier_rows, member, preferred_element_type=jnp.float32
    )
    ranking = jnp.sum(before_count * member, axis=2).astype(jnp.int32)
    level_ids = jnp.arange(levels, dtype=jnp.int32)[:, None]
    merged_cap = capacity + (levels - 1) * ordinary
    level_counts = jnp.sum(member.astype(jnp.float32), axis=1)
    earlier_levels = jnp.cumsum(level_counts, axis=0) - level_counts
    merged_rank = ranking + jnp.sum(earlier_levels[:, None, :] * member, axis=2).astype(jnp.int32)
    merged_slot = owner_of * merged_cap + merged_rank
    wanted = level_ids * codes_here + row_of
    merged_requests = (
        jnp.full((owners * merged_cap,), -1, jnp.int32)
        .at[merged_slot.reshape(-1)]
        .set(wanted.reshape(-1))
    )
    arrived = lax.all_to_all(
        merged_requests.reshape(owners, merged_cap), SEQ, split_axis=0, concat_axis=0, tiled=True
    ).reshape(owners * merged_cap)
    filled = arrived >= 0
    safe_rows = jnp.maximum(arrived, 0)
    flat_table = codebook.reshape(levels * codes_here, column_width)
    looked_up = jnp.where(filled[:, None], flat_table[safe_rows], 0.0).reshape(
        owners, merged_cap, column_width
    )
    fetched_rows = lax.all_to_all(looked_up, SEQ, split_axis=0, concat_axis=0, tiled=True).reshape(
        owners * merged_cap, column_width
    )
    residual = pooled
    grad_flat = jnp.zeros((owners * merged_cap, column_width), jnp.float32)
    for level_idx in range(levels):
        picked = fetched_rows[merged_slot[level_idx]]
        grad_flat = grad_flat.at[merged_slot[level_idx]].set(picked - residual)
        residual = residual - picked
    came_back = lax.all_to_all(
        grad_flat.reshape(owners, merged_cap, column_width),
        SEQ,
        split_axis=0,
        concat_axis=0,
        tiled=True,
    ).reshape(owners * merged_cap, column_width)
    came_back = jnp.where(filled[:, None], came_back, 0.0)
    gradient_table = (
        jnp.zeros((levels * codes_here, column_width), jnp.float32).at[safe_rows].add(came_back)
    )
    return (residual, gradient_table.reshape(levels, codes_here, column_width))


def solution(mesh):
    finer = Mesh(
        mesh.devices.reshape(8, 4, 2, mesh.shape["book"]), ("seq_0", "seq_1", "seq_2", "book")
    )
    placed = (
        P(SEQ, None),
        P(),
        P(None, "book"),
        P(None, "book"),
        P(),
        P(None, "book"),
        P("book"),
        P("book"),
        P("book"),
        P("book", None),
        P(None, SEQ, "book"),
        P(None, SEQ),
    )
    return jax.shard_map(
        body,
        mesh=finer,
        in_specs=placed,
        out_specs=(P(SEQ, "book"), P(None, SEQ, "book")),
        check_vma=False,
    )
```

profile of v0, /device:TPU:1, one launch (start us, length us, event | category | flops | bytes accessed | tf_op | source)
XLA Modules:
  0.0 332.2 jit_solution(9552655645958083074)
XLA Ops:
  13.5 5.3 %all-reduce = f32[8]{0:T(128)S(1)} all-reduce(f32[8]{0:T(128)S(1)} %dynamic-update-slice), channel_id=2, replica_groups=mesh['seq_0'=8,'seq_1'=4,'seq_2'=2,'book'=4] {'seq_2'}, use_global_device_ids=true, to_apply=%add | all-reduce | flops 8 | bytes 64
  24.7 2.9 convert_multiply_fusion.1
  27.6 2.9 reshape_reshape.3
  30.5 2.9 copy.133
  33.4 14.7 %while.24 = (s32[]{:T(128)}, f32[4,128,128]{2,1,0:T(8,128)S(1)}, f32[4,256,4]{1,2,0:T(4,128)S(1)}, f32[4,256,4,128]{1,3,2,0:T(8,128)}, f32[4,256,4]{1,2,0:T(4,12...) while((s32[]{:T(128)}, f32[4,128,128]{2,1,0:T(8,128)S(1)}, ...), condition=%wide.region_5.6_spmd.clone, body=%wide.region_2.5_spmd.clone.sunk | while | flops 201917456 | bytes 1246787 | solution.py:135
  52.0 7.0 %all-reduce.1 = f32[16]{0:T(128)S(1)} all-reduce(f32[16]{0:T(128)S(1)} %get-tuple-element.242), channel_id=4, replica_groups=mesh['seq_0'=8,'seq_1'=4,'seq_2'=2,'book'=4] {'seq_1'}, use_global_device_ids=true, to_apply=%add.1 | all-reduce | flops 16 | bytes 128
  59.2 19.5 %all-gather.7.cloned.1.call-done = f32[4,4,128,128]{3,2,1,0:T(8,128)} async-done(((f32[1,4,128,128]{3,2,1,0:T(8,128)}), f32[4,4,128,128]{3,2,1,0:T(8,128)}) %all-gather.7.cloned.1.call-update) | async-done | bytes 1048592 | tf_op jit(solution)/shard_map/all_gather | solution.py:23
  81.4 3.4 %scatter_custom_fusion = s32[1280]{0:T(1024)S(1)} fusion(s32[768]{0:T(1024)S(1)} %fusion.95, s32[768]{0:T(1024)S(1)} %reshape.508, s32[]{:T(128)} %constant.129.clone.1), kind=kCustom, calls=%fused_computation.178 | custom fusion | bytes 5124 | tf_op jit(solution)/shard_map/scatter | solution.py:181
  85.5 10.6 %all-to-all-start.1 = ((s32[64,1,20]{2,1,0:T(1,128)}), s32[64,1,20]{2,1,0:T(1,128)S(1)}, u32[]{:S(2)}, u32[]{:S(2)}) async-start(s32[64,1,20]{2,1,0:T(1,128)} %bitcast.52), calls=%async_computation.1 | async-start | bytes 65536 | tf_op jit(solution)/shard_map/all_to_all | solution.py:183
  96.1 14.0 %all-gather.3 = f32[8,1,4]{2,1,0:T(1,128)S(1)} all-gather(f32[1,1,4]{2,1,0:T(1,128)S(1)} %get-tuple-element.237), channel_id=1, replica_groups=mesh['seq_0'=8,'seq_1'=4,'seq_2'=2,'book'=4] {'seq_0'}, dimensions={0}, use_global_device_ids=true | all-gather | bytes 144 | tf_op jit(solution)/shard_map/all_gather | solution.py:23
  110.1 4.8 %convert_multiply_fusion = f32[1024,512]{1,0:T(8,128)} fusion(bf16[1024,512]{1,0:T(8,128)(2,1)} %param.19, f32[1024]{0:T(1024)S(1)} %copy-done.13, f32[1024]{0:T(1024)S(1)} %add_rsqrt_fusion.1, bf16[1024,1024]{1,0:T(8,128)(2,1)} %param.16), kind=kOutput, calls=%fused_computation.70 | convolution fusion | flops 1081081856 | bytes 5251072 | tf_op jit(solution)/shard_map/dot_general | solution.py:115
  115.0 3.0 reshape.460
  117.9 2.9 copy.139
  123.5 4.1 %gather_fusion = f32[1280,256]{1,0:T(8,128)} fusion(f32[3072,256]{1,0:T(8,128)S(1)} %bitcast.315, s32[2048]{0:T(1024)S(1)} %pad_clamp_fusion), kind=kCustom, calls=%fused_computation | custom fusion | bytes 2626560 | tf_op jit(solution)/shard_map/gather | solution.py:189
  130.7 10.7 %all-to-all-start.2 = ((f32[64,20,256]{2,1,0:T(8,128)}), f32[64,20,256]{2,1,0:T(8,128)}, u32[]{:S(2)}, u32[]{:S(2)}) async-start(f32[64,20,256]{2,1,0:T(8,128)} %broadcast_select_fusion), calls=%async_computation.2 | async-start | bytes 3145728 | tf_op jit(solution)/shard_map/all_to_all | solution.py:192
  141.4 2.6 fusion.66
  144.0 34.8 %while.23 = (s32[]{:T(128)}, f32[4,128,128]{2,1,0:T(8,128)S(1)}, f32[4,256,4,128]{1,3,2,0:T(8,128)}, f32[4,256,4]{1,2,0:T(4,128)S(1)}, f32[4,256,4,128]{1,3,2,0:...) while((s32[]{:T(128)}, f32[4,128,128]{2,1,0:T(8,128)S(1)}, ...), condition=%wide.region_9.10_spmd, body=%wide.region_6.9_spmd.sunk | while | flops 908002304 | bytes 4678193 | solution.py:137
  178.9 3.0 copy.138
  187.1 5.4 %convolution_bitcast_fusion.1 = f32[4,1024,256]{2,1,0:T(8,128)} fusion(bf16[4,256,512]{2,1,0:T(8,128)(2,1)S(1)} %bitcast.319, f32[128,8,4,128]{3,2,1,0:T(4,128)S(1)} %bitcast.317, f32[1024,512]{1,0:T(8,128)} %convert_multiply_fusion, f32[128,8,4,128]{3,2,1,0:T(4,128)} %bitcast.318, f32[512]{0:T(512)S(1)} %copy-done.10), kind=kOutput, calls=%fused_computation.74 | convolution fusion | flops 1075838976 | bytes 11536384 | tf_op jit(solution)/shard_map/dot_general | solution.py:147
  192.5 5.2 %all-to-all-start = ((f32[4,1024,256]{2,1,0:T(8,128)}), f32[4,1024,256]{2,1,0:T(8,128)}, u32[]{:S(2)}, u32[]{:S(2)}) async-start(f32[4,1024,256]{2,1,0:T(8,128)} %convolution_bitcast_fusion.1), calls=%async_computation | async-start | bytes 8388608 | tf_op jit(solution)/shard_map/all_to_all | solution.py:40
  204.6 41.3 %all-to-all-done = f32[4,1024,256]{2,1,0:T(8,128)} async-done(((f32[4,1024,256]{2,1,0:T(8,128)}), f32[4,1024,256]{2,1,0:T(8,128)}, u32[]{:S(2)}, u32[]{:S(2)}) %all-to-all-start) | async-done | bytes 4194336 | tf_op jit(solution)/shard_map/all_to_all | solution.py:40
  257.9 11.5 %all-to-all-start.3 = ((f32[64,20,256]{2,1,0:T(8,128)}), f32[64,20,256]{2,1,0:T(8,128)}, u32[]{:S(2)}, u32[]{:S(2)}) async-start(f32[64,20,256]{2,1,0:T(8,128)} %reshape.466), calls=%async_computation.3 | async-start | bytes 3145728 | tf_op jit(solution)/shard_map/all_to_all | solution.py:201
  270.4 37.9 %all-to-all-done.3 = f32[64,20,256]{2,1,0:T(8,128)} async-done(((f32[64,20,256]{2,1,0:T(8,128)}), f32[64,20,256]{2,1,0:T(8,128)}, u32[]{:S(2)}, u32[]{:S(2)}) %all-to-all-start.3) | async-done | bytes 1310752 | tf_op jit(solution)/shard_map/all_to_all | solution.py:201
  310.9 14.5 %scatter_custom_fusion.4 = f32[3072,256]{1,0:T(8,128)} fusion(s32[1280]{0:T(1024)S(1)} %reshape.474, f32[]{:T(128)} %constant.113.clone.1, f32[1280,256]{1,0:T(8,128)} %reshape.467, pred[1280]{0:T(1024)(128)(4,1)S(1)} %ge.39), kind=kCustom, calls=%fused_computation.86 | custom fusion | flops 655360 | bytes 4459520 | tf_op jit(solution)/shard_map/scatter-add | solution.py:210
  (239 shorter events, 100.4 us)
Async XLA Ops:
  7.2 116.3 %copy-start = (f32[3,1024,256]{2,1,0:T(8,128)S(1)}, f32[3,1024,256]{2,1,0:T(8,128)}, u32[]{:S(2)}) copy-start(f32[3,1024,256]{2,1,0:T(8,128)} %param.26) | copy-start | bytes 9437188
  7.2 2.4 copy-start.17
  7.2 3.6 %copy-start.13 = (f32[1024]{0:T(1024)S(1)}, f32[1024]{0:T(1024)}, u32[]{:S(2)}) copy-start(f32[1024]{0:T(1024)} %param.17) | copy-start | bytes 12292
  7.2 3.6 %copy-start.12 = (bf16[1024,4]{0,1:T(4,128)(2,1)S(1)}, bf16[1024,4]{0,1:T(4,128)(2,1)}, u32[]{:S(2)}) copy-start(bf16[1024,4]{0,1:T(4,128)(2,1)} %param.21) | copy-start | bytes 24580
  7.2 3.6 %copy-start.15 = (f32[4]{0:T(128)S(1)}, f32[4]{0:T(128)}, u32[]{:S(2)}) copy-start(f32[4]{0:T(128)} %param.22) | copy-start | bytes 52
  7.2 3.6 %copy-start.14 = (f32[4]{0:T(128)S(1)}, f32[4]{0:T(128)}, u32[]{:S(2)}) copy-start(f32[4]{0:T(128)} %param.23) | copy-start | bytes 52
  7.2 71.5 %all-gather.7.cloned.1.call-start = ((), (), s32[]{:S(2)}) async-start(), calls=%async_computation.4 | async-start | bytes 1310720 | tf_op jit(solution)/shard_map/all_gather | solution.py:23
  9.5 9.4 %copy-start.16 = (u32[256]{0:T(256)S(1)}, u32[256]{0:T(256)}, u32[]{:S(2)}) copy-start(u32[256]{0:T(256)} %constant.141) | copy-start | bytes 3076
  20.1 3.7 %copy-start.11 = (bf16[1024,512]{1,0:T(8,128)(2,1)S(1)}, bf16[1024,512]{1,0:T(8,128)(2,1)}, u32[]{:S(2)}) copy-start(bf16[1024,512]{1,0:T(8,128)(2,1)} %param.18) | copy-start | bytes 3145732
  22.7 2.0 copy-start.3
  48.1 32.6 %copy-start.9 = (s32[3,256]{1,0:T(4,128)S(1)}, s32[3,256]{1,0:T(4,128)}, u32[]{:S(2)}) copy-start(s32[3,256]{1,0:T(4,128)} %param.27) | copy-start | bytes 9220
  50.3 0.8 copy-start.7
  52.0 89.4 %all-gather.9.cloned.1.call-start = ((), (), s32[]{:S(2)}) async-start(), calls=%async_computation.5 | async-start | bytes 2359296 | tf_op jit(solution)/shard_map/all_gather | solution.py:23
  85.5 37.7 %all-to-all-start.1 = ((s32[64,1,20]{2,1,0:T(1,128)}), s32[64,1,20]{2,1,0:T(1,128)S(1)}, u32[]{:S(2)}, u32[]{:S(2)}) async-start(s32[64,1,20]{2,1,0:T(1,128)} %bitcast.52), calls=%async_computation.1 | async-start | bytes 65536 | tf_op jit(solution)/shard_map/all_to_all | solution.py:183
  130.7 10.7 %copy-start.8 = (f32[8,128,128]{2,1,0:T(8,128)S(1)}, f32[8,128,128]{2,1,0:T(8,128)}, u32[]{:S(2)}) copy-start(f32[8,128,128]{2,1,0:T(8,128)} %copy-done.7) | copy-start | bytes 1572868
  130.7 61.9 %all-to-all-start.2 = ((f32[64,20,256]{2,1,0:T(8,128)}), f32[64,20,256]{2,1,0:T(8,128)}, u32[]{:S(2)}, u32[]{:S(2)}) async-start(f32[64,20,256]{2,1,0:T(8,128)} %broadcast_select_fusion), calls=%async_computation.2 | async-start | bytes 3145728 | tf_op jit(solution)/shard_map/all_to_all | solution.py:192
  141.3 2.7 copy-start.2
  178.8 3.0 copy-start.5
  183.8 3.3 copy-start.6
  183.8 3.3 copy-start.10
  192.5 5.2 %copy-start.4 = (bf16[1024,1024]{1,0:T(8,128)(2,1)S(1)}, bf16[1024,1024]{1,0:T(8,128)(2,1)}, u32[]{:S(2)}) copy-start(bf16[1024,1024]{1,0:T(8,128)(2,1)} %param.16) | copy-start | bytes 6291460
  192.5 53.4 %all-to-all-start = ((f32[4,1024,256]{2,1,0:T(8,128)}), f32[4,1024,256]{2,1,0:T(8,128)}, u32[]{:S(2)}, u32[]{:S(2)}) async-start(f32[4,1024,256]{2,1,0:T(8,128)} %convolution_bitcast_fusion.1), calls=%async_computation | async-start | bytes 8388608 | tf_op jit(solution)/shard_map/all_to_all | solution.py:40
  257.9 50.4 %all-to-all-start.3 = ((f32[64,20,256]{2,1,0:T(8,128)}), f32[64,20,256]{2,1,0:T(8,128)}, u32[]{:S(2)}, u32[]{:S(2)}) async-start(f32[64,20,256]{2,1,0:T(8,128)} %reshape.466), calls=%async_computation.3 | async-start | bytes 3145728 | tf_op jit(solution)/shard_map/all_to_all | solution.py:201
  308.3 17.1 %copy-start.1 = (f32[3,1024,256]{2,1,0:T(8,128)S(1)}, f32[3,1024,256]{2,1,0:T(8,128)}, u32[]{:S(2)}) copy-start(f32[3,1024,256]{2,1,0:T(8,128)} %param.26) | copy-start | bytes 9437188
Sparse Core Ops, SparseCore 0:
  52.1 26.5 all-gather.6
  81.1 39.3 all-gather.8
where the time goes:
time: 333 us; the launch traced here: 332 us
  waiting for transfers between devices  98.8 us (30%)
  matrix products  52.2 us (16%)
  other arithmetic  51.2 us (15%)
  local copies, waits for them, and re-layouts  47.2 us (14%)
  starting transfers between devices  38.1 us (11%)
  blocking collectives  28.5 us (9%)
  between operations  15.9 us (5%)
    all_to_all x1, waiting for transfers between devices, sum_at_owner(): lax.all_to_all(cut_along(array, dim, devices), axis, 0, 0, tiled=True)  41.3 us
    all_to_all x1, waiting for transfers between devices, body(): lax.all_to_all(grad_flat.reshape(owners, merged_cap, column_width), SEQ,...  37.9 us
    all_gather x2, waiting for transfers between devices, carried_in(): pieces = jax.tree.map(lambda part: lax.all_gather(part, axis), total)  19.5 us
    all_gather x2, blocking collectives, carried_in(): pieces = jax.tree.map(lambda part: lax.all_gather(part, axis), total)  16.1 us
    scatter-add x1, other arithmetic, body(): jnp.zeros((levels * codes_here, column_width), jnp.float32).at[safe_rows]  14.5 us
    unnamed x2, blocking collectives  12.4 us
    all_to_all x1, starting transfers between devices, body(): lax.all_to_all(grad_flat.reshape(owners, merged_cap, column_width), SEQ,...  11.5 us
    all_to_all x1, starting transfers between devices, body(): lax.all_to_all(looked_up, SEQ, split_axis=0, concat_axis=0, tiled=True)  10.7 us
  transfers between devices with their start and end apart: 6, of which 3 were waited for; matrix products, arithmetic and copies ran while one was open for 25% of the time, Pallas kernels for 0%

commit v1 on v0

v1 whole, which is shorter than its diff:
```python
import jax
import jax.numpy as jnp
from jax import lax
from jax.experimental import pallas as pl
from jax.experimental.pallas import tpu as pltpu
from jax.sharding import Mesh
from jax.sharding import PartitionSpec as P

SEQ = ("seq_0", "seq_1", "seq_2")
OWNERS = 64
SLOTS = 20
TOTAL = OWNERS * SLOTS
LEVELS = 3
CODES = 1024
FRAMES = 1024
BLOCK = 256
STEPS = FRAMES // BLOCK
QROWS = 256
WIDTH = 256
HEADS = 4
DIM = 128
INNER = HEADS * DIM
PAYLOAD = 10 * 128

f32 = jnp.float32
bf16 = jnp.bfloat16
HIGHEST = lax.Precision.HIGHEST
NT = (((1,), (1,)), ((), ()))


def dot(a, b):
    return jnp.dot(a, b, preferred_element_type=f32)


def dot_exact(a, b):
    return jnp.dot(a, b, preferred_element_type=f32, precision=HIGHEST)


def iota(shape, dim):
    return lax.broadcasted_iota(jnp.int32, shape, dim)


def two_parts(values):
    high = values.astype(bf16)
    low = (values - high.astype(f32)).astype(bf16)
    return jnp.concatenate([high, low], axis=1)


def folded(values):
    half = values.shape[1] // 2
    return values[:, :half] + values[:, half:]


def silu(values):
    return values * jax.nn.sigmoid(values)


def per_head(columns):
    rows = columns.shape[0]
    return jnp.concatenate(
        [jnp.broadcast_to(columns[:, h : h + 1], (rows, DIM)) for h in range(HEADS)], axis=1
    )


def causal_f32():
    return (iota((BLOCK, BLOCK), 0) >= iota((BLOCK, BLOCK), 1)).astype(f32)


def state_step(state, decayed, cum, b_act):
    return state * per_head(jnp.exp(cum[BLOCK - 1 :, :])) + dot(b_act.T, decayed)


def place_codes(ids_ref, slots_ref):
    entries = LEVELS * QROWS
    ids = jnp.concatenate([ids_ref[k : k + 1, :] for k in range(LEVELS)], axis=1)
    level = iota((1, entries), 1) // QROWS
    owner = ids // CODES
    wanted = level * CODES + ids % CODES + 1
    member = (iota((OWNERS, entries), 0) == owner).astype(f32)
    before = (iota((entries, entries), 0) < iota((entries, entries), 1)).astype(bf16)
    rank = jnp.sum(member * dot(member.astype(bf16), before), axis=0, keepdims=True)
    rank = rank.astype(jnp.int32)
    slot = owner * SLOTS + rank
    for k in range(LEVELS):
        slots_ref[k : k + 1, :] = slot[:, k * QROWS : (k + 1) * QROWS]
    ranked = (iota((128, entries), 0) == rank).astype(bf16)
    high = (member * (wanted // 64).astype(f32)).astype(bf16)
    low = (member * (wanted % 64).astype(f32)).astype(bf16)
    return 64.0 * lax.dot_general(high, ranked, NT, preferred_element_type=f32) + lax.dot_general(
        low, ranked, NT, preferred_element_type=f32
    )


def front_kernel(
    frames_ref, gain_ref, x_w_ref, bc_w_ref, dt_w_ref, bias_ref, rate_ref, ids_ref,
    payload_ref, slots_ref, normed_ref, inflow_ref, bc_ref, log_ref,
    state_ref, total_ref,
):
    step = pl.program_id(0)

    @pl.when(step == 0)
    def _():
        state_ref[...] = jnp.zeros_like(state_ref)
        total_ref[...] = jnp.zeros_like(total_ref)
        asked = place_codes(ids_ref, slots_ref)
        for k in range(OWNERS):
            payload_ref[k, :, 1152:1280] = asked[k : k + 1, :]

    frames = frames_ref[...].astype(f32)
    square = jnp.mean(frames * frames, axis=1, keepdims=True)
    normed = (frames * lax.rsqrt(square + 1e-05) * gain_ref[...]).astype(bf16)
    normed_ref[...] = normed
    bc_act = silu(dot(normed, bc_w_ref[...]).astype(bf16).astype(f32)).astype(bf16)
    bc_ref[...] = bc_act
    raw = dot(normed, dt_w_ref[...]) + bias_ref[...]
    dt = jnp.maximum(raw, 0.0) + jnp.log1p(jnp.exp(-jnp.abs(raw)))
    log = -dt * rate_ref[...]
    log_ref[...] = log
    cum = dot_exact(causal_f32(), log)
    x_act = silu(dot(normed, x_w_ref[...]).astype(bf16).astype(f32))
    inflow = x_act * per_head(dt)
    inflow_ref[...] = inflow.astype(bf16)
    last = cum[BLOCK - 1 :, :]
    decayed = (inflow * per_head(jnp.exp(last - cum))).astype(bf16)
    state_ref[...] = state_step(state_ref[...], decayed, cum, bc_act[:, :DIM])
    total_ref[0:1, 0:HEADS] += last

    @pl.when(step == STEPS - 1)
    def _():
        for k in range(OWNERS):
            head, row = k // 16, (k % 16) * 8
            lanes = slice(head * DIM, (head + 1) * DIM)
            for r in range(8):
                payload_ref[k, :, r * 128 : (r + 1) * 128] = state_ref[row + r : row + r + 1, lanes]
            payload_ref[k, :, 1024:1152] = jnp.broadcast_to(
                total_ref[0:1, head : head + 1], (1, 128)
            )


def scan_kernel(arrived_ref, before_ref):
    carried = [jnp.zeros((1, 128), f32) for _ in range(8)]
    for k in range(OWNERS):
        decay = jnp.exp(arrived_ref[k, :, 1024:1152])
        for r in range(8):
            before_ref[k, r : r + 1, :] = carried[r]
            carried[r] = carried[r] * decay + arrived_ref[k, :, r * 128 : (r + 1) * 128]


def local_kernel(
    frames_ref, normed_ref, inflow_ref, bc_ref, log_ref, z_w_ref,
    inner_ref, gate_ref, reach_ref, means_ref,
    state_ref, total_ref,
):
    @pl.when(pl.program_id(0) == 0)
    def _():
        state_ref[...] = jnp.zeros_like(state_ref)
        total_ref[...] = jnp.zeros_like(total_ref)

    gate_ref[...] = silu(dot(normed_ref[...], z_w_ref[...]).astype(bf16).astype(f32))
    pool = jnp.where(
        iota((BLOCK // 4, BLOCK), 0) == iota((BLOCK // 4, BLOCK), 1) // 4, 0.25, 0.0
    ).astype(bf16)
    means = dot(pool, frames_ref[...])
    for g in range(4):
        means_ref[g] = means[:, g * WIDTH : (g + 1) * WIDTH]
    causal = iota((BLOCK, BLOCK), 0) >= iota((BLOCK, BLOCK), 1)
    log = log_ref[...]
    cum = dot_exact(causal.astype(f32), log)
    cum_rows = lax.dot_general(
        jnp.concatenate([log, jnp.zeros((BLOCK, 128 - HEADS), f32)], axis=1).T,
        causal.astype(f32), NT, preferred_element_type=f32, precision=HIGHEST,
    )
    b_act, c_act = bc_ref[:, :DIM], bc_ref[:, DIM:]
    inflow = inflow_ref[...]
    scores = jnp.where(causal, lax.dot_general(c_act, b_act, NT, preferred_element_type=f32), 0.0)
    carried = dot(c_act, state_ref[...].astype(bf16)) * per_head(jnp.exp(cum))
    for h in range(HEADS):
        lanes = slice(h * DIM, (h + 1) * DIM)
        gaps = jnp.minimum(cum[:, h : h + 1] - cum_rows[h : h + 1, :], 0.0)
        mixed = (jnp.exp(gaps) * scores).astype(bf16)
        inner_ref[:, lanes] = dot(mixed, inflow[:, lanes]) + carried[:, lanes]
    reach_ref[...] = jnp.exp(cum + total_ref[0:1, 0:HEADS])
    last = cum[BLOCK - 1 :, :]
    total_ref[0:1, 0:HEADS] += last
    decayed = (inflow.astype(f32) * per_head(jnp.exp(last - cum))).astype(bf16)
    state_ref[...] = state_step(state_ref[...], decayed, cum, b_act)


def outer_kernel(
    book_ref, inner_ref, gate_ref, reach_ref, c_ref, incoming_ref, gain_ref, out_w_ref,
    out_0, out_1, out_2, out_3, pooled_ref,
):
    step = pl.program_id(0)
    pool = jnp.where(
        iota((BLOCK // 4, BLOCK), 0) == iota((BLOCK // 4, BLOCK), 1) // 4, 0.25, 0.0
    ).astype(bf16)
    c_act = c_ref[...]
    for h in range(HEADS):
        lanes = slice(h * DIM, (h + 1) * DIM)
        carried = dot(c_act, incoming_ref[lanes, :].astype(bf16))
        rows = (inner_ref[:, lanes] + carried * reach_ref[:, h : h + 1]) * gate_ref[:, lanes]
        square = jnp.mean(rows * rows, axis=1, keepdims=True)
        rows = (rows * lax.rsqrt(square + 1e-05) * gain_ref[:, lanes]).astype(bf16)
        pooled_ref[pl.ds(step * (BLOCK // 4), BLOCK // 4), lanes] = dot(pool, rows)

    @pl.when(step == STEPS - 1)
    def _():
        pooled = pooled_ref[...]
        high = pooled.astype(bf16)
        low = (pooled - high.astype(f32)).astype(bf16)
        both = jnp.concatenate([high, low], axis=0)
        for shift, out in enumerate((out_0, out_1, out_2, out_3)):
            start = pl.multiple_of(((book_ref[0] + shift) % 4) * WIDTH, WIDTH)
            product = dot(both, out_w_ref[:, pl.ds(start, WIDTH)])
            out[...] = product[:QROWS] + product[QROWS:]


def lookup_kernel(codes_ref, table_ref, found_ref, parts_ref):
    @pl.when(pl.program_id(0) == 0)
    def _():
        parts_ref[...] = two_parts(table_ref[...])

    rows = codes_ref.shape[0]
    chosen = (codes_ref[...] == iota((rows, LEVELS * CODES), 1) + 1).astype(bf16)
    found = folded(dot(chosen, parts_ref[...]))
    found_ref[pl.ds(0, rows, 2), :] = found[:, :128]
    found_ref[pl.ds(1, rows, 2), :] = found[:, 128:]


def joined_rows(ref):
    half = ref.shape[0] // 2
    return jnp.concatenate([ref[pl.ds(0, half, 2), :], ref[pl.ds(1, half, 2), :]], axis=1)


def taken_kernel(found_ref, slots_ref, terms_ref, taken_ref):
    found = joined_rows(found_ref)
    parts = two_parts(found)
    slots = jnp.concatenate(
        [slots_ref[...].astype(f32), jnp.zeros((8 - LEVELS, QROWS), f32)], axis=0
    )
    same = (iota((QROWS, QROWS), 0) == iota((QROWS, QROWS), 1)).astype(f32)
    columns = lax.dot_general(same, slots, NT, preferred_element_type=f32, precision=HIGHEST)
    columns = columns.astype(jnp.int32)
    taken = jnp.zeros((QROWS, WIDTH), f32)
    terms = found
    for k in range(LEVELS):
        if k:
            spread = (iota((TOTAL, QROWS), 0) == slots_ref[k : k + 1, :]).astype(bf16)
            terms = terms + folded(dot(spread, two_parts(taken)))
        picks = (columns[:, k : k + 1] == iota((QROWS, TOTAL), 1)).astype(bf16)
        taken = taken + folded(dot(picks, parts))
    terms_ref[...] = terms
    taken_ref[...] = taken


def residual_kernel(
    book_ref, own_ref, from_1, from_2, from_3, means_ref, taken_ref, terms_ref, slots_ref,
    residual_ref, grads_ref,
):
    pooled = own_ref[...] + from_1[...] + from_2[...] + from_3[...] + means_ref[0]
    residual_ref[...] = pooled - taken_ref[...]
    place = iota((TOTAL, QROWS), 0)
    spread = place == slots_ref[0:1, :]
    for k in range(1, LEVELS):
        spread = spread | (place == slots_ref[k : k + 1, :])
    grads = terms_ref[...] - folded(dot(spread.astype(bf16), two_parts(pooled)))
    grads_ref[pl.ds(0, TOTAL, 2), :] = grads[:, :128]
    grads_ref[pl.ds(1, TOTAL, 2), :] = grads[:, 128:]


def table_kernel(codes_ref, grads_ref, table_ref, parts_ref):
    step = pl.program_id(0)

    @pl.when(step == 0)
    def _():
        parts_ref[...] = two_parts(joined_rows(grads_ref))

    rows = table_ref.shape[0]
    chosen = (codes_ref[...] == iota((rows, TOTAL), 0) + (step * rows + 1)).astype(bf16)
    table_ref[...] = folded(dot(chosen, parts_ref[...]))


def shape(*dims, dtype=f32):
    return jax.ShapeDtypeStruct(dims, dtype)


def whole(*dims):
    return pl.BlockSpec(dims, lambda *_: (0,) * len(dims))


def rows_of(rows, columns):
    return pl.BlockSpec((rows, columns), lambda i, *_: (i, 0))


def settings(mib):
    return pltpu.CompilerParams(vmem_limit_bytes=mib * 2**20)


def exchange(array):
    return lax.all_to_all(array, SEQ, split_axis=0, concat_axis=0, tiled=True)


def body(
    frames, norm_gain, x_weight, z_weight, bc_weight, dt_weight, dt_bias, decay_rate,
    out_gain, out_weight, codebook, code_ids,
):
    book = lax.axis_index("book").reshape(1)
    payload, slots, normed, inflow, bc_act, log = pl.pallas_call(
        front_kernel,
        grid=(STEPS,),
        in_specs=[
            rows_of(BLOCK, 1024), whole(1, 1024), whole(1024, INNER), whole(1024, 256),
            whole(1024, HEADS), whole(1, HEADS), whole(1, HEADS), whole(LEVELS, QROWS),
        ],
        out_specs=[
            whole(OWNERS, 1, PAYLOAD), whole(LEVELS, QROWS), rows_of(BLOCK, 1024),
            rows_of(BLOCK, INNER), rows_of(BLOCK, 256), rows_of(BLOCK, HEADS),
        ],
        out_shape=[
            shape(OWNERS, 1, PAYLOAD), shape(LEVELS, QROWS, dtype=jnp.int32),
            shape(FRAMES, 1024, dtype=bf16), shape(FRAMES, INNER, dtype=bf16),
            shape(FRAMES, 256, dtype=bf16), shape(FRAMES, HEADS),
        ],
        scratch_shapes=[pltpu.VMEM((DIM, INNER), f32), pltpu.VMEM((8, 128), f32)],
        compiler_params=settings(32),
        name="front",
    )(
        frames, norm_gain.reshape(1, -1), x_weight, bc_weight, dt_weight,
        dt_bias.reshape(1, -1), decay_rate.reshape(1, -1), code_ids,
    )
    arrived = exchange(payload)
    inner, gate, reach, means = pl.pallas_call(
        local_kernel,
        grid=(STEPS,),
        in_specs=[
            rows_of(BLOCK, 1024), rows_of(BLOCK, 1024), rows_of(BLOCK, INNER),
            rows_of(BLOCK, 256), rows_of(BLOCK, HEADS), whole(1024, INNER),
        ],
        out_specs=[
            rows_of(BLOCK, INNER), rows_of(BLOCK, INNER), rows_of(BLOCK, HEADS),
            pl.BlockSpec((4, BLOCK // 4, WIDTH), lambda i: (0, i, 0)),
        ],
        out_shape=[
            shape(FRAMES, INNER), shape(FRAMES, INNER), shape(FRAMES, HEADS),
            shape(4, QROWS, WIDTH),
        ],
        scratch_shapes=[pltpu.VMEM((DIM, INNER), f32), pltpu.VMEM((8, 128), f32)],
        compiler_params=settings(32),
        cost_estimate=pl.CostEstimate(flops=4 * 10**9, bytes_accessed=12 * 2**20, transcendentals=10**6),
        name="local",
    )(frames, normed, inflow, bc_act, log, z_weight)
    before = pl.pallas_call(
        scan_kernel,
        out_shape=shape(OWNERS, 8, 128),
        name="scan",
    )(arrived)
    incoming = exchange(before).reshape(INNER, DIM)
    asked = arrived[:, 0, 1152 : 1152 + SLOTS].astype(jnp.int32)
    codes_column = asked.reshape(TOTAL, 1)
    codes_row = asked.reshape(1, TOTAL)
    found = pl.pallas_call(
        lookup_kernel,
        grid=(5,),
        in_specs=[rows_of(TOTAL // 5, 1), whole(LEVELS * CODES, WIDTH)],
        out_specs=rows_of(2 * TOTAL // 5, 128),
        out_shape=shape(2 * TOTAL, 128),
        scratch_shapes=[pltpu.VMEM((LEVELS * CODES, 2 * WIDTH), bf16)],
        compiler_params=settings(32),
        cost_estimate=pl.CostEstimate(flops=6 * 10**9, bytes_accessed=5 * 2**20, transcendentals=0),
        name="lookup",
    )(codes_column, codebook.reshape(LEVELS * CODES, WIDTH))
    fetched = exchange(found.reshape(OWNERS, 2 * SLOTS, 128)).reshape(2 * TOTAL, 128)
    shares = pl.pallas_call(
        outer_kernel,
        grid_spec=pltpu.PrefetchScalarGridSpec(
            num_scalar_prefetch=1,
            grid=(STEPS,),
            in_specs=[
                rows_of(BLOCK, INNER), rows_of(BLOCK, INNER), rows_of(BLOCK, HEADS),
                pl.BlockSpec((BLOCK, DIM), lambda i, *_: (i, 1)),
                whole(INNER, DIM), whole(1, INNER), whole(INNER, 1024),
            ],
            out_specs=[whole(QROWS, WIDTH)] * 4,
            scratch_shapes=[pltpu.VMEM((QROWS, INNER), f32)],
        ),
        out_shape=[shape(QROWS, WIDTH)] * 4,
        compiler_params=settings(32),
        cost_estimate=pl.CostEstimate(flops=2 * 10**9, bytes_accessed=8 * 2**20, transcendentals=10**5),
        name="outer",
    )(book, inner, gate, reach, bc_act, incoming, out_gain.reshape(1, -1), out_weight)
    moved = [
        lax.ppermute(shares[d], "book", [(i, (i + d) % 4) for i in range(4)]) for d in (1, 2, 3)
    ]
    terms, taken = pl.pallas_call(
        taken_kernel,
        out_shape=[shape(TOTAL, WIDTH), shape(QROWS, WIDTH)],
        compiler_params=settings(48),
        cost_estimate=pl.CostEstimate(flops=3 * 10**9, bytes_accessed=3 * 2**20, transcendentals=0),
        name="taken",
    )(fetched, slots)
    residual, grads = pl.pallas_call(
        residual_kernel,
        grid_spec=pltpu.PrefetchScalarGridSpec(
            num_scalar_prefetch=1,
            grid=(1,),
            in_specs=[whole(QROWS, WIDTH)] * 4
            + [
                pl.BlockSpec((1, QROWS, WIDTH), lambda i, book: (book[0], 0, 0)),
                whole(QROWS, WIDTH), whole(TOTAL, WIDTH), whole(LEVELS, QROWS),
            ],
            out_specs=[whole(QROWS, WIDTH), whole(2 * TOTAL, 128)],
        ),
        out_shape=[shape(QROWS, WIDTH), shape(2 * TOTAL, 128)],
        compiler_params=settings(48),
        name="residual",
    )(book, shares[0], *moved, means, taken, terms, slots)
    returned = exchange(grads.reshape(OWNERS, 2 * SLOTS, 128)).reshape(2 * TOTAL, 128)
    table = pl.pallas_call(
        table_kernel,
        grid=(6,),
        in_specs=[whole(1, TOTAL), whole(2 * TOTAL, 128)],
        out_specs=rows_of(LEVELS * CODES // 6, WIDTH),
        out_shape=shape(LEVELS * CODES, WIDTH),
        scratch_shapes=[pltpu.VMEM((TOTAL, 2 * WIDTH), bf16)],
        compiler_params=settings(32),
        name="table",
    )(codes_row, returned)
    return residual, table.reshape(LEVELS, CODES, WIDTH)


def solution(mesh):
    finer = Mesh(
        mesh.devices.reshape(8, 4, 2, mesh.shape["book"]), ("seq_0", "seq_1", "seq_2", "book")
    )
    placed = (
        P(SEQ, None), P(), P(None, "book"), P(None, "book"), P(), P(None, "book"), P("book"),
        P("book"), P("book"), P("book", None), P(None, SEQ, "book"), P(None, SEQ),
    )
    return jax.shard_map(
        body,
        mesh=finer,
        in_specs=placed,
        out_specs=(P(SEQ, "book"), P(None, SEQ, "book")),
        check_vma=False,
    )
```

time: 333 us -> 162 us (0.49)
  waiting for transfers between devices: 98.8 us -> 46 us
  matrix products: 52.2 us -> 0 us
  other arithmetic: 51.2 us -> 1.64 us
  Pallas kernels: 0 us -> 38.2 us
  local copies, waits for them, and re-layouts: 47.2 us -> 21.5 us
  between operations: 15.9 us -> 0.86 us
  starting transfers between devices: 38.1 us -> 25.8 us
    dot_general x26 -> x0, matrix products: 52.2 us -> none  [the longest x4 9.16 us: block_pass(): jnp.einsum('tjh,jhp->thp', weights * scores[:, :, None], inflow, precisio...]
    pallas_call x0 -> x8, Pallas kernels: none -> 38.2 us  [the longest x1 7.27 us: body(): pl.pallas_call(front_kernel, grid=(STEPS,), in_specs=[rows_of(BLOCK, 1024...]
    all_to_all x4 -> x3, waiting for transfers between devices: 79.3 us -> 46 us  [exchange(): return lax.all_to_all(array, SEQ, split_axis=0, concat_axis=0, tiled=True)]
    all_to_all x0 -> x1, blocking collectives: none -> 27.2 us  [exchange(): return lax.all_to_all(array, SEQ, split_axis=0, concat_axis=0, tiled=True)]
    all_gather x2 -> x0, waiting for transfers between devices: 19.5 us -> none  [carried_in(): pieces = jax.tree.map(lambda part: lax.all_gather(part, axis), total)]
    all_to_all x4 -> x3, starting transfers between devices: 38 us -> 20.9 us  [exchange(): return lax.all_to_all(array, SEQ, split_axis=0, concat_axis=0, tiled=True)]
    all_gather x2 -> x0, blocking collectives: 16.1 us -> none  [carried_in(): pieces = jax.tree.map(lambda part: lax.all_gather(part, axis), total)]
    unnamed x43 -> x51, local copies, waits for them, and re-layouts: 5.97 us -> 21.1 us
  transfers between devices with their start and end apart: 6 -> 6, of which waited for: 3 -> 3; matrix products, arithmetic and copies ran while one was open for 25% -> 1% of each run, Pallas kernels for 0% -> 13%
where the time goes in v1:
time: 162 us; the launch traced here: 161 us
  waiting for transfers between devices  46 us (28%)
  Pallas kernels  38.2 us (24%)
  blocking collectives  27.2 us (17%)
  starting transfers between devices  25.8 us (16%)
  local copies, waits for them, and re-layouts  21.5 us (13%)
  other arithmetic  1.64 us (1%)
    all_to_all x3, waiting for transfers between devices, exchange(): return lax.all_to_all(array, SEQ, split_axis=0, concat_axis=0, tiled=True)  46 us
    all_to_all x1, blocking collectives, exchange(): return lax.all_to_all(array, SEQ, split_axis=0, concat_axis=0, tiled=True)  27.2 us
    unnamed x51, local copies, waits for them, and re-layouts  21.1 us
    all_to_all x3, starting transfers between devices, exchange(): return lax.all_to_all(array, SEQ, split_axis=0, concat_axis=0, tiled=True)  20.9 us
    pallas_call x1, Pallas kernels, body(): pl.pallas_call(front_kernel, grid=(STEPS,), in_specs=[rows_of(BLOCK, 1024...  7.27 us
    pallas_call x1, Pallas kernels, body(): pl.pallas_call(local_kernel, grid=(STEPS,), in_specs=[rows_of(BLOCK, 1024...  6.81 us
    pallas_call x1, Pallas kernels, body(): pl.pallas_call(table_kernel, grid=(6,), in_specs=[whole(1, TOTAL), whole(...  6.08 us
    pallas_call x1, Pallas kernels, body(): pl.pallas_call(outer_kernel, grid_spec=pltpu.PrefetchScalarGridSpec(num_s...  5.95 us
  transfers between devices with their start and end apart: 6, of which 3 were waited for; matrix products, arithmetic and copies ran while one was open for 1% of the time, Pallas kernels for 13%

profile of v1, /device:TPU:1, one launch (start us, length us, event | category | flops | bytes accessed | tf_op | source)
XLA Modules:
  0.0 161.1 jit_solution(6087080295618461964)
XLA Ops:
  1.5 1.6 copy-done
  3.1 1.2 copy-done.3
  8.1 7.3 %front.1 = (f32[64,1,1280]{2,1,0:T(1,128)S(1)}, s32[3,256]{1,0:T(4,128)S(1)}, bf16[1024,1024]{1,0:T(8,128)(2,1)S(1)}, bf16[1024,512]{1,0:T(8,128)(2,1)S(1)}, bf1...) custom-call(bf16[1024,1024]{1,0:T(8,128)(2,1)S(1)} %copy-done, f32[1,1024]{1,0:T(1,128)S(1)} %bitcast.17, ...), custom_call_target="tpu_custom_call" | custom-call | tf_op jit(solution)/shard_map/front/pallas_call | solution.py:308
  15.4 1.3 copy-done.14
  19.3 27.2 %all_to_all.20.arrived_ref = f32[64,1,1280]{2,1,0:T(1,128)} all-to-all(f32[64,1,1280]{2,1,0:T(1,128)S(1)} %get-tuple-element.27), channel_id=1, replica_groups=mesh['seq_0'=8,'seq_1'=4,'seq_2'=2,'book'=4] {'seq_0','seq_1','seq_2'}, dimensions={0} | all-to-all | bytes 655360 | tf_op jit(solution)/shard_map/all_to_all | solution.py:300
  46.5 1.9 %scan.1 = f32[64,8,128]{2,1,0:T(8,128)} custom-call(f32[64,1,1280]{2,1,0:T(1,128)} %all_to_all.20.arrived_ref), custom_call_target="tpu_custom_call" | custom-call | tf_op jit(solution)/shard_map/scan/pallas_call | solution.py:352
  48.3 5.1 %all-to-all-start.1 = ((f32[64,8,128]{2,1,0:T(8,128)}), f32[64,8,128]{2,1,0:T(8,128)S(1)}, u32[]{:S(2)}, u32[]{:S(2)}) async-start(f32[64,8,128]{2,1,0:T(8,128)} %scan.1), calls=%async_computation.1 | async-start | bytes 524288 | tf_op jit(solution)/shard_map/all_to_all | solution.py:300
  54.5 1.9 %copy-done.13 = f32[3,1024,256]{2,1,0:T(8,128)S(1)} copy-done((f32[3,1024,256]{2,1,0:T(8,128)S(1)}, f32[3,1024,256]{2,1,0:T(8,128)}, u32[]{:S(2)}) %copy-start.13) | copy-done | bytes 3145752
  56.4 5.5 %lookup.1 = f32[2560,128]{1,0:T(8,128)S(1)} custom-call(s32[1280,1]{1,0:T(8,128)S(1)} %convert_element_type.26.codes_ref, f32[3072,256]{1,0:T(8,128)S(1)} %bitcast.20), custom_call_target="tpu_custom_call" | custom-call | flops 6000000000 | bytes 5242880 | tf_op jit(solution)/shard_map/lookup/pallas_call | solution.py:361
  63.0 3.6 %all-to-all-done.1 = f32[64,8,128]{2,1,0:T(8,128)S(1)} async-done(((f32[64,8,128]{2,1,0:T(8,128)}), f32[64,8,128]{2,1,0:T(8,128)S(1)}, u32[]{:S(2)}, u32[]{:S(2)}) %all-to-all-start.1) | async-done | bytes 262176 | tf_op jit(solution)/shard_map/all_to_all | solution.py:300
  67.3 6.9 %all-to-all-start.2 = ((f32[64,40,128]{2,1,0:T(8,128)}), f32[64,40,128]{2,1,0:T(8,128)S(1)}, u32[]{:S(2)}, u32[]{:S(2)}) async-start(f32[64,40,128]{2,1,0:T(8,128)} %bitcast.15), calls=%async_computation.2 | async-start | bytes 2621440 | tf_op jit(solution)/shard_map/all_to_all | solution.py:300
  74.2 1.6 copy-done.15
  75.8 1.2 copy-done.16
  77.0 1.2 copy-done.19
  80.3 6.8 %local.1 = (f32[1024,512]{1,0:T(8,128)S(1)}, f32[1024,512]{1,0:T(8,128)S(1)}, f32[1024,4]{1,0:T(8,128)S(1)}, f32[4,256,256]{2,1,0:T(8,128)S(1)}) custom-call(bf16[1024,1024]{1,0:T(8,128)(2,1)S(1)} %copy-done.1, bf16[1024,1024]{1,0:T(8,128)(2,1)S(1)} %copy-done.15, bf16[1024,512]{1,0:T(8,128)(2,1)S(1)} %copy-done.19, bf16[1024,256]{1,0:T(8,128)(2,1)S(1)} %copy-done.21, ...), custom_call_target="tpu_custom_call" | custom-call | flops 4000000000 | bytes 12582912 | tf_op jit(solution)/shard_map/local/pallas_call | solution.py:332
  87.2 5.9 %outer.1 = (f32[256,256]{1,0:T(8,128)S(1)}, f32[256,256]{1,0:T(8,128)S(1)}, f32[256,256]{1,0:T(8,128)S(1)}, f32[256,256]{1,0:T(8,128)S(1)}) custom-call(s32[1]{0:T(128)} %bitcast.book_ref, f32[1024,512]{1,0:T(8,128)S(1)} %get-tuple-element.24.inner_ref, f32[1024,512]{1,0:T(8,128)S(1)} %get-tuple-element.25.gate_ref, ...), custom_call_target="tpu_custom_call" | custom-call | flops 2000000000 | bytes 8388608 | tf_op jit(solution)/shard_map/outer/pallas_call | solution.py:373
  93.1 1.3 collective-permute-start
  94.4 2.4 %collective-permute-start.1 = (f32[256,256]{1,0:T(8,128)S(1)}, f32[256,256]{1,0:T(8,128)S(1)}, u32[]{:S(2)}, u32[]{:S(2)}) collective-permute-start(f32[256,256]{1,0:T(8,128)S(1)} %get-tuple-element.30), channel_id=1, source_target_pairs={{0,2},{1,3},{2,0},{3,1},{4,6},{5,7},{6,4},{7,5},{8,10},{9,11},{10,... | collective-permute-start | bytes 786440 | tf_op jit(solution)/shard_map/ppermute | solution.py:392
  98.0 9.7 %all-to-all-done.2 = f32[64,40,128]{2,1,0:T(8,128)S(1)} async-done(((f32[64,40,128]{2,1,0:T(8,128)}), f32[64,40,128]{2,1,0:T(8,128)S(1)}, u32[]{:S(2)}, u32[]{:S(2)}) %all-to-all-start.2) | async-done | bytes 1310752 | tf_op jit(solution)/shard_map/all_to_all | solution.py:300
  107.8 2.9 %taken.1 = (f32[1280,256]{1,0:T(8,128)S(1)}, f32[256,256]{1,0:T(8,128)S(1)}) custom-call(f32[2560,128]{1,0:T(8,128)S(1)} %bitcast.14, s32[3,256]{1,0:T(4,128)S(1)} %get-tuple-element.33.slots_ref), custom_call_target="tpu_custom_call" | custom-call | flops 3000000000 | bytes 3145728 | tf_op jit(solution)/shard_map/taken/pallas_call | solution.py:394
  110.8 1.7 %residual.1 = (f32[256,256]{1,0:T(8,128)}, f32[2560,128]{1,0:T(8,128)}) custom-call(s32[1]{0:T(128)} %bitcast.book_ref, f32[256,256]{1,0:T(8,128)S(1)} %get-tuple-element.28.own_ref, f32[256,256]{1,0:T(8,128)S(1)} %collective-permute-done.from_1, f32[256,256]{1,0:T(8,128)S(1)} %collective-permute-done.1.from_2, ...), custom_call_target="tpu_custom_call" | custom-call | tf_op jit(solution)/shard_map/residual/pallas_call | solution.py:401
  112.5 8.9 %all-to-all-start.3 = ((f32[64,40,128]{2,1,0:T(8,128)}), f32[64,40,128]{2,1,0:T(8,128)S(1)}, u32[]{:S(2)}, u32[]{:S(2)}) async-start(f32[64,40,128]{2,1,0:T(8,128)} %bitcast.9), calls=%async_computation.3 | async-start | bytes 2621440 | tf_op jit(solution)/shard_map/all_to_all | solution.py:300
  122.3 32.7 %all-to-all-done.3 = f32[64,40,128]{2,1,0:T(8,128)S(1)} async-done(((f32[64,40,128]{2,1,0:T(8,128)}), f32[64,40,128]{2,1,0:T(8,128)S(1)}, u32[]{:S(2)}, u32[]{:S(2)}) %all-to-all-start.3) | async-done | bytes 1310752 | tf_op jit(solution)/shard_map/all_to_all | solution.py:300
  155.0 6.1 %table.1 = f32[3072,256]{1,0:T(8,128)} custom-call(s32[1,1280]{1,0:T(1,128)S(1)} %convert_element_type.25.codes_ref, f32[2560,128]{1,0:T(8,128)S(1)} %bitcast.13), custom_call_target="tpu_custom_call" | custom-call | tf_op jit(solution)/shard_map/table/pallas_call | solution.py:418
  (52 shorter events, 14.2 us)
Async XLA Ops:
  1.5 1.6 copy-start
  3.1 1.2 copy-start.3
  4.4 1.0 copy-start.6
  15.4 1.3 copy-start.14
  16.7 1.0 copy-start.18
  48.3 18.3 %all-to-all-start.1 = ((f32[64,8,128]{2,1,0:T(8,128)}), f32[64,8,128]{2,1,0:T(8,128)S(1)}, u32[]{:S(2)}, u32[]{:S(2)}) async-start(f32[64,8,128]{2,1,0:T(8,128)} %scan.1), calls=%async_computation.1 | async-start | bytes 524288 | tf_op jit(solution)/shard_map/all_to_all | solution.py:300
  54.5 1.9 %copy-start.13 = (f32[3,1024,256]{2,1,0:T(8,128)S(1)}, f32[3,1024,256]{2,1,0:T(8,128)}, u32[]{:S(2)}) copy-start(f32[3,1024,256]{2,1,0:T(8,128)} %param.22) | copy-start | bytes 9437188
  61.9 1.1 copy-start.2
  63.0 11.1 %copy-start.1 = (bf16[1024,1024]{1,0:T(8,128)(2,1)S(1)}, bf16[1024,1024]{1,0:T(8,128)(2,1)}, u32[]{:S(2)}) copy-start(bf16[1024,1024]{1,0:T(8,128)(2,1)} %frames_ref.3) | copy-start | bytes 6291460
  67.3 40.5 %all-to-all-start.2 = ((f32[64,40,128]{2,1,0:T(8,128)}), f32[64,40,128]{2,1,0:T(8,128)S(1)}, u32[]{:S(2)}, u32[]{:S(2)}) async-start(f32[64,40,128]{2,1,0:T(8,128)} %bitcast.15), calls=%async_computation.2 | async-start | bytes 2621440 | tf_op jit(solution)/shard_map/all_to_all | solution.py:300
  74.2 1.6 copy-start.15
  75.8 1.2 copy-start.16
  77.0 1.2 copy-start.19
  78.2 1.0 copy-start.21
  79.3 1.0 copy-start.23
  80.3 6.8 %copy-start.8 = (f32[64,8,128]{2,1,0:T(8,128)S(1)}, f32[64,8,128]{2,1,0:T(8,128)}, u32[]{:S(2)}) copy-start(f32[64,8,128]{2,1,0:T(8,128)} %copy-done.7) | copy-start | bytes 786436
  80.3 6.8 %copy-start.17 = (bf16[512,1024]{1,0:T(8,128)(2,1)S(1)}, bf16[512,1024]{1,0:T(8,128)(2,1)}, u32[]{:S(2)}) copy-start(bf16[512,1024]{1,0:T(8,128)(2,1)} %out_w_ref.1) | copy-start | bytes 3145732
  80.3 6.9 %copy-start.24 = (f32[512]{0:T(512)S(1)}, f32[512]{0:T(512)}, u32[]{:S(2)}) copy-start(f32[512]{0:T(512)} %param.20) | copy-start | bytes 6148
  87.1 6.0 %copy-start.4 = (f32[4,256,256]{2,1,0:T(8,128)}, f32[4,256,256]{2,1,0:T(8,128)S(1)}, u32[]{:S(2)}) copy-start(f32[4,256,256]{2,1,0:T(8,128)S(1)} %get-tuple-element.32.means_ref) | copy-start | bytes 3145732
  93.1 17.6 %collective-permute-start = (f32[256,256]{1,0:T(8,128)S(1)}, f32[256,256]{1,0:T(8,128)S(1)}, u32[]{:S(2)}, u32[]{:S(2)}) collective-permute-start(f32[256,256]{1,0:T(8,128)S(1)} %get-tuple-element.29), channel_id=1, source_target_pairs={{0,1},{1,2},{2,3},{3,0},{4,5},{5,6},{6,7},{7,4},{8,9},{9,10},{10,1... | collective-permute-start | bytes 786440 | tf_op jit(solution)/shard_map/ppermute | solution.py:392
  94.4 16.3 %collective-permute-start.1 = (f32[256,256]{1,0:T(8,128)S(1)}, f32[256,256]{1,0:T(8,128)S(1)}, u32[]{:S(2)}, u32[]{:S(2)}) collective-permute-start(f32[256,256]{1,0:T(8,128)S(1)} %get-tuple-element.30), channel_id=1, source_target_pairs={{0,2},{1,3},{2,0},{3,1},{4,6},{5,7},{6,4},{7,5},{8,10},{9,11},{10,... | collective-permute-start | bytes 786440 | tf_op jit(solution)/shard_map/ppermute | solution.py:392
  96.9 13.9 %collective-permute-start.2 = (f32[256,256]{1,0:T(8,128)S(1)}, f32[256,256]{1,0:T(8,128)S(1)}, u32[]{:S(2)}, u32[]{:S(2)}) collective-permute-start(f32[256,256]{1,0:T(8,128)S(1)} %get-tuple-element.31), channel_id=1, source_target_pairs={{0,3},{1,0},{2,1},{3,2},{4,7},{5,4},{6,5},{7,6},{8,11},{9,8},{10,9... | collective-permute-start | bytes 786440 | tf_op jit(solution)/shard_map/ppermute | solution.py:392
  107.8 3.0 %copy-start.5 = (f32[4,256,256]{2,1,0:T(8,128)S(1)}, f32[4,256,256]{2,1,0:T(8,128)}, u32[]{:S(2)}) copy-start(f32[4,256,256]{2,1,0:T(8,128)} %copy-done.4) | copy-start | bytes 3145732
  112.5 42.5 %all-to-all-start.3 = ((f32[64,40,128]{2,1,0:T(8,128)}), f32[64,40,128]{2,1,0:T(8,128)S(1)}, u32[]{:S(2)}, u32[]{:S(2)}) async-start(f32[64,40,128]{2,1,0:T(8,128)} %bitcast.9), calls=%async_computation.3 | async-start | bytes 2621440 | tf_op jit(solution)/shard_map/all_to_all | solution.py:300
  (7 other events, 5.0 us)

commit v2 on v1

--- a/solution.py
+++ b/solution.py
@@ -322,7 +322,7 @@
             shape(FRAMES, 256, dtype=bf16), shape(FRAMES, HEADS),
         ],
         scratch_shapes=[pltpu.VMEM((DIM, INNER), f32), pltpu.VMEM((8, 128), f32)],
-        compiler_params=settings(32),
+        compiler_params=settings(62),
         name="front",
     )(
         frames, norm_gain.reshape(1, -1), x_weight, bc_weight, dt_weight,
@@ -345,13 +345,15 @@
             shape(4, QROWS, WIDTH),
         ],
         scratch_shapes=[pltpu.VMEM((DIM, INNER), f32), pltpu.VMEM((8, 128), f32)],
-        compiler_params=settings(32),
+        compiler_params=settings(62),
         cost_estimate=pl.CostEstimate(flops=4 * 10**9, bytes_accessed=12 * 2**20, transcendentals=10**6),
         name="local",
     )(frames, normed, inflow, bc_act, log, z_weight)
+    arrived, inner = lax.optimization_barrier((arrived, inner))
     before = pl.pallas_call(
         scan_kernel,
         out_shape=shape(OWNERS, 8, 128),
+        compiler_params=settings(16),
         name="scan",
     )(arrived)
     incoming = exchange(before).reshape(INNER, DIM)
@@ -365,7 +367,7 @@
         out_specs=rows_of(2 * TOTAL // 5, 128),
         out_shape=shape(2 * TOTAL, 128),
         scratch_shapes=[pltpu.VMEM((LEVELS * CODES, 2 * WIDTH), bf16)],
-        compiler_params=settings(32),
+        compiler_params=settings(62),
         cost_estimate=pl.CostEstimate(flops=6 * 10**9, bytes_accessed=5 * 2**20, transcendentals=0),
         name="lookup",
     )(codes_column, codebook.reshape(LEVELS * CODES, WIDTH))
@@ -384,7 +386,7 @@
             scratch_shapes=[pltpu.VMEM((QROWS, INNER), f32)],
         ),
         out_shape=[shape(QROWS, WIDTH)] * 4,
-        compiler_params=settings(32),
+        compiler_params=settings(62),
         cost_estimate=pl.CostEstimate(flops=2 * 10**9, bytes_accessed=8 * 2**20, transcendentals=10**5),
         name="outer",
     )(book, inner, gate, reach, bc_act, incoming, out_gain.reshape(1, -1), out_weight)
@@ -394,7 +396,7 @@
     terms, taken = pl.pallas_call(
         taken_kernel,
         out_shape=[shape(TOTAL, WIDTH), shape(QROWS, WIDTH)],
-        compiler_params=settings(48),
+        compiler_params=settings(40),
         cost_estimate=pl.CostEstimate(flops=3 * 10**9, bytes_accessed=3 * 2**20, transcendentals=0),
         name="taken",
     )(fetched, slots)
@@ -411,7 +413,7 @@
             out_specs=[whole(QROWS, WIDTH), whole(2 * TOTAL, 128)],
         ),
         out_shape=[shape(QROWS, WIDTH), shape(2 * TOTAL, 128)],
-        compiler_params=settings(48),
+        compiler_params=settings(40),
         name="residual",
     )(book, shares[0], *moved, means, taken, terms, slots)
     returned = exchange(grads.reshape(OWNERS, 2 * SLOTS, 128)).reshape(2 * TOTAL, 128)
@@ -422,7 +424,7 @@
         out_specs=rows_of(LEVELS * CODES // 6, WIDTH),
         out_shape=shape(LEVELS * CODES, WIDTH),
         scratch_shapes=[pltpu.VMEM((TOTAL, 2 * WIDTH), bf16)],
-        compiler_params=settings(32),
+        compiler_params=settings(40),
         name="table",
     )(codes_row, returned)
     return residual, table.reshape(LEVELS, CODES, WIDTH)

time: 162 us -> 151 us (0.932)
  blocking collectives: 27.2 us -> 0 us
  local copies, waits for them, and re-layouts: 21.5 us -> 2.8 us
  waiting for transfers between devices: 46 us -> 61.9 us
  starting transfers between devices: 25.8 us -> 36.4 us
  Pallas kernels: 38.2 us -> 48.2 us
    all_to_all x1 -> x0, blocking collectives: 27.2 us -> none  [exchange(): return lax.all_to_all(array, SEQ, split_axis=0, concat_axis=0, tiled=True)]
    unnamed x51 -> x9, local copies, waits for them, and re-layouts: 21.1 us -> 1.59 us
    all_to_all x3 -> x4, waiting for transfers between devices: 46 us -> 61.9 us  [exchange(): return lax.all_to_all(array, SEQ, split_axis=0, concat_axis=0, tiled=True)]
    all_to_all x3 -> x4, starting transfers between devices: 20.9 us -> 31.6 us  [exchange(): return lax.all_to_all(array, SEQ, split_axis=0, concat_axis=0, tiled=True)]
    pallas_call x1, Pallas kernels: 5.95 us -> 8.9 us  [body(): pl.pallas_call(outer_kernel, grid_spec=pltpu.PrefetchScalarGridSpec(num_s...]
    pallas_call x1, Pallas kernels: 6.81 us -> 9.55 us  [body(): pl.pallas_call(local_kernel, grid=(STEPS,), in_specs=[rows_of(BLOCK, 1024...]
    pallas_call x1, Pallas kernels: 7.27 us -> 9.98 us  [body(): pl.pallas_call(front_kernel, grid=(STEPS,), in_specs=[rows_of(BLOCK, 1024...]
    pallas_call x1, Pallas kernels: 5.52 us -> 8.21 us  [body(): pl.pallas_call(lookup_kernel, grid=(5,), in_specs=[rows_of(TOTAL // 5, 1)...]
  transfers between devices with their start and end apart: 6 -> 7, of which waited for: 3 -> 4; matrix products, arithmetic and copies ran while one was open for 1% -> 1% of each run, Pallas kernels for 13% -> 20%
where the time goes in v2:
time: 151 us; the launch traced here: 150 us
  waiting for transfers between devices  61.9 us (41%)
  Pallas kernels  48.2 us (32%)
  starting transfers between devices  36.4 us (24%)
  local copies, waits for them, and re-layouts  2.8 us (2%)
    all_to_all x4, waiting for transfers between devices, exchange(): return lax.all_to_all(array, SEQ, split_axis=0, concat_axis=0, tiled=True)  61.9 us
    all_to_all x4, starting transfers between devices, exchange(): return lax.all_to_all(array, SEQ, split_axis=0, concat_axis=0, tiled=True)  31.6 us
    pallas_call x1, Pallas kernels, body(): pl.pallas_call(front_kernel, grid=(STEPS,), in_specs=[rows_of(BLOCK, 1024...  9.98 us
    pallas_call x1, Pallas kernels, body(): pl.pallas_call(local_kernel, grid=(STEPS,), in_specs=[rows_of(BLOCK, 1024...  9.55 us
    pallas_call x1, Pallas kernels, body(): pl.pallas_call(outer_kernel, grid_spec=pltpu.PrefetchScalarGridSpec(num_s...  8.9 us
    pallas_call x1, Pallas kernels, body(): pl.pallas_call(lookup_kernel, grid=(5,), in_specs=[rows_of(TOTAL // 5, 1)...  8.21 us
    pallas_call x1, Pallas kernels, body(): pl.pallas_call(table_kernel, grid=(6,), in_specs=[whole(1, TOTAL), whole(...  6.07 us
    ppermute x3, starting transfers between devices, body(): lax.ppermute(shares[d], 'book', [(i, (i + d) % 4) for i in range(4)])  4.75 us
  transfers between devices with their start and end apart: 7, of which 4 were waited for; matrix products, arithmetic and copies ran while one was open for 1% of the time, Pallas kernels for 20%

profile of v2, /device:TPU:1, one launch (start us, length us, event | category | flops | bytes accessed | tf_op | source)
XLA Modules:
  0.0 150.1 jit_solution(6580117787862341963)
XLA Ops:
  0.6 1.6 %copy.15.dt_w_ref = bf16[1024,4]{1,0:T(8,128)(2,1)} copy(bf16[1024,4]{0,1:T(4,128)(2,1)} %param.17) | data formatting | bytes 16384 | tf_op args[5]
  2.2 10.0 %front.1 = (f32[64,1,1280]{2,1,0:T(1,128)}, s32[3,256]{1,0:T(4,128)}, bf16[1024,1024]{1,0:T(8,128)(2,1)}, bf16[1024,512]{1,0:T(8,128)(2,1)}, bf16[1024,256]{1,0:T(8,128)(2,1)}, /*index=5*/f32[1024,4]{1,0:T(8,128)}) custom-call(bf16[1024,1024]{1,0:T(8,128)(2,1)} %frames_ref.3, f32[1,1024]{1,0:T(1,128)} %bitcast.19, bf16[1024,512]{1,0:T(8,128)(2,1)} %x_w_ref.1, ...), custom_call_target="tpu_custom_call" | custom-call | tf_op jit(solution)/shard_map/front/pallas_call | solution.py:308
  12.2 13.2 %all-to-all-start = ((f32[64,1,1280]{2,1,0:T(1,128)}), f32[64,1,1280]{2,1,0:T(1,128)S(1)}, u32[]{:S(2)}, u32[]{:S(2)}) async-start(f32[64,1,1280]{2,1,0:T(1,128)} %get-tuple-element.22), calls=%async_computation | async-start | bytes 655360 | tf_op jit(solution)/shard_map/all_to_all | solution.py:300
  25.4 9.6 %local.1 = (f32[1024,512]{1,0:T(8,128)}, f32[1024,512]{1,0:T(8,128)}, f32[1024,4]{1,0:T(8,128)}, f32[4,256,256]{2,1,0:T(8,128)}) custom-call(bf16[1024,1024]{1,0:T(8,128)(2,1)} %frames_ref.3, bf16[1024,1024]{1,0:T(8,128)(2,1)} %get-tuple-element.23.normed_ref, bf16[1024,512]{1,0:T(8,128)(2,1)} %get-tuple-element.24.inflow_ref, ...), custom_call_target="tpu_custom_call" | custom-call | flops 4000000000 | bytes 12582912 | tf_op jit(solution)/shard_map/local/pallas_call | solution.py:332
  34.9 4.6 %all-to-all-done.arrived_ref = f32[64,1,1280]{2,1,0:T(1,128)S(1)} async-done(((f32[64,1,1280]{2,1,0:T(1,128)}), f32[64,1,1280]{2,1,0:T(1,128)S(1)}, u32[]{:S(2)}, u32[]{:S(2)}) %all-to-all-start) | async-done | bytes 327712 | tf_op jit(solution)/shard_map/all_to_all | solution.py:300
  39.5 0.9 scan.1
  40.4 0.1 fusion
  40.5 5.7 %all-to-all-start.1 = ((f32[64,8,128]{2,1,0:T(8,128)}), f32[64,8,128]{2,1,0:T(8,128)S(1)}, u32[]{:S(2)}, u32[]{:S(2)}) async-start(f32[64,8,128]{2,1,0:T(8,128)} %scan.1), calls=%async_computation.1 | async-start | bytes 524288 | tf_op jit(solution)/shard_map/all_to_all | solution.py:300
  46.2 1.1 convert_element_type.26.codes_ref
  47.3 8.2 %lookup.1 = f32[2560,128]{1,0:T(8,128)} custom-call(s32[1280,1]{1,0:T(8,128)} %convert_element_type.26.codes_ref, f32[3072,256]{1,0:T(8,128)} %bitcast.22), custom_call_target="tpu_custom_call" | custom-call | flops 6000000000 | bytes 5242880 | tf_op jit(solution)/shard_map/lookup/pallas_call | solution.py:363
  55.6 3.8 %all-to-all-done.1 = f32[64,8,128]{2,1,0:T(8,128)S(1)} async-done(((f32[64,8,128]{2,1,0:T(8,128)}), f32[64,8,128]{2,1,0:T(8,128)S(1)}, u32[]{:S(2)}, u32[]{:S(2)}) %all-to-all-start.1) | async-done | bytes 262176 | tf_op jit(solution)/shard_map/all_to_all | solution.py:300
  59.4 6.5 %all-to-all-start.2 = ((f32[64,40,128]{2,1,0:T(8,128)}), f32[64,40,128]{2,1,0:T(8,128)S(1)}, u32[]{:S(2)}, u32[]{:S(2)}) async-start(f32[64,40,128]{2,1,0:T(8,128)} %bitcast.16), calls=%async_computation.2 | async-start | bytes 2621440 | tf_op jit(solution)/shard_map/all_to_all | solution.py:300
  65.9 8.9 %outer.1 = (f32[256,256]{1,0:T(8,128)}, f32[256,256]{1,0:T(8,128)}, f32[256,256]{1,0:T(8,128)}, f32[256,256]{1,0:T(8,128)}) custom-call(s32[1]{0:T(128)} %bitcast.book_ref, f32[1024,512]{1,0:T(8,128)} %get-tuple-element.28.inner_ref, f32[1024,512]{1,0:T(8,128)} %get-tuple-element.29.gate_ref, f32[1024,4]{1,0:T(8,128)} %get-tuple-element.30.reach_ref, ...), custom_call_target="tpu_custom_call" | custom-call | flops 2000000000 | bytes 8388608 | tf_op jit(solution)/shard_map/outer/pallas_call | solution.py:375
  74.8 1.2 collective-permute-start
  76.0 2.5 %collective-permute-start.1 = (f32[256,256]{1,0:T(8,128)}, f32[256,256]{1,0:T(8,128)S(1)}, u32[]{:S(2)}, u32[]{:S(2)}) collective-permute-start(f32[256,256]{1,0:T(8,128)} %get-tuple-element.34), channel_id=1, source_target_pairs={{0,2},{1,3},{2,0},{3,1},{4,6},{5,7},{6,4},{7,5},{8,10},{9,11},{10,... | collective-permute-start | bytes 786440 | tf_op jit(solution)/shard_map/ppermute | solution.py:394
  78.4 1.1 collective-permute-start.2
  79.5 19.9 %all-to-all-done.2 = f32[64,40,128]{2,1,0:T(8,128)S(1)} async-done(((f32[64,40,128]{2,1,0:T(8,128)}), f32[64,40,128]{2,1,0:T(8,128)S(1)}, u32[]{:S(2)}, u32[]{:S(2)}) %all-to-all-start.2) | async-done | bytes 1310752 | tf_op jit(solution)/shard_map/all_to_all | solution.py:300
  99.5 2.9 %taken.1 = (f32[1280,256]{1,0:T(8,128)S(1)}, f32[256,256]{1,0:T(8,128)S(1)}) custom-call(f32[2560,128]{1,0:T(8,128)S(1)} %bitcast.14, s32[3,256]{1,0:T(4,128)S(1)} %copy-done.2), custom_call_target="tpu_custom_call" | custom-call | flops 3000000000 | bytes 3145728 | tf_op jit(solution)/shard_map/taken/pallas_call | solution.py:396
  102.4 0.0 collective-permute-done.from_1
  102.4 1.7 %residual.1 = (f32[256,256]{1,0:T(8,128)}, f32[2560,128]{1,0:T(8,128)}) custom-call(s32[1]{0:T(128)} %bitcast.book_ref, f32[256,256]{1,0:T(8,128)S(1)} %copy-done.1, f32[256,256]{1,0:T(8,128)S(1)} %collective-permute-done.from_1, f32[256,256]{1,0:T(8,128)S(1)} %collective-permute-done.1.from_2, f32[256,256]{1,0:T(8,128)S(1)} %collective-permute-done.2.from_3, ...), custom_call_target="tpu_custom_call" | custom-call | tf_op jit(solution)/shard_map/residual/pallas_call | solution.py:403
  104.1 6.3 %all-to-all-start.3 = ((f32[64,40,128]{2,1,0:T(8,128)}), f32[64,40,128]{2,1,0:T(8,128)S(1)}, u32[]{:S(2)}, u32[]{:S(2)}) async-start(f32[64,40,128]{2,1,0:T(8,128)} %bitcast.9), calls=%async_computation.3 | async-start | bytes 2621440 | tf_op jit(solution)/shard_map/all_to_all | solution.py:300
  110.5 0.1 convert_element_type.25.codes_ref
  110.6 33.5 %all-to-all-done.3 = f32[64,40,128]{2,1,0:T(8,128)S(1)} async-done(((f32[64,40,128]{2,1,0:T(8,128)}), f32[64,40,128]{2,1,0:T(8,128)S(1)}, u32[]{:S(2)}, u32[]{:S(2)}) %all-to-all-start.3) | async-done | bytes 1310752 | tf_op jit(solution)/shard_map/all_to_all | solution.py:300
  144.1 6.1 %table.1 = f32[3072,256]{1,0:T(8,128)} custom-call(s32[1,1280]{1,0:T(1,128)S(1)} %convert_element_type.25.codes_ref, f32[2560,128]{1,0:T(8,128)S(1)} %bitcast.13), custom_call_target="tpu_custom_call" | custom-call | tf_op jit(solution)/shard_map/table/pallas_call | solution.py:420
  (11 shorter events, 0.0 us)
Async XLA Ops:
  12.2 27.3 %all-to-all-start = ((f32[64,1,1280]{2,1,0:T(1,128)}), f32[64,1,1280]{2,1,0:T(1,128)S(1)}, u32[]{:S(2)}, u32[]{:S(2)}) async-start(f32[64,1,1280]{2,1,0:T(1,128)} %get-tuple-element.22), calls=%async_computation | async-start | bytes 655360 | tf_op jit(solution)/shard_map/all_to_all | solution.py:300
  40.5 18.9 %all-to-all-start.1 = ((f32[64,8,128]{2,1,0:T(8,128)}), f32[64,8,128]{2,1,0:T(8,128)S(1)}, u32[]{:S(2)}, u32[]{:S(2)}) async-start(f32[64,8,128]{2,1,0:T(8,128)} %scan.1), calls=%async_computation.1 | async-start | bytes 524288 | tf_op jit(solution)/shard_map/all_to_all | solution.py:300
  59.4 6.5 %copy-start.3 = (f32[64,8,128]{2,1,0:T(8,128)}, f32[64,8,128]{2,1,0:T(8,128)S(1)}, u32[]{:S(2)}) copy-start(f32[64,8,128]{2,1,0:T(8,128)S(1)} %all-to-all-done.1) | copy-start | bytes 786436
  59.4 40.1 %all-to-all-start.2 = ((f32[64,40,128]{2,1,0:T(8,128)}), f32[64,40,128]{2,1,0:T(8,128)S(1)}, u32[]{:S(2)}, u32[]{:S(2)}) async-start(f32[64,40,128]{2,1,0:T(8,128)} %bitcast.16), calls=%async_computation.2 | async-start | bytes 2621440 | tf_op jit(solution)/shard_map/all_to_all | solution.py:300
  65.9 33.6 %copy-start.2 = (s32[3,256]{1,0:T(4,128)S(1)}, s32[3,256]{1,0:T(4,128)}, u32[]{:S(2)}) copy-start(s32[3,256]{1,0:T(4,128)} %get-tuple-element.37.slots_ref) | copy-start | bytes 9220
  74.8 27.6 %collective-permute-start = (f32[256,256]{1,0:T(8,128)}, f32[256,256]{1,0:T(8,128)S(1)}, u32[]{:S(2)}, u32[]{:S(2)}) collective-permute-start(f32[256,256]{1,0:T(8,128)} %get-tuple-element.33), channel_id=1, source_target_pairs={{0,1},{1,2},{2,3},{3,0},{4,5},{5,6},{6,7},{7,4},{8,9},{9,10},{10,1... | collective-permute-start | bytes 786440 | tf_op jit(solution)/shard_map/ppermute | solution.py:394
  76.0 26.4 %collective-permute-start.1 = (f32[256,256]{1,0:T(8,128)}, f32[256,256]{1,0:T(8,128)S(1)}, u32[]{:S(2)}, u32[]{:S(2)}) collective-permute-start(f32[256,256]{1,0:T(8,128)} %get-tuple-element.34), channel_id=1, source_target_pairs={{0,2},{1,3},{2,0},{3,1},{4,6},{5,7},{6,4},{7,5},{8,10},{9,11},{10,... | collective-permute-start | bytes 786440 | tf_op jit(solution)/shard_map/ppermute | solution.py:394
  78.4 24.0 %collective-permute-start.2 = (f32[256,256]{1,0:T(8,128)}, f32[256,256]{1,0:T(8,128)S(1)}, u32[]{:S(2)}, u32[]{:S(2)}) collective-permute-start(f32[256,256]{1,0:T(8,128)} %get-tuple-element.35), channel_id=1, source_target_pairs={{0,3},{1,0},{2,1},{3,2},{4,7},{5,4},{6,5},{7,6},{8,11},{9,8},{10,9... | collective-permute-start | bytes 786440 | tf_op jit(solution)/shard_map/ppermute | solution.py:394
  99.5 2.9 %copy-start = (f32[4,256,256]{2,1,0:T(8,128)S(1)}, f32[4,256,256]{2,1,0:T(8,128)}, u32[]{:S(2)}) copy-start(f32[4,256,256]{2,1,0:T(8,128)} %get-tuple-element.36.means_ref) | copy-start | bytes 3145732
  99.5 2.9 %copy-start.1 = (f32[256,256]{1,0:T(8,128)S(1)}, f32[256,256]{1,0:T(8,128)}, u32[]{:S(2)}) copy-start(f32[256,256]{1,0:T(8,128)} %get-tuple-element.32.own_ref) | copy-start | bytes 786436
  104.1 39.9 %all-to-all-start.3 = ((f32[64,40,128]{2,1,0:T(8,128)}), f32[64,40,128]{2,1,0:T(8,128)S(1)}, u32[]{:S(2)}, u32[]{:S(2)}) async-start(f32[64,40,128]{2,1,0:T(8,128)} %bitcast.9), calls=%async_computation.3 | async-start | bytes 2621440 | tf_op jit(solution)/shard_map/all_to_all | solution.py:300

commit v3 on v2

--- a/solution.py
+++ b/solution.py
@@ -32,8 +32,11 @@
     return jnp.dot(a, b, preferred_element_type=f32)
 
 
-def dot_exact(a, b):
-    return jnp.dot(a, b, preferred_element_type=f32, precision=HIGHEST)
+def three_parts(values):
+    high = values.astype(bf16)
+    rest = values - high.astype(f32)
+    middle = rest.astype(bf16)
+    return high, middle, (rest - middle.astype(f32)).astype(bf16)
 
 
 def iota(shape, dim):
@@ -62,8 +65,9 @@
     )
 
 
-def causal_f32():
-    return (iota((BLOCK, BLOCK), 0) >= iota((BLOCK, BLOCK), 1)).astype(f32)
+def running_sum(causal, values):
+    ones = causal.astype(bf16)
+    return sum(dot(ones, part) for part in three_parts(values))
 
 
 def state_step(state, decayed, cum, b_act):
@@ -77,9 +81,14 @@
     owner = ids // CODES
     wanted = level * CODES + ids % CODES + 1
     member = (iota((OWNERS, entries), 0) == owner).astype(f32)
-    before = (iota((entries, entries), 0) < iota((entries, entries), 1)).astype(bf16)
-    rank = jnp.sum(member * dot(member.astype(bf16), before), axis=0, keepdims=True)
-    rank = rank.astype(jnp.int32)
+    before = (iota((QROWS, QROWS), 0) < iota((QROWS, QROWS), 1)).astype(bf16)
+    seen = jnp.zeros((OWNERS, 1), f32)
+    ranks = []
+    for k in range(LEVELS):
+        part = member[:, k * QROWS : (k + 1) * QROWS]
+        ranks.append(jnp.sum(part * (dot(part.astype(bf16), before) + seen), axis=0, keepdims=True))
+        seen = seen + jnp.sum(part, axis=1, keepdims=True)
+    rank = jnp.concatenate(ranks, axis=1).astype(jnp.int32)
     slot = owner * SLOTS + rank
     for k in range(LEVELS):
         slots_ref[k : k + 1, :] = slot[:, k * QROWS : (k + 1) * QROWS]
@@ -112,11 +121,12 @@
     normed_ref[...] = normed
     bc_act = silu(dot(normed, bc_w_ref[...]).astype(bf16).astype(f32)).astype(bf16)
     bc_ref[...] = bc_act
-    raw = dot(normed, dt_w_ref[...]) + bias_ref[...]
+    raw = lax.dot_general(normed, dt_w_ref[...], NT, preferred_element_type=f32) + bias_ref[...]
     dt = jnp.maximum(raw, 0.0) + jnp.log1p(jnp.exp(-jnp.abs(raw)))
     log = -dt * rate_ref[...]
     log_ref[...] = log
-    cum = dot_exact(causal_f32(), log)
+    causal = iota((BLOCK, BLOCK), 0) >= iota((BLOCK, BLOCK), 1)
+    cum = running_sum(causal, log)
     x_act = silu(dot(normed, x_w_ref[...]).astype(bf16).astype(f32))
     inflow = x_act * per_head(dt)
     inflow_ref[...] = inflow.astype(bf16)
@@ -165,11 +175,8 @@
         means_ref[g] = means[:, g * WIDTH : (g + 1) * WIDTH]
     causal = iota((BLOCK, BLOCK), 0) >= iota((BLOCK, BLOCK), 1)
     log = log_ref[...]
-    cum = dot_exact(causal.astype(f32), log)
-    cum_rows = lax.dot_general(
-        jnp.concatenate([log, jnp.zeros((BLOCK, 128 - HEADS), f32)], axis=1).T,
-        causal.astype(f32), NT, preferred_element_type=f32, precision=HIGHEST,
-    )
+    cum = running_sum(causal, log)
+    cum_rows = jnp.concatenate([cum, jnp.zeros((BLOCK, 128 - HEADS), f32)], axis=1).T
     b_act, c_act = bc_ref[:, :DIM], bc_ref[:, DIM:]
     inflow = inflow_ref[...]
     scores = jnp.where(causal, lax.dot_general(c_act, b_act, NT, preferred_element_type=f32), 0.0)
@@ -215,16 +222,32 @@
             out[...] = product[:QROWS] + product[QROWS:]
 
 
-def lookup_kernel(codes_ref, table_ref, found_ref, parts_ref):
-    @pl.when(pl.program_id(0) == 0)
-    def _():
-        parts_ref[...] = two_parts(table_ref[...])
-
-    rows = codes_ref.shape[0]
-    chosen = (codes_ref[...] == iota((rows, LEVELS * CODES), 1) + 1).astype(bf16)
-    found = folded(dot(chosen, parts_ref[...]))
-    found_ref[pl.ds(0, rows, 2), :] = found[:, :128]
-    found_ref[pl.ds(1, rows, 2), :] = found[:, 128:]
+def lookup_kernel(arrived_ref, table_ref, found_ref, asked_ref, columns_ref, total_ref):
+    level = pl.program_id(0)
+
+    @pl.when(level == 0)
+    def _():
+        for k in range(OWNERS):
+            asked_ref[k : k + 1, :] = arrived_ref[k, :, 1152:1280]
+        turned = asked_ref[...].T
+        for k in range(OWNERS):
+            columns_ref[k * SLOTS : (k + 1) * SLOTS, :] = jnp.broadcast_to(
+                turned[:SLOTS, k : k + 1], (SLOTS, 128)
+            )
+        total_ref[...] = jnp.zeros_like(total_ref)
+
+    first = level * CODES + 1
+    place = iota((TOTAL, 128), 1) + first
+    asked = columns_ref[...].astype(jnp.int32)
+    chosen = jnp.concatenate(
+        [(asked == place + g * 128).astype(bf16) for g in range(CODES // 128)], axis=1
+    )
+    total_ref[...] += dot(chosen, table_ref[0].astype(bf16))
+
+    @pl.when(level == LEVELS - 1)
+    def _():
+        found_ref[pl.ds(0, TOTAL, 2), :] = total_ref[:, :128]
+        found_ref[pl.ds(1, TOTAL, 2), :] = total_ref[:, 128:]
 
 
 def joined_rows(ref):
@@ -234,7 +257,7 @@
 
 def taken_kernel(found_ref, slots_ref, terms_ref, taken_ref):
     found = joined_rows(found_ref)
-    parts = two_parts(found)
+    rounded = found.astype(bf16)
     slots = jnp.concatenate(
         [slots_ref[...].astype(f32), jnp.zeros((8 - LEVELS, QROWS), f32)], axis=0
     )
@@ -248,7 +271,7 @@
             spread = (iota((TOTAL, QROWS), 0) == slots_ref[k : k + 1, :]).astype(bf16)
             terms = terms + folded(dot(spread, two_parts(taken)))
         picks = (columns[:, k : k + 1] == iota((QROWS, TOTAL), 1)).astype(bf16)
-        taken = taken + folded(dot(picks, parts))
+        taken = taken + dot(picks, rounded)
     terms_ref[...] = terms
     taken_ref[...] = taken
 
@@ -268,16 +291,16 @@
     grads_ref[pl.ds(1, TOTAL, 2), :] = grads[:, 128:]
 
 
-def table_kernel(codes_ref, grads_ref, table_ref, parts_ref):
+def table_kernel(codes_ref, grads_ref, table_ref, rounded_ref):
     step = pl.program_id(0)
 
     @pl.when(step == 0)
     def _():
-        parts_ref[...] = two_parts(joined_rows(grads_ref))
+        rounded_ref[...] = joined_rows(grads_ref).astype(bf16)
 
     rows = table_ref.shape[0]
     chosen = (codes_ref[...] == iota((rows, TOTAL), 0) + (step * rows + 1)).astype(bf16)
-    table_ref[...] = folded(dot(chosen, parts_ref[...]))
+    table_ref[...] = dot(chosen, rounded_ref[...])
 
 
 def shape(*dims, dtype=f32):
@@ -310,7 +333,7 @@
         grid=(STEPS,),
         in_specs=[
             rows_of(BLOCK, 1024), whole(1, 1024), whole(1024, INNER), whole(1024, 256),
-            whole(1024, HEADS), whole(1, HEADS), whole(1, HEADS), whole(LEVELS, QROWS),
+            whole(HEADS, 1024), whole(1, HEADS), whole(1, HEADS), whole(LEVELS, QROWS),
         ],
         out_specs=[
             whole(OWNERS, 1, PAYLOAD), whole(LEVELS, QROWS), rows_of(BLOCK, 1024),
@@ -325,7 +348,7 @@
         compiler_params=settings(62),
         name="front",
     )(
-        frames, norm_gain.reshape(1, -1), x_weight, bc_weight, dt_weight,
+        frames, norm_gain.reshape(1, -1), x_weight, bc_weight, dt_weight.T,
         dt_bias.reshape(1, -1), decay_rate.reshape(1, -1), code_ids,
     )
     arrived = exchange(payload)
@@ -350,6 +373,23 @@
         name="local",
     )(frames, normed, inflow, bc_act, log, z_weight)
     arrived, inner = lax.optimization_barrier((arrived, inner))
+    found = pl.pallas_call(
+        lookup_kernel,
+        grid=(LEVELS,),
+        in_specs=[
+            whole(OWNERS, 1, PAYLOAD), pl.BlockSpec((1, CODES, WIDTH), lambda i: (i, 0, 0)),
+        ],
+        out_specs=whole(2 * TOTAL, 128),
+        out_shape=shape(2 * TOTAL, 128),
+        scratch_shapes=[
+            pltpu.VMEM((OWNERS, 128), f32), pltpu.VMEM((TOTAL, 128), f32),
+            pltpu.VMEM((TOTAL, WIDTH), f32),
+        ],
+        compiler_params=settings(56),
+        cost_estimate=pl.CostEstimate(flops=4 * 10**9, bytes_accessed=5 * 2**20, transcendentals=0),
+        name="lookup",
+    )(arrived, codebook)
+    fetched = exchange(found.reshape(OWNERS, 2 * SLOTS, 128)).reshape(2 * TOTAL, 128)
     before = pl.pallas_call(
         scan_kernel,
         out_shape=shape(OWNERS, 8, 128),
@@ -357,21 +397,6 @@
         name="scan",
     )(arrived)
     incoming = exchange(before).reshape(INNER, DIM)
-    asked = arrived[:, 0, 1152 : 1152 + SLOTS].astype(jnp.int32)
-    codes_column = asked.reshape(TOTAL, 1)
-    codes_row = asked.reshape(1, TOTAL)
-    found = pl.pallas_call(
-        lookup_kernel,
-        grid=(5,),
-        in_specs=[rows_of(TOTAL // 5, 1), whole(LEVELS * CODES, WIDTH)],
-        out_specs=rows_of(2 * TOTAL // 5, 128),
-        out_shape=shape(2 * TOTAL, 128),
-        scratch_shapes=[pltpu.VMEM((LEVELS * CODES, 2 * WIDTH), bf16)],
-        compiler_params=settings(62),
-        cost_estimate=pl.CostEstimate(flops=6 * 10**9, bytes_accessed=5 * 2**20, transcendentals=0),
-        name="lookup",
-    )(codes_column, codebook.reshape(LEVELS * CODES, WIDTH))
-    fetched = exchange(found.reshape(OWNERS, 2 * SLOTS, 128)).reshape(2 * TOTAL, 128)
     shares = pl.pallas_call(
         outer_kernel,
         grid_spec=pltpu.PrefetchScalarGridSpec(
@@ -417,16 +442,18 @@
         name="residual",
     )(book, shares[0], *moved, means, taken, terms, slots)
     returned = exchange(grads.reshape(OWNERS, 2 * SLOTS, 128)).reshape(2 * TOTAL, 128)
+    arrived, grads = lax.optimization_barrier((arrived, grads))
+    codes = arrived[:, 0, 1152 : 1152 + SLOTS].astype(jnp.int32).reshape(1, TOTAL)
     table = pl.pallas_call(
         table_kernel,
         grid=(6,),
         in_specs=[whole(1, TOTAL), whole(2 * TOTAL, 128)],
         out_specs=rows_of(LEVELS * CODES // 6, WIDTH),
         out_shape=shape(LEVELS * CODES, WIDTH),
-        scratch_shapes=[pltpu.VMEM((TOTAL, 2 * WIDTH), bf16)],
+        scratch_shapes=[pltpu.VMEM((TOTAL, WIDTH), bf16)],
         compiler_params=settings(40),
         name="table",
-    )(codes_row, returned)
+    )(codes, returned)
     return residual, table.reshape(LEVELS, CODES, WIDTH)
 
 

time: 151 us -> 144 us (0.954)
  Pallas kernels: 48.2 us -> 42.1 us
  waiting for transfers between devices: 61.9 us -> 64.8 us
  local copies, waits for them, and re-layouts: 2.8 us -> 0.13 us
  starting transfers between devices: 36.4 us -> 34.3 us
    all_to_all x4, waiting for transfers between devices: 61.9 us -> 64.8 us  [exchange(): return lax.all_to_all(array, SEQ, split_axis=0, concat_axis=0, tiled=True)]
    pallas_call x1, Pallas kernels: 8.21 us -> 5.84 us  [body(): pl.pallas_call(lookup_kernel, grid=(LEVELS,), in_specs=[whole(OWNERS, 1,...]
    all_to_all x4, starting transfers between devices: 31.6 us -> 29.5 us  [exchange(): return lax.all_to_all(array, SEQ, split_axis=0, concat_axis=0, tiled=True)]
    unnamed x9 -> x10, local copies, waits for them, and re-layouts: 1.59 us -> 0.02 us
    pallas_call x1, Pallas kernels: 6.07 us -> 4.52 us  [body(): pl.pallas_call(table_kernel, grid=(6,), in_specs=[whole(1, TOTAL), whole(...]
  transfers between devices with their start and end apart: 7 -> 7, of which waited for: 4 -> 4; matrix products, arithmetic and copies ran while one was open for 1% -> 1% of each run, Pallas kernels for 20% -> 18%
where the time goes in v3:
time: 144 us; the launch traced here: 143 us
  waiting for transfers between devices  64.8 us (45%)
  Pallas kernels  42.1 us (29%)
  starting transfers between devices  34.3 us (24%)
    all_to_all x4, waiting for transfers between devices, exchange(): return lax.all_to_all(array, SEQ, split_axis=0, concat_axis=0, tiled=True)  64.8 us
    all_to_all x4, starting transfers between devices, exchange(): return lax.all_to_all(array, SEQ, split_axis=0, concat_axis=0, tiled=True)  29.5 us
    pallas_call x1, Pallas kernels, body(): pl.pallas_call(local_kernel, grid=(STEPS,), in_specs=[rows_of(BLOCK, 1024...  9.21 us
    pallas_call x1, Pallas kernels, body(): pl.pallas_call(outer_kernel, grid_spec=pltpu.PrefetchScalarGridSpec(num_s...  8.86 us
    pallas_call x1, Pallas kernels, body(): pl.pallas_call(front_kernel, grid=(STEPS,), in_specs=[rows_of(BLOCK, 1024...  8.85 us
    pallas_call x1, Pallas kernels, body(): pl.pallas_call(lookup_kernel, grid=(LEVELS,), in_specs=[whole(OWNERS, 1,...  5.84 us
    ppermute x3, starting transfers between devices, body(): lax.ppermute(shares[d], 'book', [(i, (i + d) % 4) for i in range(4)])  4.79 us
    pallas_call x1, Pallas kernels, body(): pl.pallas_call(table_kernel, grid=(6,), in_specs=[whole(1, TOTAL), whole(...  4.52 us
  transfers between devices with their start and end apart: 7, of which 4 were waited for; matrix products, arithmetic and copies ran while one was open for 1% of the time, Pallas kernels for 18%

profile of v3, /device:TPU:1, one launch (start us, length us, event | category | flops | bytes accessed | tf_op | source)
XLA Modules:
  0.0 143.0 jit_solution(3099276042661908973)
XLA Ops:
  0.6 8.8 %front.1 = (f32[64,1,1280]{2,1,0:T(1,128)}, s32[3,256]{1,0:T(4,128)}, bf16[1024,1024]{1,0:T(8,128)(2,1)}, bf16[1024,512]{1,0:T(8,128)(2,1)}, bf16[1024,256]{1,0:T(8,128)(2,1)}, /*index=5*/f32[1024,4]{1,0:T(8,128)}) custom-call(bf16[1024,1024]{1,0:T(8,128)(2,1)} %frames_ref.3, f32[1,1024]{1,0:T(1,128)} %bitcast.18, bf16[1024,512]{1,0:T(8,128)(2,1)} %x_w_ref.1, ...), custom_call_target="tpu_custom_call" | custom-call | tf_op jit(solution)/shard_map/front/pallas_call | solution.py:331
  9.5 13.2 %all-to-all-start = ((f32[64,1,1280]{2,1,0:T(1,128)}), f32[64,1,1280]{2,1,0:T(1,128)S(1)}, u32[]{:S(2)}, u32[]{:S(2)}) async-start(f32[64,1,1280]{2,1,0:T(1,128)} %get-tuple-element.23), calls=%async_computation | async-start | bytes 655360 | tf_op jit(solution)/shard_map/all_to_all | solution.py:323
  22.6 9.2 %local.1 = (f32[1024,512]{1,0:T(8,128)}, f32[1024,512]{1,0:T(8,128)}, f32[1024,4]{1,0:T(8,128)}, f32[4,256,256]{2,1,0:T(8,128)}) custom-call(bf16[1024,1024]{1,0:T(8,128)(2,1)} %frames_ref.3, bf16[1024,1024]{1,0:T(8,128)(2,1)} %get-tuple-element.24.normed_ref, bf16[1024,512]{1,0:T(8,128)(2,1)} %get-tuple-element.25.inflow_ref, ...), custom_call_target="tpu_custom_call" | custom-call | flops 4000000000 | bytes 12582912 | tf_op jit(solution)/shard_map/local/pallas_call | solution.py:355
  31.9 5.0 %all-to-all-done.arrived_ref = f32[64,1,1280]{2,1,0:T(1,128)S(1)} async-done(((f32[64,1,1280]{2,1,0:T(1,128)}), f32[64,1,1280]{2,1,0:T(1,128)S(1)}, u32[]{:S(2)}, u32[]{:S(2)}) %all-to-all-start) | async-done | bytes 327712 | tf_op jit(solution)/shard_map/all_to_all | solution.py:323
  36.8 0.9 scan.1
  37.7 5.3 %all-to-all-start.1 = ((f32[64,8,128]{2,1,0:T(8,128)}), f32[64,8,128]{2,1,0:T(8,128)S(1)}, u32[]{:S(2)}, u32[]{:S(2)}) async-start(f32[64,8,128]{2,1,0:T(8,128)} %scan.1), calls=%async_computation.1 | async-start | bytes 524288 | tf_op jit(solution)/shard_map/all_to_all | solution.py:323
  43.1 5.8 %lookup.1 = f32[2560,128]{1,0:T(8,128)} custom-call(f32[64,1,1280]{2,1,0:T(1,128)} %copy-done, f32[3,1024,256]{2,1,0:T(8,128)} %table_ref.1), custom_call_target="tpu_custom_call" | custom-call | flops 4000000000 | bytes 5242880 | tf_op jit(solution)/shard_map/lookup/pallas_call | solution.py:376
  48.9 7.3 %all-to-all-done.1 = f32[64,8,128]{2,1,0:T(8,128)S(1)} async-done(((f32[64,8,128]{2,1,0:T(8,128)}), f32[64,8,128]{2,1,0:T(8,128)S(1)}, u32[]{:S(2)}, u32[]{:S(2)}) %all-to-all-start.1) | async-done | bytes 262176 | tf_op jit(solution)/shard_map/all_to_all | solution.py:323
  56.2 4.7 %all-to-all-start.2 = ((f32[64,40,128]{2,1,0:T(8,128)}), f32[64,40,128]{2,1,0:T(8,128)S(1)}, u32[]{:S(2)}, u32[]{:S(2)}) async-start(f32[64,40,128]{2,1,0:T(8,128)} %bitcast.15), calls=%async_computation.2 | async-start | bytes 2621440 | tf_op jit(solution)/shard_map/all_to_all | solution.py:323
  61.0 8.9 %outer.1 = (f32[256,256]{1,0:T(8,128)}, f32[256,256]{1,0:T(8,128)}, f32[256,256]{1,0:T(8,128)}, f32[256,256]{1,0:T(8,128)}) custom-call(s32[1]{0:T(128)} %bitcast.book_ref, f32[1024,512]{1,0:T(8,128)} %get-tuple-element.29.inner_ref, f32[1024,512]{1,0:T(8,128)} %get-tuple-element.30.gate_ref, f32[1024,4]{1,0:T(8,128)} %get-tuple-element.31.reach_ref, ...), custom_call_target="tpu_custom_call" | custom-call | flops 2000000000 | bytes 8388608 | tf_op jit(solution)/shard_map/outer/pallas_call | solution.py:400
  69.8 1.2 collective-permute-start
  71.0 2.5 %collective-permute-start.1 = (f32[256,256]{1,0:T(8,128)}, f32[256,256]{1,0:T(8,128)S(1)}, u32[]{:S(2)}, u32[]{:S(2)}) collective-permute-start(f32[256,256]{1,0:T(8,128)} %get-tuple-element.35), channel_id=1, source_target_pairs={{0,2},{1,3},{2,0},{3,1},{4,6},{5,7},{6,4},{7,5},{8,10},{9,11},{10,... | collective-permute-start | bytes 786440 | tf_op jit(solution)/shard_map/ppermute | solution.py:419
  73.5 1.1 collective-permute-start.2
  74.6 19.9 %all-to-all-done.2 = f32[64,40,128]{2,1,0:T(8,128)S(1)} async-done(((f32[64,40,128]{2,1,0:T(8,128)}), f32[64,40,128]{2,1,0:T(8,128)S(1)}, u32[]{:S(2)}, u32[]{:S(2)}) %all-to-all-start.2) | async-done | bytes 1310752 | tf_op jit(solution)/shard_map/all_to_all | solution.py:323
  94.6 2.2 %taken.1 = (f32[1280,256]{1,0:T(8,128)S(1)}, f32[256,256]{1,0:T(8,128)S(1)}) custom-call(f32[2560,128]{1,0:T(8,128)S(1)} %bitcast.13, s32[3,256]{1,0:T(4,128)S(1)} %copy-done.3), custom_call_target="tpu_custom_call" | custom-call | flops 3000000000 | bytes 3145728 | tf_op jit(solution)/shard_map/taken/pallas_call | solution.py:421
  96.7 0.0 collective-permute-done.from_1
  96.8 0.0 collective-permute-done.1.from_2
  96.8 0.0 collective-permute-done.2.from_3
  96.8 1.7 %residual.1 = (f32[256,256]{1,0:T(8,128)}, f32[2560,128]{1,0:T(8,128)}) custom-call(s32[1]{0:T(128)} %bitcast.book_ref, f32[256,256]{1,0:T(8,128)S(1)} %copy-done.2, f32[256,256]{1,0:T(8,128)S(1)} %collective-permute-done.from_1, f32[256,256]{1,0:T(8,128)S(1)} %collective-permute-done.1.from_2, f32[256,256]{1,0:T(8,128)S(1)} %collective-permute-done.2.from_3, ...), custom_call_target="tpu_custom_call" | custom-call | tf_op jit(solution)/shard_map/residual/pallas_call | solution.py:428
  98.5 6.3 %all-to-all-start.3 = ((f32[64,40,128]{2,1,0:T(8,128)}), f32[64,40,128]{2,1,0:T(8,128)S(1)}, u32[]{:S(2)}, u32[]{:S(2)}) async-start(f32[64,40,128]{2,1,0:T(8,128)} %bitcast.9), calls=%async_computation.3 | async-start | bytes 2621440 | tf_op jit(solution)/shard_map/all_to_all | solution.py:323
  104.8 0.9 convert_reduce_fusion
  105.7 0.1 convert_element_type.14.codes_ref
  105.8 32.6 %all-to-all-done.3 = f32[64,40,128]{2,1,0:T(8,128)S(1)} async-done(((f32[64,40,128]{2,1,0:T(8,128)}), f32[64,40,128]{2,1,0:T(8,128)S(1)}, u32[]{:S(2)}, u32[]{:S(2)}) %all-to-all-start.3) | async-done | bytes 1310752 | tf_op jit(solution)/shard_map/all_to_all | solution.py:323
  138.4 4.5 %table.1 = f32[3072,256]{1,0:T(8,128)} custom-call(s32[1,1280]{1,0:T(1,128)S(1)} %convert_element_type.14.codes_ref, f32[2560,128]{1,0:T(8,128)S(1)} %bitcast.12), custom_call_target="tpu_custom_call" | custom-call | tf_op jit(solution)/shard_map/table/pallas_call | solution.py:447
  (10 shorter events, 0.0 us)
Async XLA Ops:
  9.5 27.3 %all-to-all-start = ((f32[64,1,1280]{2,1,0:T(1,128)}), f32[64,1,1280]{2,1,0:T(1,128)S(1)}, u32[]{:S(2)}, u32[]{:S(2)}) async-start(f32[64,1,1280]{2,1,0:T(1,128)} %get-tuple-element.23), calls=%async_computation | async-start | bytes 655360 | tf_op jit(solution)/shard_map/all_to_all | solution.py:323
  36.8 6.3 %copy-start = (f32[64,1,1280]{2,1,0:T(1,128)}, f32[64,1,1280]{2,1,0:T(1,128)S(1)}, u32[]{:S(2)}) copy-start(f32[64,1,1280]{2,1,0:T(1,128)S(1)} %all-to-all-done.arrived_ref) | copy-start | bytes 983044
  37.7 18.5 %all-to-all-start.1 = ((f32[64,8,128]{2,1,0:T(8,128)}), f32[64,8,128]{2,1,0:T(8,128)S(1)}, u32[]{:S(2)}, u32[]{:S(2)}) async-start(f32[64,8,128]{2,1,0:T(8,128)} %scan.1), calls=%async_computation.1 | async-start | bytes 524288 | tf_op jit(solution)/shard_map/all_to_all | solution.py:323
  56.2 4.7 %copy-start.4 = (f32[64,8,128]{2,1,0:T(8,128)}, f32[64,8,128]{2,1,0:T(8,128)S(1)}, u32[]{:S(2)}) copy-start(f32[64,8,128]{2,1,0:T(8,128)S(1)} %all-to-all-done.1) | copy-start | bytes 786436
  56.2 38.3 %all-to-all-start.2 = ((f32[64,40,128]{2,1,0:T(8,128)}), f32[64,40,128]{2,1,0:T(8,128)S(1)}, u32[]{:S(2)}, u32[]{:S(2)}) async-start(f32[64,40,128]{2,1,0:T(8,128)} %bitcast.15), calls=%async_computation.2 | async-start | bytes 2621440 | tf_op jit(solution)/shard_map/all_to_all | solution.py:323
  61.0 33.6 %copy-start.3 = (s32[3,256]{1,0:T(4,128)S(1)}, s32[3,256]{1,0:T(4,128)}, u32[]{:S(2)}) copy-start(s32[3,256]{1,0:T(4,128)} %get-tuple-element.38.slots_ref) | copy-start | bytes 9220
  69.8 26.9 %collective-permute-start = (f32[256,256]{1,0:T(8,128)}, f32[256,256]{1,0:T(8,128)S(1)}, u32[]{:S(2)}, u32[]{:S(2)}) collective-permute-start(f32[256,256]{1,0:T(8,128)} %get-tuple-element.34), channel_id=1, source_target_pairs={{0,1},{1,2},{2,3},{3,0},{4,5},{5,6},{6,7},{7,4},{8,9},{9,10},{10,1... | collective-permute-start | bytes 786440 | tf_op jit(solution)/shard_map/ppermute | solution.py:419
  71.0 25.7 %collective-permute-start.1 = (f32[256,256]{1,0:T(8,128)}, f32[256,256]{1,0:T(8,128)S(1)}, u32[]{:S(2)}, u32[]{:S(2)}) collective-permute-start(f32[256,256]{1,0:T(8,128)} %get-tuple-element.35), channel_id=1, source_target_pairs={{0,2},{1,3},{2,0},{3,1},{4,6},{5,7},{6,4},{7,5},{8,10},{9,11},{10,... | collective-permute-start | bytes 786440 | tf_op jit(solution)/shard_map/ppermute | solution.py:419
  73.5 23.3 %collective-permute-start.2 = (f32[256,256]{1,0:T(8,128)}, f32[256,256]{1,0:T(8,128)S(1)}, u32[]{:S(2)}, u32[]{:S(2)}) collective-permute-start(f32[256,256]{1,0:T(8,128)} %get-tuple-element.36), channel_id=1, source_target_pairs={{0,3},{1,0},{2,1},{3,2},{4,7},{5,4},{6,5},{7,6},{8,11},{9,8},{10,9... | collective-permute-start | bytes 786440 | tf_op jit(solution)/shard_map/ppermute | solution.py:419
  94.6 2.2 %copy-start.1 = (f32[4,256,256]{2,1,0:T(8,128)S(1)}, f32[4,256,256]{2,1,0:T(8,128)}, u32[]{:S(2)}) copy-start(f32[4,256,256]{2,1,0:T(8,128)} %get-tuple-element.37.means_ref) | copy-start | bytes 3145732
  94.6 2.2 %copy-start.2 = (f32[256,256]{1,0:T(8,128)S(1)}, f32[256,256]{1,0:T(8,128)}, u32[]{:S(2)}) copy-start(f32[256,256]{1,0:T(8,128)} %get-tuple-element.33.own_ref) | copy-start | bytes 786436
  98.5 39.9 %all-to-all-start.3 = ((f32[64,40,128]{2,1,0:T(8,128)}), f32[64,40,128]{2,1,0:T(8,128)S(1)}, u32[]{:S(2)}, u32[]{:S(2)}) async-start(f32[64,40,128]{2,1,0:T(8,128)} %bitcast.9), calls=%async_computation.3 | async-start | bytes 2621440 | tf_op jit(solution)/shard_map/all_to_all | solution.py:323

commit v4 on v3

--- a/solution.py
+++ b/solution.py
@@ -1,3 +1,5 @@
+import functools
+
 import jax
 import jax.numpy as jnp
 from jax import lax
@@ -9,8 +11,10 @@
 SEQ = ("seq_0", "seq_1", "seq_2")
 OWNERS = 64
 SLOTS = 20
-TOTAL = OWNERS * SLOTS
+FEW = 16
+LATE = SLOTS - FEW
 LEVELS = 3
+LOW = 4
 CODES = 1024
 FRAMES = 1024
 BLOCK = 256
@@ -74,7 +78,7 @@
     return state * per_head(jnp.exp(cum[BLOCK - 1 :, :])) + dot(b_act.T, decayed)
 
 
-def place_codes(ids_ref, slots_ref):
+def place_codes(ids_ref, slots_ref, few_ref, hot_ref):
     entries = LEVELS * QROWS
     ids = jnp.concatenate([ids_ref[k : k + 1, :] for k in range(LEVELS)], axis=1)
     level = iota((1, entries), 1) // QROWS
@@ -83,15 +87,24 @@
     member = (iota((OWNERS, entries), 0) == owner).astype(f32)
     before = (iota((QROWS, QROWS), 0) < iota((QROWS, QROWS), 1)).astype(bf16)
     seen = jnp.zeros((OWNERS, 1), f32)
+    hot = jnp.zeros((OWNERS, 1), f32)
     ranks = []
     for k in range(LEVELS):
         part = member[:, k * QROWS : (k + 1) * QROWS]
         ranks.append(jnp.sum(part * (dot(part.astype(bf16), before) + seen), axis=0, keepdims=True))
-        seen = seen + jnp.sum(part, axis=1, keepdims=True)
+        count = jnp.sum(part, axis=1, keepdims=True)
+        seen = seen + count
+        hot = jnp.maximum(hot, jnp.where(count > LOW, 1.0, 0.0))
     rank = jnp.concatenate(ranks, axis=1).astype(jnp.int32)
     slot = owner * SLOTS + rank
+    neighbour = owner + 1 - 2 * (owner % 2)
+    few = jnp.where(rank < FEW, owner * FEW + rank, neighbour * FEW + rank - LATE)
     for k in range(LEVELS):
         slots_ref[k : k + 1, :] = slot[:, k * QROWS : (k + 1) * QROWS]
+        few_ref[k : k + 1, :] = few[:, k * QROWS : (k + 1) * QROWS]
+    chip = (iota((OWNERS // 2, OWNERS), 0) == iota((OWNERS // 2, OWNERS), 1) // 2).astype(bf16)
+    on_chip = dot(chip, jnp.broadcast_to(hot, (OWNERS, 128)).astype(bf16))
+    hot_ref[...] = jnp.max(on_chip, axis=0, keepdims=True)
     ranked = (iota((128, entries), 0) == rank).astype(bf16)
     high = (member * (wanted // 64).astype(f32)).astype(bf16)
     low = (member * (wanted % 64).astype(f32)).astype(bf16)
@@ -102,7 +115,7 @@
 
 def front_kernel(
     frames_ref, gain_ref, x_w_ref, bc_w_ref, dt_w_ref, bias_ref, rate_ref, ids_ref,
-    payload_ref, slots_ref, normed_ref, inflow_ref, bc_ref, log_ref,
+    payload_ref, slots_ref, few_ref, hot_ref, normed_ref, inflow_ref, bc_ref, log_ref,
     state_ref, total_ref,
 ):
     step = pl.program_id(0)
@@ -111,7 +124,7 @@
     def _():
         state_ref[...] = jnp.zeros_like(state_ref)
         total_ref[...] = jnp.zeros_like(total_ref)
-        asked = place_codes(ids_ref, slots_ref)
+        asked = place_codes(ids_ref, slots_ref, few_ref, hot_ref)
         for k in range(OWNERS):
             payload_ref[k, :, 1152:1280] = asked[k : k + 1, :]
 
@@ -222,7 +235,14 @@
             out[...] = product[:QROWS] + product[QROWS:]
 
 
-def lookup_kernel(arrived_ref, table_ref, found_ref, asked_ref, columns_ref, total_ref):
+def split_rows(ref, values):
+    rows = values.shape[0]
+    ref[pl.ds(0, rows, 2), :] = values[:, :128]
+    ref[pl.ds(1, rows, 2), :] = values[:, 128:]
+
+
+def lookup_kernel(cuts, arrived_ref, table_ref, *refs):
+    founds, (asked_ref, columns_ref, total_ref) = refs[: len(cuts)], refs[len(cuts) :]
     level = pl.program_id(0)
 
     @pl.when(level == 0)
@@ -230,14 +250,16 @@
         for k in range(OWNERS):
             asked_ref[k : k + 1, :] = arrived_ref[k, :, 1152:1280]
         turned = asked_ref[...].T
-        for k in range(OWNERS):
-            columns_ref[k * SLOTS : (k + 1) * SLOTS, :] = jnp.broadcast_to(
-                turned[:SLOTS, k : k + 1], (SLOTS, 128)
-            )
+        start = 0
+        for low, high in cuts:
+            for k in range(OWNERS):
+                columns_ref[start : start + high - low, :] = jnp.broadcast_to(
+                    turned[low:high, k : k + 1], (high - low, 128)
+                )
+                start += high - low
         total_ref[...] = jnp.zeros_like(total_ref)
 
-    first = level * CODES + 1
-    place = iota((TOTAL, 128), 1) + first
+    place = iota((OWNERS * SLOTS, 128), 1) + (level * CODES + 1)
     asked = columns_ref[...].astype(jnp.int32)
     chosen = jnp.concatenate(
         [(asked == place + g * 128).astype(bf16) for g in range(CODES // 128)], axis=1
@@ -246,8 +268,8 @@
 
     @pl.when(level == LEVELS - 1)
     def _():
-        found_ref[pl.ds(0, TOTAL, 2), :] = total_ref[:, :128]
-        found_ref[pl.ds(1, TOTAL, 2), :] = total_ref[:, 128:]
+        for (low, high), found_ref in zip(cuts, founds):
+            split_rows(found_ref, total_ref[OWNERS * low : OWNERS * high, :])
 
 
 def joined_rows(ref):
@@ -257,6 +279,7 @@
 
 def taken_kernel(found_ref, slots_ref, terms_ref, taken_ref):
     found = joined_rows(found_ref)
+    total = found.shape[0]
     rounded = found.astype(bf16)
     slots = jnp.concatenate(
         [slots_ref[...].astype(f32), jnp.zeros((8 - LEVELS, QROWS), f32)], axis=0
@@ -268,9 +291,9 @@
     terms = found
     for k in range(LEVELS):
         if k:
-            spread = (iota((TOTAL, QROWS), 0) == slots_ref[k : k + 1, :]).astype(bf16)
+            spread = (iota((total, QROWS), 0) == slots_ref[k : k + 1, :]).astype(bf16)
             terms = terms + folded(dot(spread, two_parts(taken)))
-        picks = (columns[:, k : k + 1] == iota((QROWS, TOTAL), 1)).astype(bf16)
+        picks = (columns[:, k : k + 1] == iota((QROWS, total), 1)).astype(bf16)
         taken = taken + dot(picks, rounded)
     terms_ref[...] = terms
     taken_ref[...] = taken
@@ -282,24 +305,29 @@
 ):
     pooled = own_ref[...] + from_1[...] + from_2[...] + from_3[...] + means_ref[0]
     residual_ref[...] = pooled - taken_ref[...]
-    place = iota((TOTAL, QROWS), 0)
+    place = iota((terms_ref.shape[0], QROWS), 0)
     spread = place == slots_ref[0:1, :]
     for k in range(1, LEVELS):
         spread = spread | (place == slots_ref[k : k + 1, :])
     grads = terms_ref[...] - folded(dot(spread.astype(bf16), two_parts(pooled)))
-    grads_ref[pl.ds(0, TOTAL, 2), :] = grads[:, :128]
-    grads_ref[pl.ds(1, TOTAL, 2), :] = grads[:, 128:]
-
-
-def table_kernel(codes_ref, grads_ref, table_ref, rounded_ref):
+    split_rows(grads_ref, grads)
+
+
+def table_kernel(codes_ref, *refs):
+    grads_refs, (table_ref, rounded_ref) = refs[:-2], refs[-2:]
     step = pl.program_id(0)
 
     @pl.when(step == 0)
     def _():
-        rounded_ref[...] = joined_rows(grads_ref).astype(bf16)
+        start = 0
+        for grads_ref in grads_refs:
+            rows = grads_ref.shape[0] // 2
+            rounded_ref[start : start + rows, :] = joined_rows(grads_ref).astype(bf16)
+            start += rows
 
     rows = table_ref.shape[0]
-    chosen = (codes_ref[...] == iota((rows, TOTAL), 0) + (step * rows + 1)).astype(bf16)
+    place = iota((rows, codes_ref.shape[1]), 0) + (step * rows + 1)
+    chosen = (codes_ref[...] == place).astype(bf16)
     table_ref[...] = dot(chosen, rounded_ref[...])
 
 
@@ -323,80 +351,37 @@
     return lax.all_to_all(array, SEQ, split_axis=0, concat_axis=0, tiled=True)
 
 
-def body(
-    frames, norm_gain, x_weight, z_weight, bc_weight, dt_weight, dt_bias, decay_rate,
-    out_gain, out_weight, codebook, code_ids,
-):
-    book = lax.axis_index("book").reshape(1)
-    payload, slots, normed, inflow, bc_act, log = pl.pallas_call(
-        front_kernel,
-        grid=(STEPS,),
-        in_specs=[
-            rows_of(BLOCK, 1024), whole(1, 1024), whole(1024, INNER), whole(1024, 256),
-            whole(HEADS, 1024), whole(1, HEADS), whole(1, HEADS), whole(LEVELS, QROWS),
-        ],
-        out_specs=[
-            whole(OWNERS, 1, PAYLOAD), whole(LEVELS, QROWS), rows_of(BLOCK, 1024),
-            rows_of(BLOCK, INNER), rows_of(BLOCK, 256), rows_of(BLOCK, HEADS),
-        ],
-        out_shape=[
-            shape(OWNERS, 1, PAYLOAD), shape(LEVELS, QROWS, dtype=jnp.int32),
-            shape(FRAMES, 1024, dtype=bf16), shape(FRAMES, INNER, dtype=bf16),
-            shape(FRAMES, 256, dtype=bf16), shape(FRAMES, HEADS),
-        ],
-        scratch_shapes=[pltpu.VMEM((DIM, INNER), f32), pltpu.VMEM((8, 128), f32)],
-        compiler_params=settings(62),
-        name="front",
-    )(
-        frames, norm_gain.reshape(1, -1), x_weight, bc_weight, dt_weight.T,
-        dt_bias.reshape(1, -1), decay_rate.reshape(1, -1), code_ids,
-    )
-    arrived = exchange(payload)
-    inner, gate, reach, means = pl.pallas_call(
-        local_kernel,
-        grid=(STEPS,),
-        in_specs=[
-            rows_of(BLOCK, 1024), rows_of(BLOCK, 1024), rows_of(BLOCK, INNER),
-            rows_of(BLOCK, 256), rows_of(BLOCK, HEADS), whole(1024, INNER),
-        ],
-        out_specs=[
-            rows_of(BLOCK, INNER), rows_of(BLOCK, INNER), rows_of(BLOCK, HEADS),
-            pl.BlockSpec((4, BLOCK // 4, WIDTH), lambda i: (0, i, 0)),
-        ],
-        out_shape=[
-            shape(FRAMES, INNER), shape(FRAMES, INNER), shape(FRAMES, HEADS),
-            shape(4, QROWS, WIDTH),
-        ],
-        scratch_shapes=[pltpu.VMEM((DIM, INNER), f32), pltpu.VMEM((8, 128), f32)],
-        compiler_params=settings(62),
-        cost_estimate=pl.CostEstimate(flops=4 * 10**9, bytes_accessed=12 * 2**20, transcendentals=10**6),
-        name="local",
-    )(frames, normed, inflow, bc_act, log, z_weight)
-    arrived, inner = lax.optimization_barrier((arrived, inner))
-    found = pl.pallas_call(
-        lookup_kernel,
+def looked_up(arrived, codebook, cuts):
+    return pl.pallas_call(
+        functools.partial(lookup_kernel, cuts),
         grid=(LEVELS,),
         in_specs=[
             whole(OWNERS, 1, PAYLOAD), pl.BlockSpec((1, CODES, WIDTH), lambda i: (i, 0, 0)),
         ],
-        out_specs=whole(2 * TOTAL, 128),
-        out_shape=shape(2 * TOTAL, 128),
+        out_specs=[whole(2 * OWNERS * (high - low), 128) for low, high in cuts],
+        out_shape=[shape(2 * OWNERS * (high - low), 128) for low, high in cuts],
         scratch_shapes=[
-            pltpu.VMEM((OWNERS, 128), f32), pltpu.VMEM((TOTAL, 128), f32),
-            pltpu.VMEM((TOTAL, WIDTH), f32),
-        ],
-        compiler_params=settings(56),
+            pltpu.VMEM((OWNERS, 128), f32), pltpu.VMEM((OWNERS * SLOTS, 128), f32),
+            pltpu.VMEM((OWNERS * SLOTS, WIDTH), f32),
+        ],
+        compiler_params=settings(62),
         cost_estimate=pl.CostEstimate(flops=4 * 10**9, bytes_accessed=5 * 2**20, transcendentals=0),
         name="lookup",
     )(arrived, codebook)
-    fetched = exchange(found.reshape(OWNERS, 2 * SLOTS, 128)).reshape(2 * TOTAL, 128)
+
+
+def scanned(arrived):
     before = pl.pallas_call(
         scan_kernel,
         out_shape=shape(OWNERS, 8, 128),
         compiler_params=settings(16),
         name="scan",
     )(arrived)
-    incoming = exchange(before).reshape(INNER, DIM)
+    arrived, before = lax.optimization_barrier((arrived, before))
+    return exchange(before).reshape(INNER, DIM), arrived
+
+
+def shared_out(book, incoming, inner, gate, reach, bc_act, out_gain, out_weight):
     shares = pl.pallas_call(
         outer_kernel,
         grid_spec=pltpu.PrefetchScalarGridSpec(
@@ -418,13 +403,19 @@
     moved = [
         lax.ppermute(shares[d], "book", [(i, (i + d) % 4) for i in range(4)]) for d in (1, 2, 3)
     ]
+    return [shares[0], *moved]
+
+
+def gradient_terms(book, found, slots, shares, means):
+    fetched = exchange(found)
+    total = OWNERS * found.shape[1] // 2
     terms, taken = pl.pallas_call(
         taken_kernel,
-        out_shape=[shape(TOTAL, WIDTH), shape(QROWS, WIDTH)],
+        out_shape=[shape(total, WIDTH), shape(QROWS, WIDTH)],
         compiler_params=settings(40),
         cost_estimate=pl.CostEstimate(flops=3 * 10**9, bytes_accessed=3 * 2**20, transcendentals=0),
         name="taken",
-    )(fetched, slots)
+    )(fetched.reshape(2 * total, 128), slots)
     residual, grads = pl.pallas_call(
         residual_kernel,
         grid_spec=pltpu.PrefetchScalarGridSpec(
@@ -433,27 +424,128 @@
             in_specs=[whole(QROWS, WIDTH)] * 4
             + [
                 pl.BlockSpec((1, QROWS, WIDTH), lambda i, book: (book[0], 0, 0)),
-                whole(QROWS, WIDTH), whole(TOTAL, WIDTH), whole(LEVELS, QROWS),
+                whole(QROWS, WIDTH), whole(total, WIDTH), whole(LEVELS, QROWS),
             ],
-            out_specs=[whole(QROWS, WIDTH), whole(2 * TOTAL, 128)],
+            out_specs=[whole(QROWS, WIDTH), whole(2 * total, 128)],
         ),
-        out_shape=[shape(QROWS, WIDTH), shape(2 * TOTAL, 128)],
+        out_shape=[shape(QROWS, WIDTH), shape(2 * total, 128)],
         compiler_params=settings(40),
         name="residual",
-    )(book, shares[0], *moved, means, taken, terms, slots)
-    returned = exchange(grads.reshape(OWNERS, 2 * SLOTS, 128)).reshape(2 * TOTAL, 128)
-    arrived, grads = lax.optimization_barrier((arrived, grads))
-    codes = arrived[:, 0, 1152 : 1152 + SLOTS].astype(jnp.int32).reshape(1, TOTAL)
-    table = pl.pallas_call(
+    )(book, *shares, means, taken, terms, slots)
+    return residual, grads.reshape(found.shape)
+
+
+def gathered_table(codes, *grads):
+    return pl.pallas_call(
         table_kernel,
         grid=(6,),
-        in_specs=[whole(1, TOTAL), whole(2 * TOTAL, 128)],
+        in_specs=[whole(*codes.shape)] + [whole(*part.shape) for part in grads],
         out_specs=rows_of(LEVELS * CODES // 6, WIDTH),
         out_shape=shape(LEVELS * CODES, WIDTH),
-        scratch_shapes=[pltpu.VMEM((TOTAL, WIDTH), bf16)],
+        scratch_shapes=[pltpu.VMEM((codes.shape[1], WIDTH), bf16)],
         compiler_params=settings(40),
         name="table",
-    )(codes, returned)
+    )(codes, *grads)
+
+
+def asked_codes(arrived, low, high):
+    return arrived[:, 0, 1152 + low : 1152 + high].astype(jnp.int32).reshape(1, -1)
+
+
+def other_core(array):
+    return lax.ppermute(array, "seq_2", [(0, 1), (1, 0)])
+
+
+def with_all_slots(
+    book, arrived, few, slots, inner, gate, reach, means, bc_act, out_gain, out_weight, codebook
+):
+    incoming, arrived = scanned(arrived)
+    [found] = looked_up(arrived, codebook, [(0, SLOTS)])
+    shares = shared_out(book, incoming, inner, gate, reach, bc_act, out_gain, out_weight)
+    residual, grads = gradient_terms(
+        book, found.reshape(OWNERS, 2 * SLOTS, 128), slots, shares, means
+    )
+    arrived, grads = lax.optimization_barrier((arrived, grads))
+    returned = exchange(grads).reshape(-1, 128)
+    return residual, gathered_table(asked_codes(arrived, 0, SLOTS), returned)
+
+
+def with_few_slots(
+    book, arrived, few, slots, inner, gate, reach, means, bc_act, out_gain, out_weight, codebook
+):
+    incoming, arrived = scanned(arrived)
+    found, late = looked_up(arrived, codebook, [(0, FEW), (FEW, SLOTS)])
+    late, incoming = lax.optimization_barrier((late, incoming))
+    late = other_core(late).reshape(OWNERS, 2 * LATE, 128)
+    found = found.reshape(OWNERS, 2 * FEW, 128)
+    found = found + jnp.pad(late, ((0, 0), (2 * (FEW - LATE), 0), (0, 0)))
+    shares = shared_out(book, incoming, inner, gate, reach, bc_act, out_gain, out_weight)
+    residual, grads = gradient_terms(book, found, few, shares, means)
+    arrived, grads = lax.optimization_barrier((arrived, grads))
+    codes = jnp.concatenate(
+        [asked_codes(arrived, 0, FEW), asked_codes(arrived, FEW, SLOTS)], axis=1
+    )
+    returned = exchange(grads)
+    late = other_core(returned[:, 2 * (FEW - LATE) :].reshape(-1, 128))
+    return residual, gathered_table(codes, returned.reshape(-1, 128), late)
+
+
+def body(
+    frames, norm_gain, x_weight, z_weight, bc_weight, dt_weight, dt_bias, decay_rate,
+    out_gain, out_weight, codebook, code_ids,
+):
+    book = lax.axis_index("book").reshape(1)
+    payload, slots, few, hot, normed, inflow, bc_act, log = pl.pallas_call(
+        front_kernel,
+        grid=(STEPS,),
+        in_specs=[
+            rows_of(BLOCK, 1024), whole(1, 1024), whole(1024, INNER), whole(1024, 256),
+            whole(HEADS, 1024), whole(1, HEADS), whole(1, HEADS), whole(LEVELS, QROWS),
+        ],
+        out_specs=[
+            whole(OWNERS, 1, PAYLOAD), whole(LEVELS, QROWS), whole(LEVELS, QROWS),
+            whole(1, 128), rows_of(BLOCK, 1024),
+            rows_of(BLOCK, INNER), rows_of(BLOCK, 256), rows_of(BLOCK, HEADS),
+        ],
+        out_shape=[
+            shape(OWNERS, 1, PAYLOAD), shape(LEVELS, QROWS, dtype=jnp.int32),
+            shape(LEVELS, QROWS, dtype=jnp.int32), shape(1, 128),
+            shape(FRAMES, 1024, dtype=bf16), shape(FRAMES, INNER, dtype=bf16),
+            shape(FRAMES, 256, dtype=bf16), shape(FRAMES, HEADS),
+        ],
+        scratch_shapes=[pltpu.VMEM((DIM, INNER), f32), pltpu.VMEM((8, 128), f32)],
+        compiler_params=settings(62),
+        name="front",
+    )(
+        frames, norm_gain.reshape(1, -1), x_weight, bc_weight, dt_weight.T,
+        dt_bias.reshape(1, -1), decay_rate.reshape(1, -1), code_ids,
+    )
+    arrived = exchange(payload)
+    inner, gate, reach, means = pl.pallas_call(
+        local_kernel,
+        grid=(STEPS,),
+        in_specs=[
+            rows_of(BLOCK, 1024), rows_of(BLOCK, 1024), rows_of(BLOCK, INNER),
+            rows_of(BLOCK, 256), rows_of(BLOCK, HEADS), whole(1024, INNER),
+        ],
+        out_specs=[
+            rows_of(BLOCK, INNER), rows_of(BLOCK, INNER), rows_of(BLOCK, HEADS),
+            pl.BlockSpec((4, BLOCK // 4, WIDTH), lambda i: (0, i, 0)),
+        ],
+        out_shape=[
+            shape(FRAMES, INNER), shape(FRAMES, INNER), shape(FRAMES, HEADS),
+            shape(4, QROWS, WIDTH),
+        ],
+        scratch_shapes=[pltpu.VMEM((DIM, INNER), f32), pltpu.VMEM((8, 128), f32)],
+        compiler_params=settings(62),
+        cost_estimate=pl.CostEstimate(flops=4 * 10**9, bytes_accessed=12 * 2**20, transcendentals=10**6),
+        name="local",
+    )(frames, normed, inflow, bc_act, log, z_weight)
+    arrived, inner = lax.optimization_barrier((arrived, inner))
+    residual, table = lax.cond(
+        hot[0, 0] < 1.5, with_few_slots, with_all_slots,
+        book, arrived, few, slots, inner, gate, reach, means, bc_act, out_gain, out_weight, codebook,
+    )
     return residual, table.reshape(LEVELS, CODES, WIDTH)
 
 

time: 144 us -> 142 us (0.986); the launches traced: 143 us -> 139 us
  waiting for transfers between devices: 64.8 us -> 56.1 us
  starting transfers between devices: 34.3 us -> 37 us
  other arithmetic: 0.86 us -> 2.57 us
    all_to_all x4, waiting for transfers between devices: 64.8 us -> 53.7 us  [exchange(): return lax.all_to_all(array, SEQ, split_axis=0, concat_axis=0, tiled=True)]
    ppermute x3 -> x5, waiting for transfers between devices: 0.01 us -> 2.36 us  [the longest x2 2.35 us: other_core(): return lax.ppermute(array, 'seq_2', [(0, 1), (1, 0)])]
    add x0 -> x1, other arithmetic: none -> 2.3 us  [with_few_slots(): found = found + jnp.pad(late, ((0, 0), (2 * (FEW - LATE), 0), (0, 0)))]
    ppermute x3 -> x5, starting transfers between devices: 4.79 us -> 6.49 us  [the longest x3 4.79 us: shared_out(): lax.ppermute(shares[d], 'book', [(i, (i + d) % 4) for i in range(4)])]
  transfers between devices with their start and end apart: 7 -> 9, of which waited for: 4 -> 6; matrix products, arithmetic and copies ran while one was open for 1% -> 0% of each run, Pallas kernels for 18% -> 19%
where the time goes in v4:
time: 142 us; the launch traced here: 139 us
  waiting for transfers between devices  56.1 us (40%)
  Pallas kernels  42.1 us (30%)
  starting transfers between devices  37 us (26%)
  other arithmetic  2.57 us (2%)
    all_to_all x4, waiting for transfers between devices, exchange(): return lax.all_to_all(array, SEQ, split_axis=0, concat_axis=0, tiled=True)  53.7 us
    all_to_all x4, starting transfers between devices, exchange(): return lax.all_to_all(array, SEQ, split_axis=0, concat_axis=0, tiled=True)  30.5 us
    pallas_call x1, Pallas kernels, body(): pl.pallas_call(local_kernel, grid=(STEPS,), in_specs=[rows_of(BLOCK, 1024...  9.16 us
    pallas_call x1, Pallas kernels, shared_out(): pl.pallas_call(outer_kernel, grid_spec=pltpu.PrefetchScalarGridSpec(num_s...  8.97 us
    pallas_call x1, Pallas kernels, body(): pl.pallas_call(front_kernel, grid=(STEPS,), in_specs=[rows_of(BLOCK, 1024...  8.76 us
    pallas_call x1, Pallas kernels, looked_up(): pl.pallas_call(functools.partial(lookup_kernel, cuts), grid=(LEVELS,), in...  5.81 us
    ppermute x3, starting transfers between devices, shared_out(): lax.ppermute(shares[d], 'book', [(i, (i + d) % 4) for i in range(4)])  4.79 us
    pallas_call x1, Pallas kernels, gathered_table(): pl.pallas_call(table_kernel, grid=(6,), in_specs=[whole(*codes.shape)] +...  4.52 us
  transfers between devices with their start and end apart: 9, of which 6 were waited for; matrix products, arithmetic and copies ran while one was open for 0% of the time, Pallas kernels for 19%

profile of v4, /device:TPU:1, one launch (start us, length us, event | category | flops | bytes accessed | tf_op | source)
XLA Modules:
  0.0 139.4 jit_solution(14394333915042812486)
XLA Ops:
  0.6 8.8 %front.1 = (f32[64,1,1280]{2,1,0:T(1,128)}, s32[3,256]{1,0:T(4,128)S(1)}, s32[3,256]{1,0:T(4,128)S(1)}, f32[1,128]{1,0:T(1,128)}, bf16[1024,1024]{1,0:T(8,128)(2...) custom-call(bf16[1024,1024]{1,0:T(8,128)(2,1)} %frames_ref.3, ...), custom_call_target="tpu_custom_call" | custom-call | tf_op jit(solution)/shard_map/front/pallas_call | solution.py:498
  9.4 13.2 %all-to-all-start.6 = ((f32[64,1,1280]{2,1,0:T(1,128)}), f32[64,1,1280]{2,1,0:T(1,128)S(1)}, u32[]{:S(2)}, u32[]{:S(2)}) async-start(f32[64,1,1280]{2,1,0:T(1,128)} %get-tuple-element.112), calls=%async_computation.6 | async-start | bytes 655360 | tf_op jit(solution)/shard_map/all_to_all | solution.py:351
  23.2 9.2 %local.1 = (f32[1024,512]{1,0:T(8,128)}, f32[1024,512]{1,0:T(8,128)}, f32[1024,4]{1,0:T(8,128)}, f32[4,256,256]{2,1,0:T(8,128)}) custom-call(bf16[1024,1024]{1,0:T(8,128)(2,1)} %frames_ref.3, bf16[1024,1024]{1,0:T(8,128)(2,1)} %get-tuple-element.113.normed_ref, bf16[1024,512]{1,0:T(8,128)(2,1)} %get-tuple-element.114.inflow_ref, ...), custom_call_target="tpu_custom_call" | custom-call | flops 4000000000 | bytes 12582912 | tf_op jit(solution)/shard_map/local/pallas_call | solution.py:524
  32.4 4.4 %all-to-all-done.6 = f32[64,1,1280]{2,1,0:T(1,128)S(1)} async-done(((f32[64,1,1280]{2,1,0:T(1,128)}), f32[64,1,1280]{2,1,0:T(1,128)S(1)}, u32[]{:S(2)}, u32[]{:S(2)}) %all-to-all-start.6) | async-done | bytes 327712 | tf_op jit(solution)/shard_map/all_to_all | solution.py:351
  36.7 102.6 %conditional.1 = (f32[256,256]{1,0:T(8,128)}, f32[3,1024,256]{2,1,0:T(8,128)}) conditional(s32[]{:T(128)} %bitcast.20, (f32[64,1,1280]{2,1,0:T(1,128)S(1)}, f32[512]{0:T(512)S(1)}, s32[1]{0:T(128)}, f32[1024,512]{1,0:T(8,128)}, f32[1024,512]{1,0:T(8,128)}, /*index=5*/f32[1024,4]{1,0:T(8,128)}, bf16[1024,256]{1,0:T(8,128)(2,1)S(1)}, ...), branch_computations={%region_0.0_spmd, %region_1.2_spmd} | conditional | flops 9000263680 | bytes 40401320 | solution.py:545
  36.7 0.9 scan.3
  37.7 6.2 %all-to-all-start.3 = ((f32[64,8,128]{2,1,0:T(8,128)}), f32[64,8,128]{2,1,0:T(8,128)S(1)}, u32[]{:S(2)}, u32[]{:S(2)}) async-start(f32[64,8,128]{2,1,0:T(8,128)} %scan.3), calls=%async_computation.3 | async-start | bytes 524288 | tf_op jit(solution)/shard_map/cond/branch_1_fun/all_to_all | solution.py:351
  43.9 5.8 %lookup.3 = (f32[2048,128]{1,0:T(8,128)}, f32[512,128]{1,0:T(8,128)}) custom-call(f32[64,1,1280]{2,1,0:T(1,128)S(1)} %get-tuple-element.93.arrived_ref, f32[3,1024,256]{2,1,0:T(8,128)} %get-tuple-element.75.table_ref), custom_call_target="tpu_custom_call" | custom-call | flops 4000000000 | bytes 5242880 | tf_op jit(solution)/shard_map/cond/branch_1_fun/lookup/pallas_call | solution.py:355
  49.7 7.3 %all-to-all-done.3 = f32[64,8,128]{2,1,0:T(8,128)S(1)} async-done(((f32[64,8,128]{2,1,0:T(8,128)}), f32[64,8,128]{2,1,0:T(8,128)S(1)}, u32[]{:S(2)}, u32[]{:S(2)}) %all-to-all-start.3) | async-done | bytes 262176 | tf_op jit(solution)/shard_map/cond/branch_1_fun/all_to_all | solution.py:351
  57.3 1.5 %collective-permute-done.6 = f32[512,128]{1,0:T(8,128)S(1)} collective-permute-done((f32[512,128]{1,0:T(8,128)}, f32[512,128]{1,0:T(8,128)S(1)}, u32[]{:S(2)}, u32[]{:S(2)}) %collective-permute-start.6) | collective-permute-done | bytes 262176 | tf_op jit(solution)/shard_map/cond/branch_1_fun/ppermute | solution.py:456
  58.8 2.3 %pad_add_fusion = f32[64,32,128]{2,1,0:T(8,128)} fusion(f32[64,32,128]{2,1,0:T(8,128)} %bitcast.31, f32[64,8,128]{2,1,0:T(8,128)S(1)} %bitcast.32), kind=kLoop, calls=%fused_computation.1 | loop fusion | flops 262144 | bytes 2359296 | tf_op jit(solution)/shard_map/cond/branch_1_fun/add | solution.py:481
  61.1 4.7 %all-to-all-start.4 = ((f32[64,32,128]{2,1,0:T(8,128)}), f32[64,32,128]{2,1,0:T(8,128)S(1)}, u32[]{:S(2)}, u32[]{:S(2)}) async-start(f32[64,32,128]{2,1,0:T(8,128)} %pad_add_fusion), calls=%async_computation.4 | async-start | bytes 2097152 | tf_op jit(solution)/shard_map/cond/branch_1_fun/all_to_all | solution.py:351
  65.8 9.0 %outer.3 = (f32[256,256]{1,0:T(8,128)}, f32[256,256]{1,0:T(8,128)}, f32[256,256]{1,0:T(8,128)}, f32[256,256]{1,0:T(8,128)}) custom-call(s32[1]{0:T(128)} %get-tuple-element.68.book_ref, f32[1024,512]{1,0:T(8,128)} %get-tuple-element.69.inner_ref, f32[1024,512]{1,0:T(8,128)} %get-tuple-element.70.gate_ref, f32[1024,4]{1,0:T(8,128)} %get-tuple-element.71.reach_ref, ...), custom_call_target="tpu_custom_call" | custom-call | flops 2000000000 | bytes 8388608 | tf_op jit(solution)/shard_map/cond/branch_1_fun/outer/pallas_call | solution.py:385
  74.8 1.2 collective-permute-start.3
  76.0 2.4 %collective-permute-start.4 = (f32[256,256]{1,0:T(8,128)}, f32[256,256]{1,0:T(8,128)S(1)}, u32[]{:S(2)}, u32[]{:S(2)}) collective-permute-start(f32[256,256]{1,0:T(8,128)} %get-tuple-element.83), channel_id=1, source_target_pairs={{0,2},{1,3},{2,0},{3,1},{4,6},{5,7},{6,4},{7,5},{8,10},{9,11},{10,... | collective-permute-start | bytes 786440 | tf_op jit(solution)/shard_map/cond/branch_1_fun/ppermute | solution.py:404
  78.4 1.1 collective-permute-start.5
  79.6 14.2 %all-to-all-done.4 = f32[64,32,128]{2,1,0:T(8,128)S(1)} async-done(((f32[64,32,128]{2,1,0:T(8,128)}), f32[64,32,128]{2,1,0:T(8,128)S(1)}, u32[]{:S(2)}, u32[]{:S(2)}) %all-to-all-start.4) | async-done | bytes 1048608 | tf_op jit(solution)/shard_map/cond/branch_1_fun/all_to_all | solution.py:351
  93.8 2.4 %taken.3 = (f32[1024,256]{1,0:T(8,128)S(1)}, f32[256,256]{1,0:T(8,128)S(1)}) custom-call(f32[2048,128]{1,0:T(8,128)S(1)} %bitcast.27, s32[3,256]{1,0:T(4,128)S(1)} %get-tuple-element.88.slots_ref), custom_call_target="tpu_custom_call" | custom-call | flops 3000000000 | bytes 3145728 | tf_op jit(solution)/shard_map/cond/branch_1_fun/taken/pallas_call | solution.py:412
  96.2 1.5 %residual.3 = (f32[256,256]{1,0:T(8,128)}, f32[2048,128]{1,0:T(8,128)}) custom-call(s32[1]{0:T(128)} %get-tuple-element.68.book_ref, f32[256,256]{1,0:T(8,128)S(1)} %copy-done.1, f32[256,256]{1,0:T(8,128)S(1)} %collective-permute-done.3.from_1, f32[256,256]{1,0:T(8,128)S(1)} %collective-permute-done.4.from_2, f32[256,256]{1,0:T(8,128)S(1)} %collective-permute-done.5.from_3, ...), custom_call_target="tpu_custom_call" | custom-call | tf_op jit(solution)/shard_map/cond/branch_1_fun/residual/pallas_call | solution.py:419
  97.8 6.5 %all-to-all-start.5 = ((f32[64,32,128]{2,1,0:T(8,128)}), f32[64,32,128]{2,1,0:T(8,128)S(1)}, u32[]{:S(2)}, u32[]{:S(2)}) async-start(f32[64,32,128]{2,1,0:T(8,128)} %bitcast.12), calls=%async_computation.5 | async-start | bytes 2097152 | tf_op jit(solution)/shard_map/cond/branch_1_fun/all_to_all | solution.py:351
  104.4 27.8 %all-to-all-done.5 = f32[64,32,128]{2,1,0:T(8,128)S(1)} async-done(((f32[64,32,128]{2,1,0:T(8,128)}), f32[64,32,128]{2,1,0:T(8,128)S(1)}, u32[]{:S(2)}, u32[]{:S(2)}) %all-to-all-start.5) | async-done | bytes 1048608 | tf_op jit(solution)/shard_map/cond/branch_1_fun/all_to_all | solution.py:351
  132.3 1.4 %collective-permute-start.7 = (f32[512,128]{1,0:T(8,128)S(1)}, f32[512,128]{1,0:T(8,128)S(1)}, u32[]{:S(2)}, u32[]{:S(2)}) collective-permute-start(f32[512,128]{1,0:T(8,128)S(1)} %slice_bitcast_fusion), channel_id=1, source_target_pairs={{0,4},{4,0},{1,5},{5,1},{2,6},{6,2},{3,7},{7,3},{8,12},{12,8},{9,1... | collective-permute-start | bytes 786440 | tf_op jit(solution)/shard_map/cond/branch_1_fun/ppermute | solution.py:456
  134.0 0.9 collective-permute-done.7.refs_1_
  134.9 4.5 %table.3 = f32[3072,256]{1,0:T(8,128)} custom-call(s32[1,1280]{1,0:T(1,128)S(1)} %pad_add_fusion.1.codes_ref, f32[2048,128]{1,0:T(8,128)S(1)} %bitcast.24, f32[512,128]{1,0:T(8,128)S(1)} %collective-permute-done.7.refs_1_), custom_call_target="tpu_custom_call" | custom-call | tf_op jit(solution)/shard_map/cond/branch_1_fun/table/pallas_call | solution.py:439
  (20 shorter events, 0.8 us)
Async XLA Ops:
  9.4 27.3 %all-to-all-start.6 = ((f32[64,1,1280]{2,1,0:T(1,128)}), f32[64,1,1280]{2,1,0:T(1,128)S(1)}, u32[]{:S(2)}, u32[]{:S(2)}) async-start(f32[64,1,1280]{2,1,0:T(1,128)} %get-tuple-element.112), calls=%async_computation.6 | async-start | bytes 655360 | tf_op jit(solution)/shard_map/all_to_all | solution.py:351
  23.2 13.5 %copy-start.8 = (f32[512]{0:T(512)S(1)}, f32[512]{0:T(512)}, u32[]{:S(2)}) copy-start(f32[512]{0:T(512)} %param.22) | copy-start | bytes 6148
  36.7 12.9 %copy-start.7 = (bf16[1024,256]{1,0:T(8,128)(2,1)}, bf16[1024,256]{1,0:T(8,128)(2,1)S(1)}, u32[]{:S(2)}) copy-start(bf16[1024,256]{1,0:T(8,128)(2,1)S(1)} %get-tuple-element.72.c_ref) | copy-start | bytes 1572868 | tf_op jit(solution)/shard_map/cond
  37.7 19.4 %all-to-all-start.3 = ((f32[64,8,128]{2,1,0:T(8,128)}), f32[64,8,128]{2,1,0:T(8,128)S(1)}, u32[]{:S(2)}, u32[]{:S(2)}) async-start(f32[64,8,128]{2,1,0:T(8,128)} %scan.3), calls=%async_computation.3 | async-start | bytes 524288 | tf_op jit(solution)/shard_map/cond/branch_1_fun/all_to_all | solution.py:351
  57.0 4.0 %copy-start.4 = (f32[64,8,128]{2,1,0:T(8,128)}, f32[64,8,128]{2,1,0:T(8,128)S(1)}, u32[]{:S(2)}) copy-start(f32[64,8,128]{2,1,0:T(8,128)S(1)} %all-to-all-done.3) | copy-start | bytes 786436 | tf_op jit(solution)/shard_map/cond
  57.0 1.7 %collective-permute-start.6 = (f32[512,128]{1,0:T(8,128)}, f32[512,128]{1,0:T(8,128)S(1)}, u32[]{:S(2)}, u32[]{:S(2)}) collective-permute-start(f32[512,128]{1,0:T(8,128)} %get-tuple-element.87), channel_id=1, source_target_pairs={{0,4},{4,0},{1,5},{5,1},{2,6},{6,2},{3,7},{7,3},{8,12},{12,8},{9,1... | collective-permute-start | bytes 786440 | tf_op jit(solution)/shard_map/cond/branch_1_fun/ppermute | solution.py:456
  61.1 32.7 %all-to-all-start.4 = ((f32[64,32,128]{2,1,0:T(8,128)}), f32[64,32,128]{2,1,0:T(8,128)S(1)}, u32[]{:S(2)}, u32[]{:S(2)}) async-start(f32[64,32,128]{2,1,0:T(8,128)} %pad_add_fusion), calls=%async_computation.4 | async-start | bytes 2097152 | tf_op jit(solution)/shard_map/cond/branch_1_fun/all_to_all | solution.py:351
  74.8 21.4 %collective-permute-start.3 = (f32[256,256]{1,0:T(8,128)}, f32[256,256]{1,0:T(8,128)S(1)}, u32[]{:S(2)}, u32[]{:S(2)}) collective-permute-start(f32[256,256]{1,0:T(8,128)} %get-tuple-element.82), channel_id=1, source_target_pairs={{0,1},{1,2},{2,3},{3,0},{4,5},{5,6},{6,7},{7,4},{8,9},{9,10},{10,1... | collective-permute-start | bytes 786440 | tf_op jit(solution)/shard_map/cond/branch_1_fun/ppermute | solution.py:404
  76.0 20.2 %collective-permute-start.4 = (f32[256,256]{1,0:T(8,128)}, f32[256,256]{1,0:T(8,128)S(1)}, u32[]{:S(2)}, u32[]{:S(2)}) collective-permute-start(f32[256,256]{1,0:T(8,128)} %get-tuple-element.83), channel_id=1, source_target_pairs={{0,2},{1,3},{2,0},{3,1},{4,6},{5,7},{6,4},{7,5},{8,10},{9,11},{10,... | collective-permute-start | bytes 786440 | tf_op jit(solution)/shard_map/cond/branch_1_fun/ppermute | solution.py:404
  78.4 17.8 %collective-permute-start.5 = (f32[256,256]{1,0:T(8,128)}, f32[256,256]{1,0:T(8,128)S(1)}, u32[]{:S(2)}, u32[]{:S(2)}) collective-permute-start(f32[256,256]{1,0:T(8,128)} %get-tuple-element.84), channel_id=1, source_target_pairs={{0,3},{1,0},{2,1},{3,2},{4,7},{5,4},{6,5},{7,6},{8,11},{9,8},{10,9... | collective-permute-start | bytes 786440 | tf_op jit(solution)/shard_map/cond/branch_1_fun/ppermute | solution.py:404
  93.8 2.4 %copy-start.1 = (f32[256,256]{1,0:T(8,128)S(1)}, f32[256,256]{1,0:T(8,128)}, u32[]{:S(2)}) copy-start(f32[256,256]{1,0:T(8,128)} %get-tuple-element.81.own_ref) | copy-start | bytes 786436 | tf_op jit(solution)/shard_map/cond
  93.8 2.4 %copy-start.3 = (f32[4,256,256]{2,1,0:T(8,128)S(1)}, f32[4,256,256]{2,1,0:T(8,128)}, u32[]{:S(2)}) copy-start(f32[4,256,256]{2,1,0:T(8,128)} %get-tuple-element.85.means_ref) | copy-start | bytes 3145732 | tf_op jit(solution)/shard_map/cond
  97.8 34.5 %all-to-all-start.5 = ((f32[64,32,128]{2,1,0:T(8,128)}), f32[64,32,128]{2,1,0:T(8,128)S(1)}, u32[]{:S(2)}, u32[]{:S(2)}) async-start(f32[64,32,128]{2,1,0:T(8,128)} %bitcast.12), calls=%async_computation.5 | async-start | bytes 2097152 | tf_op jit(solution)/shard_map/cond/branch_1_fun/all_to_all | solution.py:351
  132.3 2.6 %collective-permute-start.7 = (f32[512,128]{1,0:T(8,128)S(1)}, f32[512,128]{1,0:T(8,128)S(1)}, u32[]{:S(2)}, u32[]{:S(2)}) collective-permute-start(f32[512,128]{1,0:T(8,128)S(1)} %slice_bitcast_fusion), channel_id=1, source_target_pairs={{0,4},{4,0},{1,5},{5,1},{2,6},{6,2},{3,7},{7,3},{8,12},{12,8},{9,1... | collective-permute-start | bytes 786440 | tf_op jit(solution)/shard_map/cond/branch_1_fun/ppermute | solution.py:456

commit v5 on v4

--- a/solution.py
+++ b/solution.py
@@ -24,7 +24,8 @@
 HEADS = 4
 DIM = 128
 INNER = HEADS * DIM
-PAYLOAD = 10 * 128
+PAYLOAD = 9 * 128
+ASKED = 8 * 128
 
 f32 = jnp.float32
 bf16 = jnp.bfloat16
@@ -60,6 +61,10 @@
 
 def silu(values):
     return values * jax.nn.sigmoid(values)
+
+
+def filled(columns):
+    return jnp.concatenate([columns, jnp.zeros((columns.shape[0], 128 - HEADS), f32)], axis=1)
 
 
 def per_head(columns):
@@ -126,7 +131,7 @@
         total_ref[...] = jnp.zeros_like(total_ref)
         asked = place_codes(ids_ref, slots_ref, few_ref, hot_ref)
         for k in range(OWNERS):
-            payload_ref[k, :, 1152:1280] = asked[k : k + 1, :]
+            payload_ref[k, :, ASKED:] = asked[k : k + 1, :]
 
     frames = frames_ref[...].astype(f32)
     square = jnp.mean(frames * frames, axis=1, keepdims=True)
@@ -137,7 +142,7 @@
     raw = lax.dot_general(normed, dt_w_ref[...], NT, preferred_element_type=f32) + bias_ref[...]
     dt = jnp.maximum(raw, 0.0) + jnp.log1p(jnp.exp(-jnp.abs(raw)))
     log = -dt * rate_ref[...]
-    log_ref[...] = log
+    log_ref[...] = filled(log)
     causal = iota((BLOCK, BLOCK), 0) >= iota((BLOCK, BLOCK), 1)
     cum = running_sum(causal, log)
     x_act = silu(dot(normed, x_w_ref[...]).astype(bf16).astype(f32))
@@ -155,15 +160,15 @@
             lanes = slice(head * DIM, (head + 1) * DIM)
             for r in range(8):
                 payload_ref[k, :, r * 128 : (r + 1) * 128] = state_ref[row + r : row + r + 1, lanes]
-            payload_ref[k, :, 1024:1152] = jnp.broadcast_to(
-                total_ref[0:1, head : head + 1], (1, 128)
+            payload_ref[k, :, ASKED:] = jnp.where(
+                iota((1, 128), 1) < 64, payload_ref[k, :, ASKED:], total_ref[0:1, head : head + 1]
             )
 
 
 def scan_kernel(arrived_ref, before_ref):
     carried = [jnp.zeros((1, 128), f32) for _ in range(8)]
     for k in range(OWNERS):
-        decay = jnp.exp(arrived_ref[k, :, 1024:1152])
+        decay = jnp.exp(jnp.broadcast_to(arrived_ref[k, :, PAYLOAD - 1 :], (1, 128)))
         for r in range(8):
             before_ref[k, r : r + 1, :] = carried[r]
             carried[r] = carried[r] * decay + arrived_ref[k, :, r * 128 : (r + 1) * 128]
@@ -187,9 +192,9 @@
     for g in range(4):
         means_ref[g] = means[:, g * WIDTH : (g + 1) * WIDTH]
     causal = iota((BLOCK, BLOCK), 0) >= iota((BLOCK, BLOCK), 1)
-    log = log_ref[...]
+    log = log_ref[:, :HEADS]
     cum = running_sum(causal, log)
-    cum_rows = jnp.concatenate([cum, jnp.zeros((BLOCK, 128 - HEADS), f32)], axis=1).T
+    cum_rows = filled(cum).T
     b_act, c_act = bc_ref[:, :DIM], bc_ref[:, DIM:]
     inflow = inflow_ref[...]
     scores = jnp.where(causal, lax.dot_general(c_act, b_act, NT, preferred_element_type=f32), 0.0)
@@ -199,7 +204,7 @@
         gaps = jnp.minimum(cum[:, h : h + 1] - cum_rows[h : h + 1, :], 0.0)
         mixed = (jnp.exp(gaps) * scores).astype(bf16)
         inner_ref[:, lanes] = dot(mixed, inflow[:, lanes]) + carried[:, lanes]
-    reach_ref[...] = jnp.exp(cum + total_ref[0:1, 0:HEADS])
+    reach_ref[...] = filled(jnp.exp(cum + total_ref[0:1, 0:HEADS]))
     last = cum[BLOCK - 1 :, :]
     total_ref[0:1, 0:HEADS] += last
     decayed = (inflow.astype(f32) * per_head(jnp.exp(last - cum))).astype(bf16)
@@ -248,7 +253,7 @@
     @pl.when(level == 0)
     def _():
         for k in range(OWNERS):
-            asked_ref[k : k + 1, :] = arrived_ref[k, :, 1152:1280]
+            asked_ref[k : k + 1, :] = arrived_ref[k, :, ASKED:]
         turned = asked_ref[...].T
         start = 0
         for low, high in cuts:
@@ -277,45 +282,51 @@
     return jnp.concatenate([ref[pl.ds(0, half, 2), :], ref[pl.ds(1, half, 2), :]], axis=1)
 
 
-def taken_kernel(found_ref, slots_ref, terms_ref, taken_ref):
+def places_kernel(slots_ref, columns_ref, spreads_ref):
+    total = spreads_ref.shape[0]
+    slots = jnp.concatenate(
+        [slots_ref[...].astype(f32), jnp.zeros((128 - LEVELS, QROWS), f32)], axis=0
+    )
+    columns_ref[...] = slots.T.astype(jnp.int32)
+    place = iota((total, QROWS), 0)
+    spread = place == slots_ref[0:1, :]
+    for k in range(1, LEVELS):
+        here = place == slots_ref[k : k + 1, :]
+        spreads_ref[:, (k - 1) * QROWS : k * QROWS] = here.astype(bf16)
+        spread = spread | here
+    spreads_ref[:, (LEVELS - 1) * QROWS :] = spread.astype(bf16)
+
+
+def taken_kernel(found_ref, columns_ref, spreads_ref, terms_ref, taken_ref):
     found = joined_rows(found_ref)
-    total = found.shape[0]
     rounded = found.astype(bf16)
-    slots = jnp.concatenate(
-        [slots_ref[...].astype(f32), jnp.zeros((8 - LEVELS, QROWS), f32)], axis=0
-    )
-    same = (iota((QROWS, QROWS), 0) == iota((QROWS, QROWS), 1)).astype(f32)
-    columns = lax.dot_general(same, slots, NT, preferred_element_type=f32, precision=HIGHEST)
-    columns = columns.astype(jnp.int32)
     taken = jnp.zeros((QROWS, WIDTH), f32)
     terms = found
     for k in range(LEVELS):
         if k:
-            spread = (iota((total, QROWS), 0) == slots_ref[k : k + 1, :]).astype(bf16)
+            spread = spreads_ref[:, (k - 1) * QROWS : k * QROWS]
             terms = terms + folded(dot(spread, two_parts(taken)))
-        picks = (columns[:, k : k + 1] == iota((QROWS, total), 1)).astype(bf16)
+        places = iota((QROWS, found.shape[0]), 1)
+        picks = (columns_ref[:, k : k + 1] == places).astype(bf16)
         taken = taken + dot(picks, rounded)
     terms_ref[...] = terms
     taken_ref[...] = taken
 
 
 def residual_kernel(
-    book_ref, own_ref, from_1, from_2, from_3, means_ref, taken_ref, terms_ref, slots_ref,
+    book_ref, own_ref, from_1, from_2, from_3, means_ref, taken_ref, terms_ref, spread_ref,
     residual_ref, grads_ref,
 ):
     pooled = own_ref[...] + from_1[...] + from_2[...] + from_3[...] + means_ref[0]
     residual_ref[...] = pooled - taken_ref[...]
-    place = iota((terms_ref.shape[0], QROWS), 0)
-    spread = place == slots_ref[0:1, :]
-    for k in range(1, LEVELS):
-        spread = spread | (place == slots_ref[k : k + 1, :])
-    grads = terms_ref[...] - folded(dot(spread.astype(bf16), two_parts(pooled)))
+    grads = terms_ref[...] - folded(dot(spread_ref[...], two_parts(pooled)))
     split_rows(grads_ref, grads)
 
 
 def table_kernel(codes_ref, *refs):
-    grads_refs, (table_ref, rounded_ref) = refs[:-2], refs[-2:]
+    grads_refs, (table_ref, rounded_ref, low_ref, high_ref) = refs[:-4], refs[-4:]
     step = pl.program_id(0)
+    total = codes_ref.shape[1]
 
     @pl.when(step == 0)
     def _():
@@ -324,11 +335,20 @@
             rows = grads_ref.shape[0] // 2
             rounded_ref[start : start + rows, :] = joined_rows(grads_ref).astype(bf16)
             start += rows
-
-    rows = table_ref.shape[0]
-    place = iota((rows, codes_ref.shape[1]), 0) + (step * rows + 1)
-    chosen = (codes_ref[...] == place).astype(bf16)
-    table_ref[...] = dot(chosen, rounded_ref[...])
+        code = codes_ref[...] - 1
+        low_ref[...] = ((code & 127) == iota((128, total), 0)).astype(bf16)
+        high_ref[...] = jnp.broadcast_to(code >> 7, (16, total))
+
+    groups = table_ref.shape[0] // 128
+    chosen = []
+    for g in range(groups):
+        mask = (high_ref[...] == step * groups + g).astype(bf16)
+        chosen.append(low_ref[...] * jnp.concatenate([mask] * 8, axis=0))
+    table_ref[...] = dot(jnp.concatenate(chosen, axis=0), rounded_ref[...])
+
+
+def add_kernel(found_ref, late_ref, sum_ref):
+    sum_ref[...] = found_ref[...] + late_ref[...]
 
 
 def shape(*dims, dtype=f32):
@@ -388,7 +408,7 @@
             num_scalar_prefetch=1,
             grid=(STEPS,),
             in_specs=[
-                rows_of(BLOCK, INNER), rows_of(BLOCK, INNER), rows_of(BLOCK, HEADS),
+                rows_of(BLOCK, INNER), rows_of(BLOCK, INNER), rows_of(BLOCK, 128),
                 pl.BlockSpec((BLOCK, DIM), lambda i, *_: (i, 1)),
                 whole(INNER, DIM), whole(1, INNER), whole(INNER, 1024),
             ],
@@ -407,15 +427,25 @@
 
 
 def gradient_terms(book, found, slots, shares, means):
+    total = OWNERS * found.shape[1] // 2
     fetched = exchange(found)
-    total = OWNERS * found.shape[1] // 2
+    own, slots = lax.optimization_barrier((shares[0], slots))
+    columns, spreads = pl.pallas_call(
+        places_kernel,
+        out_shape=[
+            shape(QROWS, 128, dtype=jnp.int32), shape(total, LEVELS * QROWS, dtype=bf16),
+        ],
+        compiler_params=settings(32),
+        cost_estimate=pl.CostEstimate(flops=10**9, bytes_accessed=2**20, transcendentals=0),
+        name="places",
+    )(slots)
     terms, taken = pl.pallas_call(
         taken_kernel,
         out_shape=[shape(total, WIDTH), shape(QROWS, WIDTH)],
-        compiler_params=settings(40),
+        compiler_params=settings(24),
         cost_estimate=pl.CostEstimate(flops=3 * 10**9, bytes_accessed=3 * 2**20, transcendentals=0),
         name="taken",
-    )(fetched.reshape(2 * total, 128), slots)
+    )(fetched.reshape(2 * total, 128), columns, spreads)
     residual, grads = pl.pallas_call(
         residual_kernel,
         grid_spec=pltpu.PrefetchScalarGridSpec(
@@ -424,32 +454,36 @@
             in_specs=[whole(QROWS, WIDTH)] * 4
             + [
                 pl.BlockSpec((1, QROWS, WIDTH), lambda i, book: (book[0], 0, 0)),
-                whole(QROWS, WIDTH), whole(total, WIDTH), whole(LEVELS, QROWS),
+                whole(QROWS, WIDTH), whole(total, WIDTH),
+                pl.BlockSpec((total, QROWS), lambda i, book: (0, LEVELS - 1)),
             ],
             out_specs=[whole(QROWS, WIDTH), whole(2 * total, 128)],
         ),
         out_shape=[shape(QROWS, WIDTH), shape(2 * total, 128)],
-        compiler_params=settings(40),
+        compiler_params=settings(24),
         name="residual",
-    )(book, *shares, means, taken, terms, slots)
+    )(book, own, *shares[1:], means, taken, terms, spreads)
     return residual, grads.reshape(found.shape)
 
 
 def gathered_table(codes, *grads):
     return pl.pallas_call(
         table_kernel,
-        grid=(6,),
+        grid=(3,),
         in_specs=[whole(*codes.shape)] + [whole(*part.shape) for part in grads],
-        out_specs=rows_of(LEVELS * CODES // 6, WIDTH),
+        out_specs=rows_of(CODES, WIDTH),
         out_shape=shape(LEVELS * CODES, WIDTH),
-        scratch_shapes=[pltpu.VMEM((codes.shape[1], WIDTH), bf16)],
+        scratch_shapes=[
+            pltpu.VMEM((codes.shape[1], WIDTH), bf16), pltpu.VMEM((128, codes.shape[1]), bf16),
+            pltpu.VMEM((16, codes.shape[1]), jnp.int32),
+        ],
         compiler_params=settings(40),
         name="table",
     )(codes, *grads)
 
 
 def asked_codes(arrived, low, high):
-    return arrived[:, 0, 1152 + low : 1152 + high].astype(jnp.int32).reshape(1, -1)
+    return arrived[:, 0, ASKED + low : ASKED + high].astype(jnp.int32).reshape(1, -1)
 
 
 def other_core(array):
@@ -478,14 +512,24 @@
     late, incoming = lax.optimization_barrier((late, incoming))
     late = other_core(late).reshape(OWNERS, 2 * LATE, 128)
     found = found.reshape(OWNERS, 2 * FEW, 128)
-    found = found + jnp.pad(late, ((0, 0), (2 * (FEW - LATE), 0), (0, 0)))
+    last = pl.BlockSpec((OWNERS, 2 * LATE, 128), lambda i: (0, FEW // LATE - 1, 0))
+    found = pl.pallas_call(
+        add_kernel,
+        grid=(1,),
+        in_specs=[last, whole(OWNERS, 2 * LATE, 128)],
+        out_specs=last,
+        out_shape=shape(OWNERS, 2 * FEW, 128),
+        input_output_aliases={0: 0},
+        compiler_params=settings(57),
+        name="relayed",
+    )(found, late)
     shares = shared_out(book, incoming, inner, gate, reach, bc_act, out_gain, out_weight)
     residual, grads = gradient_terms(book, found, few, shares, means)
     arrived, grads = lax.optimization_barrier((arrived, grads))
     codes = jnp.concatenate(
         [asked_codes(arrived, 0, FEW), asked_codes(arrived, FEW, SLOTS)], axis=1
     )
-    returned = exchange(grads)
+    returned, codes = lax.optimization_barrier((exchange(grads), codes))
     late = other_core(returned[:, 2 * (FEW - LATE) :].reshape(-1, 128))
     return residual, gathered_table(codes, returned.reshape(-1, 128), late)
 
@@ -505,13 +549,13 @@
         out_specs=[
             whole(OWNERS, 1, PAYLOAD), whole(LEVELS, QROWS), whole(LEVELS, QROWS),
             whole(1, 128), rows_of(BLOCK, 1024),
-            rows_of(BLOCK, INNER), rows_of(BLOCK, 256), rows_of(BLOCK, HEADS),
+            rows_of(BLOCK, INNER), rows_of(BLOCK, 256), rows_of(BLOCK, 128),
         ],
         out_shape=[
             shape(OWNERS, 1, PAYLOAD), shape(LEVELS, QROWS, dtype=jnp.int32),
             shape(LEVELS, QROWS, dtype=jnp.int32), shape(1, 128),
             shape(FRAMES, 1024, dtype=bf16), shape(FRAMES, INNER, dtype=bf16),
-            shape(FRAMES, 256, dtype=bf16), shape(FRAMES, HEADS),
+            shape(FRAMES, 256, dtype=bf16), shape(FRAMES, 128),
         ],
         scratch_shapes=[pltpu.VMEM((DIM, INNER), f32), pltpu.VMEM((8, 128), f32)],
         compiler_params=settings(62),
@@ -526,14 +570,14 @@
         grid=(STEPS,),
         in_specs=[
             rows_of(BLOCK, 1024), rows_of(BLOCK, 1024), rows_of(BLOCK, INNER),
-            rows_of(BLOCK, 256), rows_of(BLOCK, HEADS), whole(1024, INNER),
+            rows_of(BLOCK, 256), rows_of(BLOCK, 128), whole(1024, INNER),
         ],
         out_specs=[
-            rows_of(BLOCK, INNER), rows_of(BLOCK, INNER), rows_of(BLOCK, HEADS),
+            rows_of(BLOCK, INNER), rows_of(BLOCK, INNER), rows_of(BLOCK, 128),
             pl.BlockSpec((4, BLOCK // 4, WIDTH), lambda i: (0, i, 0)),
         ],
         out_shape=[
-            shape(FRAMES, INNER), shape(FRAMES, INNER), shape(FRAMES, HEADS),
+            shape(FRAMES, INNER), shape(FRAMES, INNER), shape(FRAMES, 128),
             shape(4, QROWS, WIDTH),
         ],
         scratch_shapes=[pltpu.VMEM((DIM, INNER), f32), pltpu.VMEM((8, 128), f32)],

time: 142 us -> 139 us (0.979); the launches traced: 139 us -> 138 us
  waiting for transfers between devices: 56.1 us -> 53.5 us
    all_to_all x4, waiting for transfers between devices: 53.7 us -> 50.8 us  [exchange(): return lax.all_to_all(array, SEQ, split_axis=0, concat_axis=0, tiled=True)]
    add x1 -> x0, other arithmetic: 2.3 us -> none  [with_few_slots(): found = found + jnp.pad(late, ((0, 0), (2 * (FEW - LATE), 0), (0, 0)))]
    pallas_call x1 -> x3, Pallas kernels: 4.52 us -> 6.59 us  [the longest x1 3.79 us: gathered_table(): pl.pallas_call(table_kernel, grid=(3,), in_specs=[whole(*codes.shape)] +...]
    convert_element_type x2, other arithmetic: 0.27 us -> 1.79 us  [asked_codes(): arrived[:, 0, ASKED + low:ASKED + high].astype(jnp.int32).reshape(1, -1)]
  transfers between devices with their start and end apart: 9 -> 9, of which waited for: 6 -> 6; matrix products, arithmetic and copies ran while one was open for 0% -> 1% of each run, Pallas kernels for 19% -> 19%
where the time goes in v5:
time: 139 us; the launch traced here: 138 us
  waiting for transfers between devices  53.5 us (38%)
  Pallas kernels  43.2 us (31%)
  starting transfers between devices  37.5 us (27%)
  other arithmetic  1.79 us (1%)
    all_to_all x4, waiting for transfers between devices, exchange(): return lax.all_to_all(array, SEQ, split_axis=0, concat_axis=0, tiled=True)  50.8 us
    all_to_all x4, starting transfers between devices, exchange(): return lax.all_to_all(array, SEQ, split_axis=0, concat_axis=0, tiled=True)  31 us
    pallas_call x1, Pallas kernels, body(): pl.pallas_call(local_kernel, grid=(STEPS,), in_specs=[rows_of(BLOCK, 1024...  9.17 us
    pallas_call x1, Pallas kernels, body(): pl.pallas_call(front_kernel, grid=(STEPS,), in_specs=[rows_of(BLOCK, 1024...  8.84 us
    pallas_call x1, Pallas kernels, shared_out(): pl.pallas_call(outer_kernel, grid_spec=pltpu.PrefetchScalarGridSpec(num_s...  8.63 us
    pallas_call x1, Pallas kernels, looked_up(): pl.pallas_call(functools.partial(lookup_kernel, cuts), grid=(LEVELS,), in...  5.8 us
    ppermute x3, starting transfers between devices, shared_out(): lax.ppermute(shares[d], 'book', [(i, (i + d) % 4) for i in range(4)])  4.79 us
    pallas_call x1, Pallas kernels, gathered_table(): pl.pallas_call(table_kernel, grid=(3,), in_specs=[whole(*codes.shape)] +...  3.79 us
  transfers between devices with their start and end apart: 9, of which 6 were waited for; matrix products, arithmetic and copies ran while one was open for 1% of the time, Pallas kernels for 19%

profile of v5, /device:TPU:1, one launch (start us, length us, event | category | flops | bytes accessed | tf_op | source)
XLA Modules:
  0.0 138.3 jit_solution(12087967055064635836)
XLA Ops:
  0.6 8.8 %front.1 = (f32[64,1,1152]{2,1,0:T(1,128)}, s32[3,256]{1,0:T(4,128)S(1)}, s32[3,256]{1,0:T(4,128)S(1)}, f32[1,128]{1,0:T(1,128)}, bf16[1024,1024]{1,0:T(8,128)(2...) custom-call(bf16[1024,1024]{1,0:T(8,128)(2,1)} %frames_ref.3, ...), custom_call_target="tpu_custom_call" | custom-call | tf_op jit(solution)/shard_map/front/pallas_call | solution.py:542
  9.5 13.2 %all-to-all-start.6 = ((f32[64,1,1152]{2,1,0:T(1,128)}), f32[64,1,1152]{2,1,0:T(1,128)S(1)}, u32[]{:S(2)}, u32[]{:S(2)}) async-start(f32[64,1,1152]{2,1,0:T(1,128)} %get-tuple-element.122), calls=%async_computation.6 | async-start | bytes 589824 | tf_op jit(solution)/shard_map/all_to_all | solution.py:371
  23.3 9.2 %local.1 = (f32[1024,512]{1,0:T(8,128)}, f32[1024,512]{1,0:T(8,128)}, f32[1024,128]{1,0:T(8,128)}, f32[4,256,256]{2,1,0:T(8,128)}) custom-call(bf16[1024,1024]{1,0:T(8,128)(2,1)} %frames_ref.3, bf16[1024,1024]{1,0:T(8,128)(2,1)} %get-tuple-element.123.normed_ref, bf16[1024,512]{1,0:T(8,128)(2,1)} %get-tuple-element.124.inflow_ref, ...), custom_call_target="tpu_custom_call" | custom-call | flops 4000000000 | bytes 12582912 | tf_op jit(solution)/shard_map/local/pallas_call | solution.py:568
  32.5 3.9 %all-to-all-done.6 = f32[64,1,1152]{2,1,0:T(1,128)S(1)} async-done(((f32[64,1,1152]{2,1,0:T(1,128)}), f32[64,1,1152]{2,1,0:T(1,128)S(1)}, u32[]{:S(2)}, u32[]{:S(2)}) %all-to-all-start.6) | async-done | bytes 294944 | tf_op jit(solution)/shard_map/all_to_all | solution.py:371
  36.4 101.9 %conditional.1 = (f32[256,256]{1,0:T(8,128)}, f32[3,1024,256]{2,1,0:T(8,128)}) conditional(s32[]{:T(128)} %bitcast.20, (f32[64,1,1152]{2,1,0:T(1,128)S(1)}, f32[512]{0:T(512)S(1)}, s32[1]{0:T(128)}, f32[1024,512]{1,0:T(8,128)}, f32[1024,512]{1,0:T(8,128)}, /*index=5*/f32[1024,128]{1,0:T(8,128)}, bf16[1024,256]{1,0:T(8,128)(2,1)S(1)}, ...), branch_computations={%region_0.0_spmd, %region_1.0_spmd} | conditional | flops 10000002048 | bytes 43416060 | solution.py:589
  36.4 1.0 scan.3
  37.4 6.7 %all-to-all-start.3 = ((f32[64,8,128]{2,1,0:T(8,128)}), f32[64,8,128]{2,1,0:T(8,128)S(1)}, u32[]{:S(2)}, u32[]{:S(2)}) async-start(f32[64,8,128]{2,1,0:T(8,128)} %scan.3), calls=%async_computation.3 | async-start | bytes 524288 | tf_op jit(solution)/shard_map/cond/branch_1_fun/all_to_all | solution.py:371
  44.0 5.8 %lookup.3 = (f32[2048,128]{1,0:T(8,128)}, f32[512,128]{1,0:T(8,128)}) custom-call(f32[64,1,1152]{2,1,0:T(1,128)S(1)} %get-tuple-element.102.arrived_ref, f32[3,1024,256]{2,1,0:T(8,128)} %get-tuple-element.79.table_ref), custom_call_target="tpu_custom_call" | custom-call | flops 4000000000 | bytes 5242880 | tf_op jit(solution)/shard_map/cond/branch_1_fun/lookup/pallas_call | solution.py:375
  49.8 7.4 %all-to-all-done.3 = f32[64,8,128]{2,1,0:T(8,128)S(1)} async-done(((f32[64,8,128]{2,1,0:T(8,128)}), f32[64,8,128]{2,1,0:T(8,128)S(1)}, u32[]{:S(2)}, u32[]{:S(2)}) %all-to-all-start.3) | async-done | bytes 262176 | tf_op jit(solution)/shard_map/cond/branch_1_fun/all_to_all | solution.py:371
  57.4 1.5 %collective-permute-done.6 = f32[512,128]{1,0:T(8,128)S(1)} collective-permute-done((f32[512,128]{1,0:T(8,128)}, f32[512,128]{1,0:T(8,128)S(1)}, u32[]{:S(2)}, u32[]{:S(2)}) %collective-permute-start.6) | collective-permute-done | bytes 262176 | tf_op jit(solution)/shard_map/cond/branch_1_fun/ppermute | solution.py:490
  59.6 1.8 %relayed.1 = f32[64,32,128]{2,1,0:T(8,128)} custom-call(f32[64,32,128]{2,1,0:T(8,128)} %bitcast.28, f32[64,8,128]{2,1,0:T(8,128)} %bitcast.32), custom_call_target="tpu_custom_call", output_to_operand_aliasing={{}: (0, {})} | custom-call | tf_op jit(solution)/shard_map/cond/branch_1_fun/relayed/pallas_call | solution.py:516
  61.5 4.7 %all-to-all-start.4 = ((f32[64,32,128]{2,1,0:T(8,128)}), f32[64,32,128]{2,1,0:T(8,128)S(1)}, u32[]{:S(2)}, u32[]{:S(2)}) async-start(f32[64,32,128]{2,1,0:T(8,128)} %relayed.1), calls=%async_computation.4 | async-start | bytes 2097152 | tf_op jit(solution)/shard_map/cond/branch_1_fun/all_to_all | solution.py:371
  66.2 8.6 %outer.3 = (f32[256,256]{1,0:T(8,128)}, f32[256,256]{1,0:T(8,128)}, f32[256,256]{1,0:T(8,128)}, f32[256,256]{1,0:T(8,128)}) custom-call(s32[1]{0:T(128)} %get-tuple-element.72.book_ref, f32[1024,512]{1,0:T(8,128)} %get-tuple-element.73.inner_ref, f32[1024,512]{1,0:T(8,128)} %get-tuple-element.74.gate_ref, f32[1024,128]{1,0:T(8,128)} %get-tuple-element.75.reach_ref, ...), custom_call_target="tpu_custom_call" | custom-call | flops 2000000000 | bytes 8388608 | tf_op jit(solution)/shard_map/cond/branch_1_fun/outer/pallas_call | solution.py:405
  74.8 1.2 collective-permute-start.3
  76.1 2.4 %collective-permute-start.4 = (f32[256,256]{1,0:T(8,128)}, f32[256,256]{1,0:T(8,128)S(1)}, u32[]{:S(2)}, u32[]{:S(2)}) collective-permute-start(f32[256,256]{1,0:T(8,128)} %get-tuple-element.89), channel_id=1, source_target_pairs={{0,2},{1,3},{2,0},{3,1},{4,6},{5,7},{6,4},{7,5},{8,10},{9,11},{10,... | collective-permute-start | bytes 786440 | tf_op jit(solution)/shard_map/cond/branch_1_fun/ppermute | solution.py:424
  78.5 1.1 collective-permute-start.5
  80.6 13.6 %all-to-all-done.4 = f32[64,32,128]{2,1,0:T(8,128)S(1)} async-done(((f32[64,32,128]{2,1,0:T(8,128)}), f32[64,32,128]{2,1,0:T(8,128)S(1)}, u32[]{:S(2)}, u32[]{:S(2)}) %all-to-all-start.4) | async-done | bytes 1048608 | tf_op jit(solution)/shard_map/cond/branch_1_fun/all_to_all | solution.py:371
  94.2 1.7 %taken.3 = (f32[1024,256]{1,0:T(8,128)S(1)}, f32[256,256]{1,0:T(8,128)S(1)}) custom-call(f32[2048,128]{1,0:T(8,128)S(1)} %bitcast.27, s32[256,128]{1,0:T(8,128)S(1)} %get-tuple-element.95.columns_ref, bf16[1024,768]{1,0:T(8,128)(2,1)S(1)} %get-tuple-element.96.spreads_ref.spread_ref), custom_call_target="tpu_custom_call" | custom-call | flops 3000000000 | bytes 3145728 | tf_op jit(solution)/shard_map/cond/branch_1_fun/taken/pallas_call | solution.py:442
  95.9 1.5 %residual.3 = (f32[256,256]{1,0:T(8,128)}, f32[2048,128]{1,0:T(8,128)}) custom-call(s32[1]{0:T(128)} %get-tuple-element.72.book_ref, f32[256,256]{1,0:T(8,128)S(1)} %copy-done.1, f32[256,256]{1,0:T(8,128)S(1)} %collective-permute-done.3.from_1, f32[256,256]{1,0:T(8,128)S(1)} %collective-permute-done.4.from_2, f32[256,256]{1,0:T(8,128)S(1)} %collective-permute-done.5.from_3, ...), custom_call_target="tpu_custom_call" | custom-call | tf_op jit(solution)/shard_map/cond/branch_1_fun/residual/pallas_call | solution.py:449
  97.4 6.5 %all-to-all-start.5 = ((f32[64,32,128]{2,1,0:T(8,128)}), f32[64,32,128]{2,1,0:T(8,128)S(1)}, u32[]{:S(2)}, u32[]{:S(2)}) async-start(f32[64,32,128]{2,1,0:T(8,128)} %bitcast.12), calls=%async_computation.5 | async-start | bytes 2097152 | tf_op jit(solution)/shard_map/cond/branch_1_fun/all_to_all | solution.py:371
  105.8 26.0 %all-to-all-done.5 = f32[64,32,128]{2,1,0:T(8,128)S(1)} async-done(((f32[64,32,128]{2,1,0:T(8,128)}), f32[64,32,128]{2,1,0:T(8,128)S(1)}, u32[]{:S(2)}, u32[]{:S(2)}) %all-to-all-start.5) | async-done | bytes 1048608 | tf_op jit(solution)/shard_map/cond/branch_1_fun/all_to_all | solution.py:371
  131.9 1.4 %collective-permute-start.7 = (f32[512,128]{1,0:T(8,128)S(1)}, f32[512,128]{1,0:T(8,128)S(1)}, u32[]{:S(2)}, u32[]{:S(2)}) collective-permute-start(f32[512,128]{1,0:T(8,128)S(1)} %slice_bitcast_fusion), channel_id=1, source_target_pairs={{0,4},{4,0},{1,5},{5,1},{2,6},{6,2},{3,7},{7,3},{8,12},{12,8},{9,1... | collective-permute-start | bytes 786440 | tf_op jit(solution)/shard_map/cond/branch_1_fun/ppermute | solution.py:490
  133.3 1.2 collective-permute-done.7.refs_1_
  134.5 3.8 %table.3 = f32[3072,256]{1,0:T(8,128)} custom-call(s32[1,1280]{1,0:T(1,128)S(1)} %pad_add_fusion.codes_ref, f32[2048,128]{1,0:T(8,128)S(1)} %bitcast.24, f32[512,128]{1,0:T(8,128)S(1)} %collective-permute-done.7.refs_1_), custom_call_target="tpu_custom_call" | custom-call | tf_op jit(solution)/shard_map/cond/branch_1_fun/table/pallas_call | solution.py:470
  (27 shorter events, 4.0 us)
Async XLA Ops:
  9.5 26.9 %all-to-all-start.6 = ((f32[64,1,1152]{2,1,0:T(1,128)}), f32[64,1,1152]{2,1,0:T(1,128)S(1)}, u32[]{:S(2)}, u32[]{:S(2)}) async-start(f32[64,1,1152]{2,1,0:T(1,128)} %get-tuple-element.122), calls=%async_computation.6 | async-start | bytes 589824 | tf_op jit(solution)/shard_map/all_to_all | solution.py:371
  23.3 13.1 %copy-start.14 = (f32[512]{0:T(512)S(1)}, f32[512]{0:T(512)}, u32[]{:S(2)}) copy-start(f32[512]{0:T(512)} %param.22) | copy-start | bytes 6148
  36.4 13.5 %copy-start.7 = (f32[64,1,1152]{2,1,0:T(1,128)}, f32[64,1,1152]{2,1,0:T(1,128)S(1)}, u32[]{:S(2)}) copy-start(f32[64,1,1152]{2,1,0:T(1,128)S(1)} %get-tuple-element.102.arrived_ref) | copy-start | bytes 884740 | tf_op jit(solution)/shard_map/cond
  36.4 13.5 %copy-start.12 = (bf16[1024,256]{1,0:T(8,128)(2,1)}, bf16[1024,256]{1,0:T(8,128)(2,1)S(1)}, u32[]{:S(2)}) copy-start(bf16[1024,256]{1,0:T(8,128)(2,1)S(1)} %get-tuple-element.76.c_ref) | copy-start | bytes 1572868 | tf_op jit(solution)/shard_map/cond
  37.4 19.8 %all-to-all-start.3 = ((f32[64,8,128]{2,1,0:T(8,128)}), f32[64,8,128]{2,1,0:T(8,128)S(1)}, u32[]{:S(2)}, u32[]{:S(2)}) async-start(f32[64,8,128]{2,1,0:T(8,128)} %scan.3), calls=%async_computation.3 | async-start | bytes 524288 | tf_op jit(solution)/shard_map/cond/branch_1_fun/all_to_all | solution.py:371
  57.2 9.0 %copy-start.9 = (f32[64,8,128]{2,1,0:T(8,128)}, f32[64,8,128]{2,1,0:T(8,128)S(1)}, u32[]{:S(2)}) copy-start(f32[64,8,128]{2,1,0:T(8,128)S(1)} %all-to-all-done.3) | copy-start | bytes 786436 | tf_op jit(solution)/shard_map/cond
  57.2 1.7 %collective-permute-start.6 = (f32[512,128]{1,0:T(8,128)}, f32[512,128]{1,0:T(8,128)S(1)}, u32[]{:S(2)}, u32[]{:S(2)}) collective-permute-start(f32[512,128]{1,0:T(8,128)} %get-tuple-element.93), channel_id=1, source_target_pairs={{0,4},{4,0},{1,5},{5,1},{2,6},{6,2},{3,7},{7,3},{8,12},{12,8},{9,1... | collective-permute-start | bytes 786440 | tf_op jit(solution)/shard_map/cond/branch_1_fun/ppermute | solution.py:490
  58.9 0.7 copy-start.8
  59.6 6.6 %copy-start.13 = (bf16[1024,256]{1,0:T(8,128)(2,1)S(1)}, bf16[1024,256]{1,0:T(8,128)(2,1)}, u32[]{:S(2)}) copy-start(bf16[1024,256]{1,0:T(8,128)(2,1)} %copy-done.12) | copy-start | bytes 1572868 | tf_op jit(solution)/shard_map/cond
  61.5 32.7 %all-to-all-start.4 = ((f32[64,32,128]{2,1,0:T(8,128)}), f32[64,32,128]{2,1,0:T(8,128)S(1)}, u32[]{:S(2)}, u32[]{:S(2)}) async-start(f32[64,32,128]{2,1,0:T(8,128)} %relayed.1), calls=%async_computation.4 | async-start | bytes 2097152 | tf_op jit(solution)/shard_map/cond/branch_1_fun/all_to_all | solution.py:371
  74.8 21.0 %collective-permute-start.3 = (f32[256,256]{1,0:T(8,128)}, f32[256,256]{1,0:T(8,128)S(1)}, u32[]{:S(2)}, u32[]{:S(2)}) collective-permute-start(f32[256,256]{1,0:T(8,128)} %get-tuple-element.88), channel_id=1, source_target_pairs={{0,1},{1,2},{2,3},{3,0},{4,5},{5,6},{6,7},{7,4},{8,9},{9,10},{10,1... | collective-permute-start | bytes 786440 | tf_op jit(solution)/shard_map/cond/branch_1_fun/ppermute | solution.py:424
  76.1 19.8 %collective-permute-start.4 = (f32[256,256]{1,0:T(8,128)}, f32[256,256]{1,0:T(8,128)S(1)}, u32[]{:S(2)}, u32[]{:S(2)}) collective-permute-start(f32[256,256]{1,0:T(8,128)} %get-tuple-element.89), channel_id=1, source_target_pairs={{0,2},{1,3},{2,0},{3,1},{4,6},{5,7},{6,4},{7,5},{8,10},{9,11},{10,... | collective-permute-start | bytes 786440 | tf_op jit(solution)/shard_map/cond/branch_1_fun/ppermute | solution.py:424
  78.5 17.4 %collective-permute-start.5 = (f32[256,256]{1,0:T(8,128)}, f32[256,256]{1,0:T(8,128)S(1)}, u32[]{:S(2)}, u32[]{:S(2)}) collective-permute-start(f32[256,256]{1,0:T(8,128)} %get-tuple-element.90), channel_id=1, source_target_pairs={{0,3},{1,0},{2,1},{3,2},{4,7},{5,4},{6,5},{7,6},{8,11},{9,8},{10,9... | collective-permute-start | bytes 786440 | tf_op jit(solution)/shard_map/cond/branch_1_fun/ppermute | solution.py:424
  94.2 1.7 %copy-start.1 = (f32[256,256]{1,0:T(8,128)S(1)}, f32[256,256]{1,0:T(8,128)}, u32[]{:S(2)}) copy-start(f32[256,256]{1,0:T(8,128)} %get-tuple-element.87.own_ref) | copy-start | bytes 786436 | tf_op jit(solution)/shard_map/cond
  94.2 1.7 %copy-start.5 = (f32[4,256,256]{2,1,0:T(8,128)S(1)}, f32[4,256,256]{2,1,0:T(8,128)}, u32[]{:S(2)}) copy-start(f32[4,256,256]{2,1,0:T(8,128)} %get-tuple-element.91.means_ref) | copy-start | bytes 3145732 | tf_op jit(solution)/shard_map/cond
  97.4 34.5 %all-to-all-start.5 = ((f32[64,32,128]{2,1,0:T(8,128)}), f32[64,32,128]{2,1,0:T(8,128)S(1)}, u32[]{:S(2)}, u32[]{:S(2)}) async-start(f32[64,32,128]{2,1,0:T(8,128)} %bitcast.12), calls=%async_computation.5 | async-start | bytes 2097152 | tf_op jit(solution)/shard_map/cond/branch_1_fun/all_to_all | solution.py:371
  131.9 2.6 %collective-permute-start.7 = (f32[512,128]{1,0:T(8,128)S(1)}, f32[512,128]{1,0:T(8,128)S(1)}, u32[]{:S(2)}, u32[]{:S(2)}) collective-permute-start(f32[512,128]{1,0:T(8,128)S(1)} %slice_bitcast_fusion), channel_id=1, source_target_pairs={{0,4},{4,0},{1,5},{5,1},{2,6},{6,2},{3,7},{7,3},{8,12},{12,8},{9,1... | collective-permute-start | bytes 786440 | tf_op jit(solution)/shard_map/cond/branch_1_fun/ppermute | solution.py:490

commit v6 on v5

--- a/solution.py
+++ b/solution.py
@@ -509,7 +509,6 @@
 ):
     incoming, arrived = scanned(arrived)
     found, late = looked_up(arrived, codebook, [(0, FEW), (FEW, SLOTS)])
-    late, incoming = lax.optimization_barrier((late, incoming))
     late = other_core(late).reshape(OWNERS, 2 * LATE, 128)
     found = found.reshape(OWNERS, 2 * FEW, 128)
     last = pl.BlockSpec((OWNERS, 2 * LATE, 128), lambda i: (0, FEW // LATE - 1, 0))
@@ -521,6 +520,7 @@
         out_shape=shape(OWNERS, 2 * FEW, 128),
         input_output_aliases={0: 0},
         compiler_params=settings(57),
+        cost_estimate=pl.CostEstimate(flops=0, bytes_accessed=0, transcendentals=0),
         name="relayed",
     )(found, late)
     shares = shared_out(book, incoming, inner, gate, reach, bc_act, out_gain, out_weight)

time: 139 us -> 137 us (0.986)
  waiting for transfers between devices: 53.5 us -> 48.9 us
  starting transfers between devices: 37.5 us -> 40.3 us
    all_to_all x4, waiting for transfers between devices: 50.8 us -> 46.4 us  [exchange(): return lax.all_to_all(array, SEQ, split_axis=0, concat_axis=0, tiled=True)]
    all_to_all x4, starting transfers between devices: 31 us -> 33.5 us  [exchange(): return lax.all_to_all(array, SEQ, split_axis=0, concat_axis=0, tiled=True)]
  transfers between devices with their start and end apart: 9 -> 9, of which waited for: 6 -> 6; matrix products, arithmetic and copies ran while one was open for 1% -> 1% of each run, Pallas kernels for 19% -> 21%
where the time goes in v6:
time: 137 us
  waiting for transfers between devices  48.9 us (36%)
  Pallas kernels  43.2 us (32%)
  starting transfers between devices  40.3 us (29%)
  other arithmetic  1.79 us (1%)
    all_to_all x4, waiting for transfers between devices, exchange(): return lax.all_to_all(array, SEQ, split_axis=0, concat_axis=0, tiled=True)  46.4 us
    all_to_all x4, starting transfers between devices, exchange(): return lax.all_to_all(array, SEQ, split_axis=0, concat_axis=0, tiled=True)  33.5 us
    pallas_call x1, Pallas kernels, body(): pl.pallas_call(local_kernel, grid=(STEPS,), in_specs=[rows_of(BLOCK, 1024...  9.17 us
    pallas_call x1, Pallas kernels, body(): pl.pallas_call(front_kernel, grid=(STEPS,), in_specs=[rows_of(BLOCK, 1024...  8.84 us
    pallas_call x1, Pallas kernels, shared_out(): pl.pallas_call(outer_kernel, grid_spec=pltpu.PrefetchScalarGridSpec(num_s...  8.63 us
    pallas_call x1, Pallas kernels, looked_up(): pl.pallas_call(functools.partial(lookup_kernel, cuts), grid=(LEVELS,), in...  5.8 us
    ppermute x3, starting transfers between devices, shared_out(): lax.ppermute(shares[d], 'book', [(i, (i + d) % 4) for i in range(4)])  4.79 us
    pallas_call x1, Pallas kernels, gathered_table(): pl.pallas_call(table_kernel, grid=(3,), in_specs=[whole(*codes.shape)] +...  3.79 us
  transfers between devices with their start and end apart: 9, of which 6 were waited for; matrix products, arithmetic and copies ran while one was open for 1% of the time, Pallas kernels for 21%

profile of v6, /device:TPU:1, one launch (start us, length us, event | category | flops | bytes accessed | tf_op | source)
XLA Modules:
  0.0 136.5 jit_solution(15138123623134331375)
XLA Ops:
  0.6 8.8 %front.1 = (f32[64,1,1152]{2,1,0:T(1,128)}, s32[3,256]{1,0:T(4,128)S(1)}, s32[3,256]{1,0:T(4,128)S(1)}, f32[1,128]{1,0:T(1,128)}, bf16[1024,1024]{1,0:T(8,128)(2...) custom-call(bf16[1024,1024]{1,0:T(8,128)(2,1)} %frames_ref.3, ...), custom_call_target="tpu_custom_call" | custom-call | tf_op jit(solution)/shard_map/front/pallas_call | solution.py:542
  9.5 13.2 %all-to-all-start.6 = ((f32[64,1,1152]{2,1,0:T(1,128)}), f32[64,1,1152]{2,1,0:T(1,128)S(1)}, u32[]{:S(2)}, u32[]{:S(2)}) async-start(f32[64,1,1152]{2,1,0:T(1,128)} %get-tuple-element.120), calls=%async_computation.6 | async-start | bytes 589824 | tf_op jit(solution)/shard_map/all_to_all | solution.py:371
  23.3 9.2 %local.1 = (f32[1024,512]{1,0:T(8,128)}, f32[1024,512]{1,0:T(8,128)}, f32[1024,128]{1,0:T(8,128)}, f32[4,256,256]{2,1,0:T(8,128)}) custom-call(bf16[1024,1024]{1,0:T(8,128)(2,1)} %frames_ref.3, bf16[1024,1024]{1,0:T(8,128)(2,1)} %get-tuple-element.121.normed_ref, bf16[1024,512]{1,0:T(8,128)(2,1)} %get-tuple-element.122.inflow_ref, ...), custom_call_target="tpu_custom_call" | custom-call | flops 4000000000 | bytes 12582912 | tf_op jit(solution)/shard_map/local/pallas_call | solution.py:568
  32.5 3.9 %all-to-all-done.6 = f32[64,1,1152]{2,1,0:T(1,128)S(1)} async-done(((f32[64,1,1152]{2,1,0:T(1,128)}), f32[64,1,1152]{2,1,0:T(1,128)S(1)}, u32[]{:S(2)}, u32[]{:S(2)}) %all-to-all-start.6) | async-done | bytes 294944 | tf_op jit(solution)/shard_map/all_to_all | solution.py:371
  36.4 100.2 %conditional.1 = (f32[256,256]{1,0:T(8,128)}, f32[3,1024,256]{2,1,0:T(8,128)}) conditional(s32[]{:T(128)} %bitcast.20, (f32[64,1,1152]{2,1,0:T(1,128)S(1)}, f32[512]{0:T(512)S(1)}, s32[1]{0:T(128)}, f32[1024,512]{1,0:T(8,128)}, f32[1024,512]{1,0:T(8,128)}, /*index=5*/f32[1024,128]{1,0:T(8,128)}, bf16[1024,256]{1,0:T(8,128)(2,1)S(1)}, ...), branch_computations={%region_0.0_spmd, %region_1.0_spmd} | conditional | flops 10000002048 | bytes 43416060 | solution.py:589
  36.4 1.0 scan.3
  37.4 6.7 %all-to-all-start.3 = ((f32[64,8,128]{2,1,0:T(8,128)}), f32[64,8,128]{2,1,0:T(8,128)S(1)}, u32[]{:S(2)}, u32[]{:S(2)}) async-start(f32[64,8,128]{2,1,0:T(8,128)} %scan.3), calls=%async_computation.3 | async-start | bytes 524288 | tf_op jit(solution)/shard_map/cond/branch_1_fun/all_to_all | solution.py:371
  44.0 5.8 %lookup.3 = (f32[2048,128]{1,0:T(8,128)}, f32[512,128]{1,0:T(8,128)}) custom-call(f32[64,1,1152]{2,1,0:T(1,128)S(1)} %get-tuple-element.100.arrived_ref, f32[3,1024,256]{2,1,0:T(8,128)} %get-tuple-element.89.table_ref), custom_call_target="tpu_custom_call" | custom-call | flops 4000000000 | bytes 5242880 | tf_op jit(solution)/shard_map/cond/branch_1_fun/lookup/pallas_call | solution.py:375
  50.3 1.4 %collective-permute-done.6 = f32[512,128]{1,0:T(8,128)S(1)} collective-permute-done((f32[512,128]{1,0:T(8,128)}, f32[512,128]{1,0:T(8,128)S(1)}, u32[]{:S(2)}, u32[]{:S(2)}) %collective-permute-start.6) | collective-permute-done | bytes 262176 | tf_op jit(solution)/shard_map/cond/branch_1_fun/ppermute | solution.py:490
  52.4 1.8 %relayed.1 = f32[64,32,128]{2,1,0:T(8,128)} custom-call(f32[64,32,128]{2,1,0:T(8,128)} %bitcast.28, f32[64,8,128]{2,1,0:T(8,128)} %bitcast.32), custom_call_target="tpu_custom_call", output_to_operand_aliasing={{}: (0, {})} | custom-call | tf_op jit(solution)/shard_map/cond/branch_1_fun/relayed/pallas_call | solution.py:515
  54.2 3.0 %all-to-all-done.3 = f32[64,8,128]{2,1,0:T(8,128)S(1)} async-done(((f32[64,8,128]{2,1,0:T(8,128)}), f32[64,8,128]{2,1,0:T(8,128)S(1)}, u32[]{:S(2)}, u32[]{:S(2)}) %all-to-all-start.3) | async-done | bytes 262176 | tf_op jit(solution)/shard_map/cond/branch_1_fun/all_to_all | solution.py:371
  57.2 7.3 %all-to-all-start.4 = ((f32[64,32,128]{2,1,0:T(8,128)}), f32[64,32,128]{2,1,0:T(8,128)S(1)}, u32[]{:S(2)}, u32[]{:S(2)}) async-start(f32[64,32,128]{2,1,0:T(8,128)} %relayed.1), calls=%async_computation.4 | async-start | bytes 2097152 | tf_op jit(solution)/shard_map/cond/branch_1_fun/all_to_all | solution.py:371
  64.5 8.6 %outer.3 = (f32[256,256]{1,0:T(8,128)}, f32[256,256]{1,0:T(8,128)}, f32[256,256]{1,0:T(8,128)}, f32[256,256]{1,0:T(8,128)}) custom-call(s32[1]{0:T(128)} %get-tuple-element.72.book_ref, f32[1024,512]{1,0:T(8,128)} %get-tuple-element.73.inner_ref, f32[1024,512]{1,0:T(8,128)} %get-tuple-element.74.gate_ref, f32[1024,128]{1,0:T(8,128)} %get-tuple-element.75.reach_ref, ...), custom_call_target="tpu_custom_call" | custom-call | flops 2000000000 | bytes 8388608 | tf_op jit(solution)/shard_map/cond/branch_1_fun/outer/pallas_call | solution.py:405
  73.1 1.2 collective-permute-start.3
  74.3 2.4 %collective-permute-start.4 = (f32[256,256]{1,0:T(8,128)}, f32[256,256]{1,0:T(8,128)S(1)}, u32[]{:S(2)}, u32[]{:S(2)}) collective-permute-start(f32[256,256]{1,0:T(8,128)} %get-tuple-element.85), channel_id=1, source_target_pairs={{0,2},{1,3},{2,0},{3,1},{4,6},{5,7},{6,4},{7,5},{8,10},{9,11},{10,... | collective-permute-start | bytes 786440 | tf_op jit(solution)/shard_map/cond/branch_1_fun/ppermute | solution.py:424
  76.8 1.1 collective-permute-start.5
  78.9 13.6 %all-to-all-done.4 = f32[64,32,128]{2,1,0:T(8,128)S(1)} async-done(((f32[64,32,128]{2,1,0:T(8,128)}), f32[64,32,128]{2,1,0:T(8,128)S(1)}, u32[]{:S(2)}, u32[]{:S(2)}) %all-to-all-start.4) | async-done | bytes 1048608 | tf_op jit(solution)/shard_map/cond/branch_1_fun/all_to_all | solution.py:371
  92.4 1.7 %taken.3 = (f32[1024,256]{1,0:T(8,128)S(1)}, f32[256,256]{1,0:T(8,128)S(1)}) custom-call(f32[2048,128]{1,0:T(8,128)S(1)} %bitcast.27, s32[256,128]{1,0:T(8,128)S(1)} %get-tuple-element.93.columns_ref, bf16[1024,768]{1,0:T(8,128)(2,1)S(1)} %get-tuple-element.94.spreads_ref.spread_ref), custom_call_target="tpu_custom_call" | custom-call | flops 3000000000 | bytes 3145728 | tf_op jit(solution)/shard_map/cond/branch_1_fun/taken/pallas_call | solution.py:442
  94.2 1.5 %residual.3 = (f32[256,256]{1,0:T(8,128)}, f32[2048,128]{1,0:T(8,128)}) custom-call(s32[1]{0:T(128)} %get-tuple-element.72.book_ref, f32[256,256]{1,0:T(8,128)S(1)} %copy-done.1, f32[256,256]{1,0:T(8,128)S(1)} %collective-permute-done.3.from_1, f32[256,256]{1,0:T(8,128)S(1)} %collective-permute-done.4.from_2, f32[256,256]{1,0:T(8,128)S(1)} %collective-permute-done.5.from_3, ...), custom_call_target="tpu_custom_call" | custom-call | tf_op jit(solution)/shard_map/cond/branch_1_fun/residual/pallas_call | solution.py:449
  95.6 6.5 %all-to-all-start.5 = ((f32[64,32,128]{2,1,0:T(8,128)}), f32[64,32,128]{2,1,0:T(8,128)S(1)}, u32[]{:S(2)}, u32[]{:S(2)}) async-start(f32[64,32,128]{2,1,0:T(8,128)} %bitcast.12), calls=%async_computation.5 | async-start | bytes 2097152 | tf_op jit(solution)/shard_map/cond/branch_1_fun/all_to_all | solution.py:371
  104.1 26.0 %all-to-all-done.5 = f32[64,32,128]{2,1,0:T(8,128)S(1)} async-done(((f32[64,32,128]{2,1,0:T(8,128)}), f32[64,32,128]{2,1,0:T(8,128)S(1)}, u32[]{:S(2)}, u32[]{:S(2)}) %all-to-all-start.5) | async-done | bytes 1048608 | tf_op jit(solution)/shard_map/cond/branch_1_fun/all_to_all | solution.py:371
  130.1 1.4 %collective-permute-start.7 = (f32[512,128]{1,0:T(8,128)S(1)}, f32[512,128]{1,0:T(8,128)S(1)}, u32[]{:S(2)}, u32[]{:S(2)}) collective-permute-start(f32[512,128]{1,0:T(8,128)S(1)} %slice_bitcast_fusion), channel_id=1, source_target_pairs={{0,4},{4,0},{1,5},{5,1},{2,6},{6,2},{3,7},{7,3},{8,12},{12,8},{9,1... | collective-permute-start | bytes 786440 | tf_op jit(solution)/shard_map/cond/branch_1_fun/ppermute | solution.py:490
  131.6 1.2 collective-permute-done.7.refs_1_
  132.7 3.8 %table.3 = f32[3072,256]{1,0:T(8,128)} custom-call(s32[1,1280]{1,0:T(1,128)S(1)} %pad_add_fusion.codes_ref, f32[2048,128]{1,0:T(8,128)S(1)} %bitcast.24, f32[512,128]{1,0:T(8,128)S(1)} %collective-permute-done.7.refs_1_), custom_call_target="tpu_custom_call" | custom-call | tf_op jit(solution)/shard_map/cond/branch_1_fun/table/pallas_call | solution.py:470
  (27 shorter events, 4.2 us)
Async XLA Ops:
  9.5 26.9 %all-to-all-start.6 = ((f32[64,1,1152]{2,1,0:T(1,128)}), f32[64,1,1152]{2,1,0:T(1,128)S(1)}, u32[]{:S(2)}, u32[]{:S(2)}) async-start(f32[64,1,1152]{2,1,0:T(1,128)} %get-tuple-element.120), calls=%async_computation.6 | async-start | bytes 589824 | tf_op jit(solution)/shard_map/all_to_all | solution.py:371
  23.3 13.1 %copy-start.14 = (f32[512]{0:T(512)S(1)}, f32[512]{0:T(512)}, u32[]{:S(2)}) copy-start(f32[512]{0:T(512)} %param.22) | copy-start | bytes 6148
  36.4 13.5 %copy-start.7 = (f32[64,1,1152]{2,1,0:T(1,128)}, f32[64,1,1152]{2,1,0:T(1,128)S(1)}, u32[]{:S(2)}) copy-start(f32[64,1,1152]{2,1,0:T(1,128)S(1)} %get-tuple-element.100.arrived_ref) | copy-start | bytes 884740 | tf_op jit(solution)/shard_map/cond
  36.4 13.5 %copy-start.12 = (bf16[1024,256]{1,0:T(8,128)(2,1)}, bf16[1024,256]{1,0:T(8,128)(2,1)S(1)}, u32[]{:S(2)}) copy-start(bf16[1024,256]{1,0:T(8,128)(2,1)S(1)} %get-tuple-element.76.c_ref) | copy-start | bytes 1572868 | tf_op jit(solution)/shard_map/cond
  37.4 19.8 %all-to-all-start.3 = ((f32[64,8,128]{2,1,0:T(8,128)}), f32[64,8,128]{2,1,0:T(8,128)S(1)}, u32[]{:S(2)}, u32[]{:S(2)}) async-start(f32[64,8,128]{2,1,0:T(8,128)} %scan.3), calls=%async_computation.3 | async-start | bytes 524288 | tf_op jit(solution)/shard_map/cond/branch_1_fun/all_to_all | solution.py:371
  49.8 1.9 %collective-permute-start.6 = (f32[512,128]{1,0:T(8,128)}, f32[512,128]{1,0:T(8,128)S(1)}, u32[]{:S(2)}, u32[]{:S(2)}) collective-permute-start(f32[512,128]{1,0:T(8,128)} %get-tuple-element.91), channel_id=1, source_target_pairs={{0,4},{4,0},{1,5},{5,1},{2,6},{6,2},{3,7},{7,3},{8,12},{12,8},{9,1... | collective-permute-start | bytes 786440 | tf_op jit(solution)/shard_map/cond/branch_1_fun/ppermute | solution.py:490
  51.7 0.7 copy-start.8
  52.4 12.1 %copy-start.13 = (bf16[1024,256]{1,0:T(8,128)(2,1)S(1)}, bf16[1024,256]{1,0:T(8,128)(2,1)}, u32[]{:S(2)}) copy-start(bf16[1024,256]{1,0:T(8,128)(2,1)} %copy-done.12) | copy-start | bytes 1572868 | tf_op jit(solution)/shard_map/cond
  57.2 7.3 %copy-start.9 = (f32[64,8,128]{2,1,0:T(8,128)}, f32[64,8,128]{2,1,0:T(8,128)S(1)}, u32[]{:S(2)}) copy-start(f32[64,8,128]{2,1,0:T(8,128)S(1)} %all-to-all-done.3) | copy-start | bytes 786436 | tf_op jit(solution)/shard_map/cond
  57.2 35.3 %all-to-all-start.4 = ((f32[64,32,128]{2,1,0:T(8,128)}), f32[64,32,128]{2,1,0:T(8,128)S(1)}, u32[]{:S(2)}, u32[]{:S(2)}) async-start(f32[64,32,128]{2,1,0:T(8,128)} %relayed.1), calls=%async_computation.4 | async-start | bytes 2097152 | tf_op jit(solution)/shard_map/cond/branch_1_fun/all_to_all | solution.py:371
  73.1 21.0 %collective-permute-start.3 = (f32[256,256]{1,0:T(8,128)}, f32[256,256]{1,0:T(8,128)S(1)}, u32[]{:S(2)}, u32[]{:S(2)}) collective-permute-start(f32[256,256]{1,0:T(8,128)} %get-tuple-element.84), channel_id=1, source_target_pairs={{0,1},{1,2},{2,3},{3,0},{4,5},{5,6},{6,7},{7,4},{8,9},{9,10},{10,1... | collective-permute-start | bytes 786440 | tf_op jit(solution)/shard_map/cond/branch_1_fun/ppermute | solution.py:424
  74.3 19.8 %collective-permute-start.4 = (f32[256,256]{1,0:T(8,128)}, f32[256,256]{1,0:T(8,128)S(1)}, u32[]{:S(2)}, u32[]{:S(2)}) collective-permute-start(f32[256,256]{1,0:T(8,128)} %get-tuple-element.85), channel_id=1, source_target_pairs={{0,2},{1,3},{2,0},{3,1},{4,6},{5,7},{6,4},{7,5},{8,10},{9,11},{10,... | collective-permute-start | bytes 786440 | tf_op jit(solution)/shard_map/cond/branch_1_fun/ppermute | solution.py:424
  76.8 17.4 %collective-permute-start.5 = (f32[256,256]{1,0:T(8,128)}, f32[256,256]{1,0:T(8,128)S(1)}, u32[]{:S(2)}, u32[]{:S(2)}) collective-permute-start(f32[256,256]{1,0:T(8,128)} %get-tuple-element.86), channel_id=1, source_target_pairs={{0,3},{1,0},{2,1},{3,2},{4,7},{5,4},{6,5},{7,6},{8,11},{9,8},{10,9... | collective-permute-start | bytes 786440 | tf_op jit(solution)/shard_map/cond/branch_1_fun/ppermute | solution.py:424
  92.4 1.7 %copy-start.1 = (f32[256,256]{1,0:T(8,128)S(1)}, f32[256,256]{1,0:T(8,128)}, u32[]{:S(2)}) copy-start(f32[256,256]{1,0:T(8,128)} %get-tuple-element.83.own_ref) | copy-start | bytes 786436 | tf_op jit(solution)/shard_map/cond
  92.4 1.7 %copy-start.5 = (f32[4,256,256]{2,1,0:T(8,128)S(1)}, f32[4,256,256]{2,1,0:T(8,128)}, u32[]{:S(2)}) copy-start(f32[4,256,256]{2,1,0:T(8,128)} %get-tuple-element.87.means_ref) | copy-start | bytes 3145732 | tf_op jit(solution)/shard_map/cond
  95.6 34.5 %all-to-all-start.5 = ((f32[64,32,128]{2,1,0:T(8,128)}), f32[64,32,128]{2,1,0:T(8,128)S(1)}, u32[]{:S(2)}, u32[]{:S(2)}) async-start(f32[64,32,128]{2,1,0:T(8,128)} %bitcast.12), calls=%async_computation.5 | async-start | bytes 2097152 | tf_op jit(solution)/shard_map/cond/branch_1_fun/all_to_all | solution.py:371
  130.1 2.6 %collective-permute-start.7 = (f32[512,128]{1,0:T(8,128)S(1)}, f32[512,128]{1,0:T(8,128)S(1)}, u32[]{:S(2)}, u32[]{:S(2)}) collective-permute-start(f32[512,128]{1,0:T(8,128)S(1)} %slice_bitcast_fusion), channel_id=1, source_target_pairs={{0,4},{4,0},{1,5},{5,1},{2,6},{6,2},{3,7},{7,3},{8,12},{12,8},{9,1... | collective-permute-start | bytes 786440 | tf_op jit(solution)/shard_map/cond/branch_1_fun/ppermute | solution.py:490

commit v7 on v6

--- a/solution.py
+++ b/solution.py
@@ -282,45 +282,40 @@
     return jnp.concatenate([ref[pl.ds(0, half, 2), :], ref[pl.ds(1, half, 2), :]], axis=1)
 
 
-def places_kernel(slots_ref, columns_ref, spreads_ref):
-    total = spreads_ref.shape[0]
+def pooled_kernel(
+    book_ref, own_ref, from_1, from_2, from_3, means_ref, slots_ref,
+    pooled_ref, base_ref, columns_ref,
+):
+    pooled = own_ref[...] + from_1[...] + from_2[...] + from_3[...] + means_ref[0]
+    pooled_ref[...] = pooled
     slots = jnp.concatenate(
         [slots_ref[...].astype(f32), jnp.zeros((128 - LEVELS, QROWS), f32)], axis=0
     )
     columns_ref[...] = slots.T.astype(jnp.int32)
-    place = iota((total, QROWS), 0)
+    place = iota((base_ref.shape[0], QROWS), 0)
     spread = place == slots_ref[0:1, :]
     for k in range(1, LEVELS):
-        here = place == slots_ref[k : k + 1, :]
-        spreads_ref[:, (k - 1) * QROWS : k * QROWS] = here.astype(bf16)
-        spread = spread | here
-    spreads_ref[:, (LEVELS - 1) * QROWS :] = spread.astype(bf16)
-
-
-def taken_kernel(found_ref, columns_ref, spreads_ref, terms_ref, taken_ref):
+        spread = spread | (place == slots_ref[k : k + 1, :])
+    base_ref[...] = -folded(dot(spread.astype(bf16), two_parts(pooled)))
+
+
+def residual_kernel(
+    found_ref, pooled_ref, base_ref, columns_ref, slots_ref, residual_ref, grads_ref
+):
     found = joined_rows(found_ref)
     rounded = found.astype(bf16)
+    place = iota((QROWS, found.shape[0]), 1)
+    turned = iota((found.shape[0], QROWS), 0)
     taken = jnp.zeros((QROWS, WIDTH), f32)
-    terms = found
+    terms = found + base_ref[...]
     for k in range(LEVELS):
         if k:
-            spread = spreads_ref[:, (k - 1) * QROWS : k * QROWS]
+            spread = (turned == slots_ref[k : k + 1, :]).astype(bf16)
             terms = terms + folded(dot(spread, two_parts(taken)))
-        places = iota((QROWS, found.shape[0]), 1)
-        picks = (columns_ref[:, k : k + 1] == places).astype(bf16)
+        picks = (columns_ref[:, k : k + 1] == place).astype(bf16)
         taken = taken + dot(picks, rounded)
-    terms_ref[...] = terms
-    taken_ref[...] = taken
-
-
-def residual_kernel(
-    book_ref, own_ref, from_1, from_2, from_3, means_ref, taken_ref, terms_ref, spread_ref,
-    residual_ref, grads_ref,
-):
-    pooled = own_ref[...] + from_1[...] + from_2[...] + from_3[...] + means_ref[0]
-    residual_ref[...] = pooled - taken_ref[...]
-    grads = terms_ref[...] - folded(dot(spread_ref[...], two_parts(pooled)))
-    split_rows(grads_ref, grads)
+    residual_ref[...] = pooled_ref[...] - taken
+    split_rows(grads_ref, terms)
 
 
 def table_kernel(codes_ref, *refs):
@@ -429,40 +424,40 @@
 def gradient_terms(book, found, slots, shares, means):
     total = OWNERS * found.shape[1] // 2
     fetched = exchange(found)
-    own, slots = lax.optimization_barrier((shares[0], slots))
-    columns, spreads = pl.pallas_call(
-        places_kernel,
-        out_shape=[
-            shape(QROWS, 128, dtype=jnp.int32), shape(total, LEVELS * QROWS, dtype=bf16),
-        ],
-        compiler_params=settings(32),
-        cost_estimate=pl.CostEstimate(flops=10**9, bytes_accessed=2**20, transcendentals=0),
-        name="places",
-    )(slots)
-    terms, taken = pl.pallas_call(
-        taken_kernel,
-        out_shape=[shape(total, WIDTH), shape(QROWS, WIDTH)],
-        compiler_params=settings(24),
-        cost_estimate=pl.CostEstimate(flops=3 * 10**9, bytes_accessed=3 * 2**20, transcendentals=0),
-        name="taken",
-    )(fetched.reshape(2 * total, 128), columns, spreads)
-    residual, grads = pl.pallas_call(
-        residual_kernel,
+    pooled, base, columns = pl.pallas_call(
+        pooled_kernel,
         grid_spec=pltpu.PrefetchScalarGridSpec(
             num_scalar_prefetch=1,
             grid=(1,),
             in_specs=[whole(QROWS, WIDTH)] * 4
             + [
                 pl.BlockSpec((1, QROWS, WIDTH), lambda i, book: (book[0], 0, 0)),
-                whole(QROWS, WIDTH), whole(total, WIDTH),
-                pl.BlockSpec((total, QROWS), lambda i, book: (0, LEVELS - 1)),
+                whole(LEVELS, QROWS),
             ],
-            out_specs=[whole(QROWS, WIDTH), whole(2 * total, 128)],
+            out_specs=[
+                whole(QROWS, WIDTH), whole(total, WIDTH), whole(QROWS, 128),
+            ],
         ),
+        out_shape=[
+            shape(QROWS, WIDTH), shape(total, WIDTH), shape(QROWS, 128, dtype=jnp.int32),
+        ],
+        compiler_params=settings(32),
+        cost_estimate=pl.CostEstimate(flops=10**9, bytes_accessed=2**20, transcendentals=0),
+        name="pooled",
+    )(book, *shares, means, slots)
+    residual, grads = pl.pallas_call(
+        residual_kernel,
+        grid=(1,),
+        in_specs=[
+            whole(2 * total, 128), whole(QROWS, WIDTH), whole(total, WIDTH), whole(QROWS, 128),
+            whole(LEVELS, QROWS),
+        ],
+        out_specs=[whole(QROWS, WIDTH), whole(2 * total, 128)],
         out_shape=[shape(QROWS, WIDTH), shape(2 * total, 128)],
         compiler_params=settings(24),
+        cost_estimate=pl.CostEstimate(flops=10**9, bytes_accessed=2**20, transcendentals=0),
         name="residual",
-    )(book, own, *shares[1:], means, taken, terms, spreads)
+    )(fetched.reshape(2 * total, 128), pooled, base, columns, slots)
     return residual, grads.reshape(found.shape)
 
 

time: 137 us -> 141 us (1.029)
  starting transfers between devices: 40.3 us -> 43.8 us
  local copies, waits for them, and re-layouts: 0.95 us -> 2.86 us
  other arithmetic: 1.79 us -> 0.27 us
    all_to_all x4, waiting for transfers between devices: 46.4 us -> 35.6 us  [exchange(): return lax.all_to_all(array, SEQ, split_axis=0, concat_axis=0, tiled=True)]
    ppermute x3, waiting for transfers between devices: 0.01 us -> 10.7 us  [shared_out(): lax.ppermute(shares[d], 'book', [(i, (i + d) % 4) for i in range(4)])]
    all_to_all x4, starting transfers between devices: 33.5 us -> 37.1 us  [exchange(): return lax.all_to_all(array, SEQ, split_axis=0, concat_axis=0, tiled=True)]
    cond x14 -> x10, local copies, waits for them, and re-layouts: 0.72 us -> 2.63 us
    convert_element_type x2, other arithmetic: 1.79 us -> 0.27 us  [asked_codes(): arrived[:, 0, ASKED + low:ASKED + high].astype(jnp.int32).reshape(1, -1)]
    pallas_call x3 -> x2, Pallas kernels: 4.11 us -> 3.52 us  [the longest x1 2.01 us: gradient_terms(): pl.pallas_call(residual_kernel, grid=(1,), in_specs=[whole(2 * total, 128...]
  transfers between devices with their start and end apart: 9 -> 9, of which waited for: 6 -> 8; matrix products, arithmetic and copies ran while one was open for 1% -> 0% of each run, Pallas kernels for 21% -> 19%
where the time goes in v7:
time: 141 us; the launch traced here: 140 us
  waiting for transfers between devices  48.7 us (35%)
  starting transfers between devices  43.8 us (31%)
  Pallas kernels  42.8 us (30%)
  local copies, waits for them, and re-layouts  2.86 us (2%)
    all_to_all x4, starting transfers between devices, exchange(): return lax.all_to_all(array, SEQ, split_axis=0, concat_axis=0, tiled=True)  37.1 us
    all_to_all x4, waiting for transfers between devices, exchange(): return lax.all_to_all(array, SEQ, split_axis=0, concat_axis=0, tiled=True)  35.6 us
    ppermute x3, waiting for transfers between devices, shared_out(): lax.ppermute(shares[d], 'book', [(i, (i + d) % 4) for i in range(4)])  10.7 us
    pallas_call x1, Pallas kernels, body(): pl.pallas_call(local_kernel, grid=(STEPS,), in_specs=[rows_of(BLOCK, 1024...  9.17 us
    pallas_call x1, Pallas kernels, shared_out(): pl.pallas_call(outer_kernel, grid_spec=pltpu.PrefetchScalarGridSpec(num_s...  8.98 us
    pallas_call x1, Pallas kernels, body(): pl.pallas_call(front_kernel, grid=(STEPS,), in_specs=[rows_of(BLOCK, 1024...  8.84 us
    pallas_call x1, Pallas kernels, looked_up(): pl.pallas_call(functools.partial(lookup_kernel, cuts), grid=(LEVELS,), in...  5.8 us
    ppermute x3, starting transfers between devices, shared_out(): lax.ppermute(shares[d], 'book', [(i, (i + d) % 4) for i in range(4)])  4.79 us
  transfers between devices with their start and end apart: 9, of which 8 were waited for; matrix products, arithmetic and copies ran while one was open for 0% of the time, Pallas kernels for 19%

profile of v7, /device:TPU:1, one launch (start us, length us, event | category | flops | bytes accessed | tf_op | source)
XLA Modules:
  0.0 139.9 jit_solution(4145232582943666618)
XLA Ops:
  0.6 8.8 %front.1 = (f32[64,1,1152]{2,1,0:T(1,128)}, s32[3,256]{1,0:T(4,128)S(1)}, s32[3,256]{1,0:T(4,128)S(1)}, f32[1,128]{1,0:T(1,128)}, bf16[1024,1024]{1,0:T(8,128)(2...) custom-call(bf16[1024,1024]{1,0:T(8,128)(2,1)} %frames_ref.3, ...), custom_call_target="tpu_custom_call" | custom-call | tf_op jit(solution)/shard_map/front/pallas_call | solution.py:537
  9.5 13.2 %all-to-all-start.6 = ((f32[64,1,1152]{2,1,0:T(1,128)}), f32[64,1,1152]{2,1,0:T(1,128)S(1)}, u32[]{:S(2)}, u32[]{:S(2)}) async-start(f32[64,1,1152]{2,1,0:T(1,128)} %get-tuple-element.114), calls=%async_computation.6 | async-start | bytes 589824 | tf_op jit(solution)/shard_map/all_to_all | solution.py:366
  23.3 9.2 %local.1 = (f32[1024,512]{1,0:T(8,128)}, f32[1024,512]{1,0:T(8,128)}, f32[1024,128]{1,0:T(8,128)}, f32[4,256,256]{2,1,0:T(8,128)}) custom-call(bf16[1024,1024]{1,0:T(8,128)(2,1)} %frames_ref.3, bf16[1024,1024]{1,0:T(8,128)(2,1)} %get-tuple-element.115.normed_ref, bf16[1024,512]{1,0:T(8,128)(2,1)} %get-tuple-element.116.inflow_ref, ...), custom_call_target="tpu_custom_call" | custom-call | flops 4000000000 | bytes 12582912 | tf_op jit(solution)/shard_map/local/pallas_call | solution.py:563
  32.5 3.9 %all-to-all-done.6 = f32[64,1,1152]{2,1,0:T(1,128)S(1)} async-done(((f32[64,1,1152]{2,1,0:T(1,128)}), f32[64,1,1152]{2,1,0:T(1,128)S(1)}, u32[]{:S(2)}, u32[]{:S(2)}) %all-to-all-start.6) | async-done | bytes 294944 | tf_op jit(solution)/shard_map/all_to_all | solution.py:366
  36.4 103.5 %conditional.1 = (f32[256,256]{1,0:T(8,128)}, f32[3,1024,256]{2,1,0:T(8,128)}) conditional(s32[]{:T(128)} %bitcast.20, (f32[64,1,1152]{2,1,0:T(1,128)S(1)}, f32[3,1024,256]{2,1,0:T(8,128)}, f32[512]{0:T(512)S(1)}, s32[1]{0:T(128)}, f32[1024,512]{1,0:T(8,128)}, /*index=5*/f32[1024,512]{1,0:T(8,128)}, f32[1024,128]{1,0:T(8,128)}, ...), branch_computations={%region_0.0_spmd, %region_1.0_spmd} | conditional | flops 8000002048 | bytes 38042052 | solution.py:584
  37.3 6.7 %all-to-all-start.4 = ((f32[64,8,128]{2,1,0:T(8,128)}), f32[64,8,128]{2,1,0:T(8,128)S(1)}, u32[]{:S(2)}, u32[]{:S(2)}) async-start(f32[64,8,128]{2,1,0:T(8,128)} %scan.3), calls=%async_computation.4 | async-start | bytes 524288 | tf_op jit(solution)/shard_map/cond/branch_1_fun/all_to_all | solution.py:366
  44.0 5.8 %lookup.3 = (f32[2048,128]{1,0:T(8,128)}, f32[512,128]{1,0:T(8,128)}) custom-call(f32[64,1,1152]{2,1,0:T(1,128)S(1)} %get-tuple-element.94.arrived_ref, f32[3,1024,256]{2,1,0:T(8,128)} %get-tuple-element.71.table_ref), custom_call_target="tpu_custom_call" | custom-call | flops 4000000000 | bytes 5242880 | tf_op jit(solution)/shard_map/cond/branch_1_fun/lookup/pallas_call | solution.py:370
  50.3 1.4 collective-permute-done.3
  52.3 1.8 %relayed.1 = f32[64,32,128]{2,1,0:T(8,128)} custom-call(f32[64,32,128]{2,1,0:T(8,128)} %bitcast.30, f32[64,8,128]{2,1,0:T(8,128)} %bitcast.34), custom_call_target="tpu_custom_call", output_to_operand_aliasing={{}: (0, {})} | custom-call | tf_op jit(solution)/shard_map/cond/branch_1_fun/relayed/pallas_call | solution.py:510
  54.1 3.1 %all-to-all-done.4 = f32[64,8,128]{2,1,0:T(8,128)S(1)} async-done(((f32[64,8,128]{2,1,0:T(8,128)}), f32[64,8,128]{2,1,0:T(8,128)S(1)}, u32[]{:S(2)}, u32[]{:S(2)}) %all-to-all-start.4) | async-done | bytes 262176 | tf_op jit(solution)/shard_map/cond/branch_1_fun/all_to_all | solution.py:366
  57.2 7.2 %all-to-all-start.3 = ((f32[64,32,128]{2,1,0:T(8,128)}), f32[64,32,128]{2,1,0:T(8,128)S(1)}, u32[]{:S(2)}, u32[]{:S(2)}) async-start(f32[64,32,128]{2,1,0:T(8,128)} %relayed.1), calls=%async_computation.3 | async-start | bytes 2097152 | tf_op jit(solution)/shard_map/cond/branch_1_fun/all_to_all | solution.py:366
  64.4 9.0 %outer.3 = (f32[256,256]{1,0:T(8,128)}, f32[256,256]{1,0:T(8,128)}, f32[256,256]{1,0:T(8,128)}, f32[256,256]{1,0:T(8,128)}) custom-call(s32[1]{0:T(128)} %get-tuple-element.74.book_ref, f32[1024,512]{1,0:T(8,128)} %get-tuple-element.75.inner_ref, f32[1024,512]{1,0:T(8,128)} %get-tuple-element.76.gate_ref, f32[1024,128]{1,0:T(8,128)} %get-tuple-element.77.reach_ref, ...), custom_call_target="tpu_custom_call" | custom-call | flops 2000000000 | bytes 8388608 | tf_op jit(solution)/shard_map/cond/branch_1_fun/outer/pallas_call | solution.py:400
  73.3 1.2 collective-permute-start.4
  74.5 2.4 %collective-permute-start.5 = (f32[256,256]{1,0:T(8,128)}, f32[256,256]{1,0:T(8,128)S(1)}, u32[]{:S(2)}, u32[]{:S(2)}) collective-permute-start(f32[256,256]{1,0:T(8,128)} %get-tuple-element.84), channel_id=1, source_target_pairs={{0,2},{1,3},{2,0},{3,1},{4,6},{5,7},{6,4},{7,5},{8,10},{9,11},{10,... | collective-permute-start | bytes 786440 | tf_op jit(solution)/shard_map/cond/branch_1_fun/ppermute | solution.py:419
  77.0 1.1 collective-permute-start.6
  78.1 4.1 %collective-permute-done.4.from_1 = f32[256,256]{1,0:T(8,128)S(1)} collective-permute-done((f32[256,256]{1,0:T(8,128)}, f32[256,256]{1,0:T(8,128)S(1)}, u32[]{:S(2)}, u32[]{:S(2)}) %collective-permute-start.4) | collective-permute-done | bytes 262176 | tf_op jit(solution)/shard_map/cond/branch_1_fun/ppermute | solution.py:419
  82.2 6.6 %collective-permute-done.5.from_2 = f32[256,256]{1,0:T(8,128)S(1)} collective-permute-done((f32[256,256]{1,0:T(8,128)}, f32[256,256]{1,0:T(8,128)S(1)}, u32[]{:S(2)}, u32[]{:S(2)}) %collective-permute-start.5) | collective-permute-done | bytes 262176 | tf_op jit(solution)/shard_map/cond/branch_1_fun/ppermute | solution.py:419
  89.7 1.5 %pooled.3 = (f32[256,256]{1,0:T(8,128)S(1)}, f32[1024,256]{1,0:T(8,128)S(1)}, s32[256,128]{1,0:T(8,128)S(1)}) custom-call(s32[1]{0:T(128)} %get-tuple-element.74.book_ref, f32[256,256]{1,0:T(8,128)S(1)} %copy-done.3, f32[256,256]{1,0:T(8,128)S(1)} %collective-permute-done.4.from_1, f32[256,256]{1,0:T(8,128)S(1)} %collective-permute-done.5.from_2, ...), custom_call_target="tpu_custom_call" | custom-call | flops 1000000000 | bytes 1048576 | tf_op jit(solution)/shard_map/cond/branch_1_fun/pooled/pallas_call | solution.py:427
  92.3 2.0 %residual.3 = (f32[256,256]{1,0:T(8,128)}, f32[2048,128]{1,0:T(8,128)S(1)}) custom-call(f32[2048,128]{1,0:T(8,128)S(1)} %bitcast.28, f32[256,256]{1,0:T(8,128)S(1)} %get-tuple-element.88.pooled_ref, f32[1024,256]{1,0:T(8,128)S(1)} %get-tuple-element.89.base_ref, s32[256,128]{1,0:T(8,128)S(1)} %get-tuple-element.90.columns_ref, ...), custom_call_target="tpu_custom_call" | custom-call | flops 1000000000 | bytes 1048576 | tf_op jit(solution)/shard_map/cond/branch_1_fun/residual/pallas_call | solution.py:448
  95.3 10.2 %all-to-all-start.5 = ((f32[64,32,128]{2,1,0:T(8,128)}), f32[64,32,128]{2,1,0:T(8,128)S(1)}, u32[]{:S(2)}, u32[]{:S(2)}) async-start(f32[64,32,128]{2,1,0:T(8,128)} %bitcast.29), calls=%async_computation.5 | async-start | bytes 2097152 | tf_op jit(solution)/shard_map/cond/branch_1_fun/all_to_all | solution.py:366
  106.0 27.5 %all-to-all-done.5 = f32[64,32,128]{2,1,0:T(8,128)S(1)} async-done(((f32[64,32,128]{2,1,0:T(8,128)}), f32[64,32,128]{2,1,0:T(8,128)S(1)}, u32[]{:S(2)}, u32[]{:S(2)}) %all-to-all-start.5) | async-done | bytes 1048608 | tf_op jit(solution)/shard_map/cond/branch_1_fun/all_to_all | solution.py:366
  133.5 1.4 %collective-permute-start.7 = (f32[512,128]{1,0:T(8,128)S(1)}, f32[512,128]{1,0:T(8,128)S(1)}, u32[]{:S(2)}, u32[]{:S(2)}) collective-permute-start(f32[512,128]{1,0:T(8,128)S(1)} %slice_bitcast_fusion), channel_id=1, source_target_pairs={{0,4},{4,0},{1,5},{5,1},{2,6},{6,2},{3,7},{7,3},{8,12},{12,8},{9,1... | collective-permute-start | bytes 786440 | tf_op jit(solution)/shard_map/cond/branch_1_fun/ppermute | solution.py:485
  134.9 1.2 collective-permute-done.7.refs_1_
  136.1 3.8 %table.3 = f32[3072,256]{1,0:T(8,128)} custom-call(s32[1,1280]{1,0:T(1,128)S(1)} %pad_add_fusion.codes_ref, f32[2048,128]{1,0:T(8,128)S(1)} %bitcast.24, f32[512,128]{1,0:T(8,128)S(1)} %collective-permute-done.7.refs_1_), custom_call_target="tpu_custom_call" | custom-call | tf_op jit(solution)/shard_map/cond/branch_1_fun/table/pallas_call | solution.py:465
  (22 shorter events, 5.7 us)
Async XLA Ops:
  9.5 26.9 %all-to-all-start.6 = ((f32[64,1,1152]{2,1,0:T(1,128)}), f32[64,1,1152]{2,1,0:T(1,128)S(1)}, u32[]{:S(2)}, u32[]{:S(2)}) async-start(f32[64,1,1152]{2,1,0:T(1,128)} %get-tuple-element.114), calls=%async_computation.6 | async-start | bytes 589824 | tf_op jit(solution)/shard_map/all_to_all | solution.py:366
  23.3 13.1 %copy-start.9 = (f32[512]{0:T(512)S(1)}, f32[512]{0:T(512)}, u32[]{:S(2)}) copy-start(f32[512]{0:T(512)} %param.22) | copy-start | bytes 6148
  36.4 13.5 %copy-start.8 = (bf16[1024,256]{1,0:T(8,128)(2,1)}, bf16[1024,256]{1,0:T(8,128)(2,1)S(1)}, u32[]{:S(2)}) copy-start(bf16[1024,256]{1,0:T(8,128)(2,1)S(1)} %get-tuple-element.78.c_ref) | copy-start | bytes 1572868 | tf_op jit(solution)/shard_map/cond
  37.3 19.8 %all-to-all-start.4 = ((f32[64,8,128]{2,1,0:T(8,128)}), f32[64,8,128]{2,1,0:T(8,128)S(1)}, u32[]{:S(2)}, u32[]{:S(2)}) async-start(f32[64,8,128]{2,1,0:T(8,128)} %scan.3), calls=%async_computation.4 | async-start | bytes 524288 | tf_op jit(solution)/shard_map/cond/branch_1_fun/all_to_all | solution.py:366
  49.8 1.8 %collective-permute-start.3 = (f32[512,128]{1,0:T(8,128)}, f32[512,128]{1,0:T(8,128)S(1)}, u32[]{:S(2)}, u32[]{:S(2)}) collective-permute-start(f32[512,128]{1,0:T(8,128)} %get-tuple-element.73), channel_id=1, source_target_pairs={{0,4},{4,0},{1,5},{5,1},{2,6},{6,2},{3,7},{7,3},{8,12},{12,8},{9,1... | collective-permute-start | bytes 786440 | tf_op jit(solution)/shard_map/cond/branch_1_fun/ppermute | solution.py:485
  51.6 0.7 copy-start.4
  57.2 7.2 %copy-start.5 = (f32[64,8,128]{2,1,0:T(8,128)}, f32[64,8,128]{2,1,0:T(8,128)S(1)}, u32[]{:S(2)}) copy-start(f32[64,8,128]{2,1,0:T(8,128)S(1)} %all-to-all-done.4) | copy-start | bytes 786436 | tf_op jit(solution)/shard_map/cond
  57.2 35.1 %all-to-all-start.3 = ((f32[64,32,128]{2,1,0:T(8,128)}), f32[64,32,128]{2,1,0:T(8,128)S(1)}, u32[]{:S(2)}, u32[]{:S(2)}) async-start(f32[64,32,128]{2,1,0:T(8,128)} %relayed.1), calls=%async_computation.3 | async-start | bytes 2097152 | tf_op jit(solution)/shard_map/cond/branch_1_fun/all_to_all | solution.py:366
  73.3 8.8 %collective-permute-start.4 = (f32[256,256]{1,0:T(8,128)}, f32[256,256]{1,0:T(8,128)S(1)}, u32[]{:S(2)}, u32[]{:S(2)}) collective-permute-start(f32[256,256]{1,0:T(8,128)} %get-tuple-element.83), channel_id=1, source_target_pairs={{0,1},{1,2},{2,3},{3,0},{4,5},{5,6},{6,7},{7,4},{8,9},{9,10},{10,1... | collective-permute-start | bytes 786440 | tf_op jit(solution)/shard_map/cond/branch_1_fun/ppermute | solution.py:419
  74.5 14.2 %collective-permute-start.5 = (f32[256,256]{1,0:T(8,128)}, f32[256,256]{1,0:T(8,128)S(1)}, u32[]{:S(2)}, u32[]{:S(2)}) collective-permute-start(f32[256,256]{1,0:T(8,128)} %get-tuple-element.84), channel_id=1, source_target_pairs={{0,2},{1,3},{2,0},{3,1},{4,6},{5,7},{6,4},{7,5},{8,10},{9,11},{10,... | collective-permute-start | bytes 786440 | tf_op jit(solution)/shard_map/cond/branch_1_fun/ppermute | solution.py:419
  77.0 11.8 %collective-permute-start.6 = (f32[256,256]{1,0:T(8,128)}, f32[256,256]{1,0:T(8,128)S(1)}, u32[]{:S(2)}, u32[]{:S(2)}) collective-permute-start(f32[256,256]{1,0:T(8,128)} %get-tuple-element.85), channel_id=1, source_target_pairs={{0,3},{1,0},{2,1},{3,2},{4,7},{5,4},{6,5},{7,6},{8,11},{9,8},{10,9... | collective-permute-start | bytes 786440 | tf_op jit(solution)/shard_map/cond/branch_1_fun/ppermute | solution.py:419
  88.8 1.0 copy-start.3
  94.3 1.0 copy-start.1
  95.3 38.1 %all-to-all-start.5 = ((f32[64,32,128]{2,1,0:T(8,128)}), f32[64,32,128]{2,1,0:T(8,128)S(1)}, u32[]{:S(2)}, u32[]{:S(2)}) async-start(f32[64,32,128]{2,1,0:T(8,128)} %bitcast.29), calls=%async_computation.5 | async-start | bytes 2097152 | tf_op jit(solution)/shard_map/cond/branch_1_fun/all_to_all | solution.py:366
  133.5 2.6 %collective-permute-start.7 = (f32[512,128]{1,0:T(8,128)S(1)}, f32[512,128]{1,0:T(8,128)S(1)}, u32[]{:S(2)}, u32[]{:S(2)}) collective-permute-start(f32[512,128]{1,0:T(8,128)S(1)} %slice_bitcast_fusion), channel_id=1, source_target_pairs={{0,4},{4,0},{1,5},{5,1},{2,6},{6,2},{3,7},{7,3},{8,12},{12,8},{9,1... | collective-permute-start | bytes 786440 | tf_op jit(solution)/shard_map/cond/branch_1_fun/ppermute | solution.py:485
